TPU v7x, 32 devices: a whole 2x2x4 slice. The times are simulated.
32 devices in a mesh: expert: 8 (over y, x, core), fsdp: 4 (over z).
Axes of the slice: x: 2, y: 2, z: 4, core: 2. Of those that a mesh axis runs over, the one named last changes fastest.
Arguments:
- tokens: bfloat16 [12288, 2048], P(('expert', 'fsdp')), may hold values from -6 to 6
- routes: int32 [12288, 4], P(('expert', 'fsdp')), may hold values from 0 to 7, all different within a row; in each aligned block of 384 rows (0 to 383, 384 to 767, ...) at most 256 rows name the same one
- seq_lengths: int32 [8, 3], P('expert'), may hold values from 1 to 1024, 1536 in all within a row
- cotangent: bfloat16 [12288, 2048], P(('expert', 'fsdp')), may hold values from -6 to 6
- norm1_gain: bfloat16 [2048], replicated, may hold values from 0.5 to 1.5
- query_weight: bfloat16 [2048, 2048], P(None, 'fsdp'), may hold values from -0.125 to 0.125
- query_bias: bfloat16 [2048], P('fsdp'), may hold values from -1.25 to 1.25
- key_weight: bfloat16 [2048, 2048], P(None, 'fsdp'), may hold values from -0.125 to 0.125
- key_bias: bfloat16 [2048], P('fsdp'), may hold values from -1.25 to 1.25
- value_weight: bfloat16 [2048, 2048], P(None, 'fsdp'), may hold values from -0.125 to 0.125
- value_bias: bfloat16 [2048], P('fsdp'), may hold values from -1.25 to 1.25
- out_weight: bfloat16 [2048, 2048], P('fsdp'), may hold values from -1 to 1
- norm2_gain: bfloat16 [2048], replicated, may hold values from 0.5 to 1.5
- router_weight: bfloat16 [2048, 8], replicated, may hold values from -0.0625 to 0.0625
- shared_switch: bfloat16 [2048], replicated, may hold values from -0.125 to 0.125
- shared_gate: bfloat16 [2048, 5632], P(None, 'fsdp'), may hold values from -0.125 to 0.125
- shared_up: bfloat16 [2048, 5632], P(None, 'fsdp'), may hold values from -0.125 to 0.125
- shared_down: bfloat16 [5632, 2048], P('fsdp'), may hold values from -0.078125 to 0.078125
- expert_gate: bfloat16 [8, 2048, 1408], P('expert', 'fsdp'), may hold values from -0.125 to 0.125
- expert_up: bfloat16 [8, 2048, 1408], P('expert', 'fsdp'), may hold values from -0.125 to 0.125
- expert_down: bfloat16 [8, 1408, 2048], P('expert', None, 'fsdp'), may hold values from -0.625 to 0.625
Outputs:
- block_out: bfloat16 [12288, 2048], P(('expert', 'fsdp'))
- grad_tokens: float32 [12288, 2048], P(('expert', 'fsdp'))
- grad_norm1_gain: float32 [2048], replicated
- grad_query_weight: float32 [2048, 2048], P(None, 'fsdp')
- grad_query_bias: float32 [2048], P('fsdp')
- grad_key_weight: float32 [2048, 2048], P(None, 'fsdp')
- grad_key_bias: float32 [2048], P('fsdp')
- grad_value_weight: float32 [2048, 2048], P(None, 'fsdp')
- grad_value_bias: float32 [2048], P('fsdp')
- grad_out_weight: float32 [2048, 2048], P('fsdp')
- grad_norm2_gain: float32 [2048], replicated
- grad_router_weight: float32 [2048, 8], replicated
- grad_shared_switch: float32 [2048], replicated
- grad_shared_gate: float32 [2048, 5632], P(None, 'fsdp')
- grad_shared_up: float32 [2048, 5632], P(None, 'fsdp')
- grad_shared_down: float32 [5632, 2048], P('fsdp')
- grad_expert_gate: float32 [8, 2048, 1408], P('expert', 'fsdp')
- grad_expert_up: float32 [8, 2048, 1408], P('expert', 'fsdp')
- grad_expert_down: float32 [8, 1408, 2048], P('expert', None, 'fsdp')
Inputs may be any that keep to these rules, and one draw needn't show every extreme that they name: `routes`: A token names 4 different experts. In the rows of one device (384 consecutive rows) no expert is named by more than 256 rows, a bound that some block reaches. `seq_lengths`: each row sums to 1536, and its largest length is exactly 1024.
All inputs are finite; a program needn't handle non-finite values.
Results may differ from a plain program's by a relative error of at most 0.025.
Values may be sent and summed in bfloat16 or wider, within the bound.
A program may use at most 448 MiB of HBM per device.

v0:
```python
import math

import jax
import jax.numpy as jnp
from jax import lax
from jax.sharding import PartitionSpec as P

HEAD_DIM = 128
TOP = 4


EPSILON = 1e-06
THETA = 1000000.0
MASKED = -1e30
PRECISE = lax.Precision.HIGHEST


def rms_rate(values):
    return lax.rsqrt(jnp.mean(values * values, axis=-1, keepdims=True) + EPSILON)


def token_layout(lengths, count):
    ends = jnp.cumsum(lengths)
    places = jnp.arange(count, dtype=jnp.int32)
    passed = (places[:, None] >= ends[None, :]).astype(jnp.int32)
    segment = jnp.sum(passed, axis=1)
    start = jnp.sum(passed * lengths[None, :], axis=1)
    return (segment, places - start)


def rotary_tables(positions, width):
    half_width = width // 2
    inverse = THETA ** (-2.0 * jnp.arange(half_width, dtype=jnp.float32) / width)
    angle = positions.astype(jnp.float32)[:, None] * inverse[None, :]
    return (jnp.cos(angle)[:, None, :], jnp.sin(angle)[:, None, :])


def rotate(values, cosine, sine):
    half_width = values.shape[-1] // 2
    first_half = values[..., :half_width]
    second_half = values[..., half_width:]
    return jnp.concatenate(
        [first_half * cosine - second_half * sine, second_half * cosine + first_half * sine],
        axis=-1,
    )


def rotate_back(grads, cosine, sine):
    half_width = grads.shape[-1] // 2
    first_half = grads[..., :half_width]
    second_half = grads[..., half_width:]
    return jnp.concatenate(
        [first_half * cosine + second_half * sine, second_half * cosine - first_half * sine],
        axis=-1,
    )


def matmul(left_matrix, right_matrix):
    return jnp.dot(left_matrix, right_matrix, preferred_element_type=jnp.float32)


def matmul_tn(left_matrix, right_matrix):
    return lax.dot_general(
        left_matrix, right_matrix, (((0,), (0,)), ((), ())), preferred_element_type=jnp.float32
    )


def matmul_nt(left_matrix, right_matrix):
    return lax.dot_general(
        left_matrix, right_matrix, (((1,), (1,)), ((), ())), preferred_element_type=jnp.float32
    )


def silu_parts(pre_values):
    sigma_values = jax.nn.sigmoid(pre_values)
    return (pre_values * sigma_values, sigma_values * (1.0 + pre_values * (1.0 - sigma_values)))


def norm_back(upstream, dh_values, values, rate, gain):
    gained = dh_values * gain
    return (
        upstream
        + rate * gained
        - values * rate**3 * jnp.mean(gained * values, axis=-1, keepdims=True)
    )


def shards(
    tokens,
    routes,
    seq_lengths,
    cotangent,
    norm1_gain,
    query_weight,
    query_bias,
    key_weight,
    key_bias,
    value_weight,
    value_bias,
    out_weight,
    norm2_gain,
    router_weight,
    shared_switch,
    shared_gate,
    shared_up,
    shared_down,
    expert_gate,
    expert_up,
    expert_down,
):
    own_count = tokens.shape[0]
    width = tokens.shape[1]
    member = lax.axis_index("fsdp")
    own_start = member * own_count
    group_tokens, group_cot, full_gate, full_up, full_down = (
        lax.all_gather(tokens, "fsdp", axis=0, tiled=True),
        lax.all_gather(cotangent, "fsdp", axis=0, tiled=True),
        lax.all_gather(expert_gate, "fsdp", axis=1, tiled=True),
        lax.all_gather(expert_up, "fsdp", axis=1, tiled=True),
        lax.all_gather(expert_down, "fsdp", axis=2, tiled=True),
    )
    count = group_tokens.shape[0]
    local_heads = query_weight.shape[1] // HEAD_DIM
    segment, positions = token_layout(seq_lengths[0], count)
    cosine, sine = rotary_tables(positions, HEAD_DIM)
    tokens_wide = group_tokens.astype(jnp.float32)
    tokens_own_wide = tokens.astype(jnp.float32)
    rate_first = rms_rate(tokens_wide)
    rate_first_own = lax.dynamic_slice_in_dim(rate_first, own_start, own_count, 0)
    gain_first = norm1_gain.astype(jnp.float32)
    normed_first = (tokens_wide * rate_first * gain_first).astype(jnp.bfloat16)
    query_pre = matmul(normed_first, query_weight) + query_bias.astype(jnp.float32)
    key_pre = matmul(normed_first, key_weight) + key_bias.astype(jnp.float32)
    value_pre = matmul(normed_first, value_weight) + value_bias.astype(jnp.float32)
    queries = rotate(query_pre.reshape(count, local_heads, HEAD_DIM), cosine, sine).astype(
        jnp.bfloat16
    )
    keys_all = rotate(key_pre.reshape(count, local_heads, HEAD_DIM), cosine, sine).astype(
        jnp.bfloat16
    )
    values_all = value_pre.reshape(count, local_heads, HEAD_DIM).astype(jnp.bfloat16)
    block_rows = math.gcd(count, 512)
    block_count = count // block_rows
    factor = 1.0 / math.sqrt(HEAD_DIM)

    def block_scores(start):
        query_rows = lax.dynamic_slice_in_dim(queries, start, block_rows, 0)
        segment_rows = lax.dynamic_slice_in_dim(segment, start, block_rows, 0)
        position_rows = lax.dynamic_slice_in_dim(positions, start, block_rows, 0)
        allowed = (segment_rows[:, None] == segment[None, :]) & (
            position_rows[:, None] >= positions[None, :]
        )
        scores = (
            jnp.einsum("qhd,khd->hqk", query_rows, keys_all, preferred_element_type=jnp.float32)
            * factor
        )
        return (query_rows, jnp.where(allowed[None], scores, MASKED))

    def forward_block(block_index):
        query_rows, scores = block_scores(block_index * block_rows)
        peak = jnp.max(scores, axis=-1, keepdims=True)
        raised = jnp.exp(scores - peak)
        total_mass = jnp.sum(raised, axis=-1, keepdims=True)
        soft_low = (raised / total_mass).astype(jnp.bfloat16)
        context = jnp.einsum(
            "hqk,khd->qhd", soft_low, values_all, preferred_element_type=jnp.float32
        )
        return (context, (peak + jnp.log(total_mass))[..., 0])

    contexts, log_mass = lax.map(forward_block, jnp.arange(block_count, dtype=jnp.int32))
    attended = contexts.reshape(count, local_heads * HEAD_DIM).astype(jnp.bfloat16)
    attn_partial = matmul(attended, out_weight)
    gain_second = norm2_gain.astype(jnp.float32)
    attn_out = lax.psum(attn_partial, "fsdp")
    resid_mid = tokens_wide + attn_out
    rate_second = rms_rate(resid_mid)
    normed_second = (resid_mid * rate_second * gain_second).astype(jnp.bfloat16)
    resid_own = lax.dynamic_slice_in_dim(resid_mid, own_start, own_count, 0)
    rate_own = lax.dynamic_slice_in_dim(rate_second, own_start, own_count, 0)
    switch_all = jax.nn.sigmoid(matmul(normed_second, shared_switch[:, None]))
    shared_gate_pre = matmul(normed_second, shared_gate)
    shared_up_pre = matmul(normed_second, shared_up)
    shared_silu, shared_slope = silu_parts(shared_gate_pre)
    shared_mid = (shared_silu * shared_up_pre).astype(jnp.bfloat16)
    shared_own = lax.psum_scatter(
        matmul(shared_mid, shared_down).astype(jnp.bfloat16),
        "fsdp",
        scatter_dimension=0,
        tiled=True,
    ).astype(jnp.float32)
    normed_own = lax.dynamic_slice_in_dim(normed_second, own_start, own_count, 0)
    switch_own = lax.dynamic_slice_in_dim(switch_all, own_start, own_count, 0)
    experts_count = router_weight.shape[1]
    expert_ids = jnp.arange(experts_count, dtype=jnp.int32)
    router_probs = jax.nn.softmax(matmul(normed_own, router_weight), axis=-1)
    route_hot = (routes[:, :, None] == expert_ids[None, None, :]).astype(jnp.float32)
    gates = jnp.sum(route_hot * router_probs[:, None, :], axis=-1)
    capacity = 4 * own_count * TOP // (3 * experts_count)
    pair_count = own_count * TOP
    flat_routes = routes.reshape(pair_count)
    pair_hot = (flat_routes[:, None] == expert_ids[None, :]).astype(jnp.int32)
    earlier = jnp.cumsum(pair_hot, axis=0) - pair_hot
    slot_of = jnp.sum(earlier * pair_hot, axis=1)
    place = flat_routes * capacity + slot_of
    slot_pair = (
        jnp.full((experts_count * capacity,), pair_count, jnp.int32)
        .at[place]
        .set(jnp.arange(pair_count, dtype=jnp.int32))
    )
    padded_own = jnp.concatenate([normed_own, jnp.zeros((1, width), jnp.bfloat16)], 0)
    send_rows = padded_own[slot_pair // TOP].reshape(experts_count, capacity, width)
    gate_mat = full_gate[0]
    up_mat = full_up[0]
    down_mat = full_down[0]
    received = lax.all_to_all(send_rows, "expert", split_axis=0, concat_axis=0, tiled=True)
    flat_rows = received.reshape(-1, width)
    silu_values = silu_parts(matmul(flat_rows, gate_mat))[0]
    middle = (silu_values * matmul(flat_rows, up_mat)).astype(jnp.bfloat16)
    result = matmul(middle, down_mat).astype(jnp.bfloat16).reshape(received.shape)
    returned = lax.all_to_all(result, "expert", split_axis=0, concat_axis=0, tiled=True)
    pair_rows = (
        returned.reshape(-1, width)[place].astype(jnp.float32).reshape(own_count, TOP, width)
    )
    experts_own = jnp.sum(gates[:, :, None] * pair_rows, axis=1)
    block_out = (resid_own + switch_own * shared_own + experts_own).astype(jnp.bfloat16)
    grad_own = cotangent.astype(jnp.float32)
    d_gates = jnp.sum(pair_rows * grad_own[:, None, :], axis=-1)
    d_pairs = (
        (gates[:, :, None] * grad_own[:, None, :]).astype(jnp.bfloat16).reshape(pair_count, width)
    )
    padded_grads = jnp.concatenate([d_pairs, jnp.zeros((1, width), jnp.bfloat16)], 0)
    send_grads = padded_grads[slot_pair].reshape(experts_count, capacity, width)
    received_grads = lax.all_to_all(send_grads, "expert", split_axis=0, concat_axis=0, tiled=True)
    rows_flat = received.reshape(-1, width)
    grads_flat = received_grads.reshape(-1, width)
    expert_gate_pre = matmul(rows_flat, gate_mat)
    expert_up_pre = matmul(rows_flat, up_mat)
    expert_silu, expert_slope = silu_parts(expert_gate_pre)
    expert_mid = (expert_silu * expert_up_pre).astype(jnp.bfloat16)
    d_expert_mid = matmul_nt(grads_flat, down_mat)
    d_expert_gate = (d_expert_mid * expert_up_pre * expert_slope).astype(jnp.bfloat16)
    d_expert_up = (d_expert_mid * expert_silu).astype(jnp.bfloat16)
    d_received = (
        (matmul_nt(d_expert_gate, gate_mat) + matmul_nt(d_expert_up, up_mat))
        .astype(jnp.bfloat16)
        .reshape(received.shape)
    )
    row_grads = lax.all_to_all(d_received, "expert", split_axis=0, concat_axis=0, tiled=True)
    expert_grads = (
        lax.psum_scatter(
            matmul_tn(rows_flat, d_expert_gate)[None].astype(jnp.bfloat16),
            "fsdp",
            scatter_dimension=1,
            tiled=True,
        ).astype(jnp.float32),
        lax.psum_scatter(
            matmul_tn(rows_flat, d_expert_up)[None].astype(jnp.bfloat16),
            "fsdp",
            scatter_dimension=1,
            tiled=True,
        ).astype(jnp.float32),
        lax.psum_scatter(
            matmul_tn(expert_mid, grads_flat)[None].astype(jnp.bfloat16),
            "fsdp",
            scatter_dimension=2,
            tiled=True,
        ).astype(jnp.float32),
    )
    experts_dh = jnp.sum(
        row_grads.reshape(-1, width)[place].astype(jnp.float32).reshape(own_count, TOP, width),
        axis=1,
    )
    d_choice = jnp.sum(d_gates[:, :, None] * route_hot, axis=1)
    d_logits = router_probs * (d_choice - jnp.sum(router_probs * d_choice, axis=-1, keepdims=True))
    normed_own_wide = normed_own.astype(jnp.float32)
    router_part = jnp.dot(
        normed_own_wide.T, d_logits, precision=PRECISE, preferred_element_type=jnp.float32
    )
    switch_logit = (
        jnp.sum(grad_own * shared_own, axis=-1, keepdims=True) * switch_own * (1.0 - switch_own)
    )
    switch_part = jnp.sum(switch_logit * normed_own_wide, axis=0)
    own_dh = (
        experts_dh
        + jnp.dot(
            d_logits,
            router_weight.astype(jnp.float32).T,
            precision=PRECISE,
            preferred_element_type=jnp.float32,
        )
        + switch_logit * shared_switch.astype(jnp.float32)
    )
    group_grad = group_cot.astype(jnp.float32)
    d_shared_out = (switch_all * group_grad).astype(jnp.bfloat16)
    d_shared_mid = matmul_nt(d_shared_out, shared_down)
    d_shared_gate = (d_shared_mid * shared_up_pre * shared_slope).astype(jnp.bfloat16)
    d_shared_up = (d_shared_mid * shared_silu).astype(jnp.bfloat16)
    shared_down_grad = matmul_tn(shared_mid, d_shared_out)
    shared_gate_grad = matmul_tn(normed_second, d_shared_gate)
    shared_up_grad = matmul_tn(normed_second, d_shared_up)
    dh_partial = matmul_nt(d_shared_gate, shared_gate) + matmul_nt(d_shared_up, shared_up)
    own_block = lax.dynamic_slice_in_dim(dh_partial, own_start, own_count, 0) + own_dh
    dh_partial = lax.dynamic_update_slice_in_dim(dh_partial, own_block, own_start, 0)
    dh_second = lax.psum(dh_partial, "fsdp")
    dh_second_own = lax.dynamic_slice_in_dim(dh_second, own_start, own_count, 0)
    d_resid = norm_back(group_grad, dh_second, resid_mid, rate_second, gain_second)
    d_resid_own = lax.dynamic_slice_in_dim(d_resid, own_start, own_count, 0)
    d_attn_out = d_resid.astype(jnp.bfloat16)
    norm2_part = jnp.sum(dh_second_own * resid_own * rate_own, axis=0)
    out_grad = matmul_tn(attended, d_attn_out)
    d_context = (
        matmul_nt(d_attn_out, out_weight).astype(jnp.bfloat16).reshape(count, local_heads, HEAD_DIM)
    )

    def backward_block(carry, block_index):
        key_acc, value_acc = carry
        start = block_index * block_rows
        query_rows, scores = block_scores(start)
        grad_rows = lax.dynamic_slice_in_dim(d_context, start, block_rows, 0)
        soft_weights = jnp.exp(scores - log_mass[block_index][..., None])
        d_soft = jnp.einsum(
            "qhd,khd->hqk", grad_rows, values_all, preferred_element_type=jnp.float32
        )
        inner = jnp.sum(soft_weights * d_soft, axis=-1, keepdims=True)
        d_scores = (soft_weights * (d_soft - inner)).astype(jnp.bfloat16)
        d_query = (
            jnp.einsum("hqk,khd->qhd", d_scores, keys_all, preferred_element_type=jnp.float32)
            * factor
        )
        key_acc = (
            key_acc
            + jnp.einsum("hqk,qhd->khd", d_scores, query_rows, preferred_element_type=jnp.float32)
            * factor
        )
        value_acc = value_acc + jnp.einsum(
            "hqk,qhd->khd",
            soft_weights.astype(jnp.bfloat16),
            grad_rows,
            preferred_element_type=jnp.float32,
        )
        return ((key_acc, value_acc), d_query)

    zero_heads = jnp.zeros((count, local_heads, HEAD_DIM), jnp.float32)
    (key_grad, value_grad), query_blocks = lax.scan(
        backward_block, (zero_heads, zero_heads), jnp.arange(block_count, dtype=jnp.int32)
    )
    query_grad = query_blocks.reshape(count, local_heads, HEAD_DIM)
    d_query_pre = (
        rotate_back(query_grad, cosine, sine)
        .astype(jnp.bfloat16)
        .reshape(count, local_heads * HEAD_DIM)
    )
    d_key_pre = (
        rotate_back(key_grad, cosine, sine)
        .astype(jnp.bfloat16)
        .reshape(count, local_heads * HEAD_DIM)
    )
    d_value_pre = value_grad.astype(jnp.bfloat16).reshape(count, local_heads * HEAD_DIM)
    dh_first_part = (
        matmul_nt(d_query_pre, query_weight)
        + matmul_nt(d_key_pre, key_weight)
        + matmul_nt(d_value_pre, value_weight)
    )
    dh_first = lax.psum(dh_first_part.astype(jnp.bfloat16), "fsdp").astype(jnp.float32)
    dh_first_own = lax.dynamic_slice_in_dim(dh_first, own_start, own_count, 0)
    norm1_part = jnp.sum(dh_first_own * tokens_own_wide * rate_first_own, axis=0)
    grad_tokens = norm_back(d_resid_own, dh_first_own, tokens_own_wide, rate_first_own, gain_first)
    stats = lax.psum((norm1_part, norm2_part, router_part, switch_part), ("expert", "fsdp"))
    summed = (
        lax.psum(matmul_tn(normed_first, d_query_pre).astype(jnp.bfloat16), "expert").astype(
            jnp.float32
        ),
        lax.psum(
            jnp.sum(d_query_pre.astype(jnp.float32), axis=0).astype(jnp.bfloat16), "expert"
        ).astype(jnp.float32),
        lax.psum(matmul_tn(normed_first, d_key_pre).astype(jnp.bfloat16), "expert").astype(
            jnp.float32
        ),
        lax.psum(
            jnp.sum(d_key_pre.astype(jnp.float32), axis=0).astype(jnp.bfloat16), "expert"
        ).astype(jnp.float32),
        lax.psum(matmul_tn(normed_first, d_value_pre).astype(jnp.bfloat16), "expert").astype(
            jnp.float32
        ),
        lax.psum(
            jnp.sum(d_value_pre.astype(jnp.float32), axis=0).astype(jnp.bfloat16), "expert"
        ).astype(jnp.float32),
        lax.psum(out_grad.astype(jnp.bfloat16), "expert").astype(jnp.float32),
        lax.psum(shared_gate_grad.astype(jnp.bfloat16), "expert").astype(jnp.float32),
        lax.psum(shared_up_grad.astype(jnp.bfloat16), "expert").astype(jnp.float32),
        lax.psum(shared_down_grad.astype(jnp.bfloat16), "expert").astype(jnp.float32),
    )
    return (
        block_out,
        grad_tokens,
        stats[0],
        summed[0],
        summed[1],
        summed[2],
        summed[3],
        summed[4],
        summed[5],
        summed[6],
        stats[1],
        stats[2],
        stats[3],
        summed[7],
        summed[8],
        summed[9],
        expert_grads[0],
        expert_grads[1],
        expert_grads[2],
    )


def solution(mesh):
    placed = (
        P(("expert", "fsdp"), None),
        P(("expert", "fsdp"), None),
        P("expert", None),
        P(("expert", "fsdp"), None),
        P(),
        P(None, "fsdp"),
        P("fsdp"),
        P(None, "fsdp"),
        P("fsdp"),
        P(None, "fsdp"),
        P("fsdp"),
        P("fsdp", None),
        P(),
        P(),
        P(),
        P(None, "fsdp"),
        P(None, "fsdp"),
        P("fsdp", None),
        P("expert", "fsdp", None),
        P("expert", "fsdp", None),
        P("expert", None, "fsdp"),
    )
    return jax.shard_map(
        shards,
        mesh=mesh,
        in_specs=placed,
        out_specs=(
            P(("expert", "fsdp"), None),
            P(("expert", "fsdp"), None),
            P(),
            P(None, "fsdp"),
            P("fsdp"),
            P(None, "fsdp"),
            P("fsdp"),
            P(None, "fsdp"),
            P("fsdp"),
            P("fsdp", None),
            P(),
            P(),
            P(),
            P(None, "fsdp"),
            P(None, "fsdp"),
            P("fsdp", None),
            P("expert", "fsdp", None),
            P("expert", "fsdp", None),
            P("expert", None, "fsdp"),
        ),
        check_vma=False,
    )
```

profile of v0, /device:TPU:0, one launch (start us, length us, event | category | flops | bytes accessed | tf_op | source)
XLA Modules:
  0.0 2996.7 jit_solution(18332616072485531755)
XLA Ops:
  16.5 111.2 %all-gather.6.cloned.1.call-done = bf16[1536,2048]{1,0:T(8,128)(2,1)} async-done(((bf16[384,2048]{1,0:T(8,128)(2,1)}), bf16[1536,2048]{1,0:T(8,128)(2,1)}) %all-gather.6.cloned.1.call-update) | async-done | bytes 6291472 | tf_op jit(solution)/shard_map/all_gather | solution.py:116
  181.6 48.8 %while.27 = (s32[]{:T(128)}, bf16[3,512,4,128]{3,1,2,0:T(8,128)(2,1)}, f32[3,4,512]{2,1,0:T(4,128)}, s32[3]{0:T(128)S(1)}, s32[1536]{0:T(1024)S(1)}, /*index=5*/...) while((s32[]{:T(128)}, ...), condition=%wide.region_7.8_spmd, body=%wide.region_4.7_spmd.sunk | while | flops 1650718720 | bytes 64577828 | solution.py:170
  241.4 423.6 %all-reduce.11.cloned.1.call-done = f32[1536,2048]{1,0:T(8,128)} async-done(((f32[1536,2048]{1,0:T(8,128)}), f32[1536,2048]{1,0:T(8,128)}) %all-reduce.11.cloned.1.call-update) | async-done | bytes 12582928 | tf_op jit(solution)/shard_map/psum | solution.py:174
  665.1 12.6 multiply_reduce_fusion.4
  691.5 13.6 fusion.109
  705.1 12.1 fusion.110
  717.2 63.8 %all-gather.14.cloned.1.call-done = bf16[1536,2048]{1,0:T(8,128)(2,1)} async-done(((bf16[384,2048]{1,0:T(8,128)(2,1)}), bf16[1536,2048]{1,0:T(8,128)(2,1)}) %all-gather.14.cloned.1.call-update) | async-done | bytes 6291472 | tf_op jit(solution)/shard_map/all_gather | solution.py:117
  781.0 23.2 multiply_convert_fusion.6
  804.2 15.0 convolution_convert_fusion.4
  831.0 97.5 %reduce-scatter.5.cloned.1.call-done = bf16[384,2048]{1,0:T(8,128)(2,1)} async-done(((bf16[1536,2048]{1,0:T(8,128)(2,1)}), bf16[384,2048]{1,0:T(8,128)(2,1)}) %reduce-scatter.5.cloned.1.call-update) | async-done | bytes 1572880 | tf_op jit(solution)/shard_map/reduce_scatter | solution.py:185
  936.3 18.5 gather_fusion
  968.3 14.8 mul.513
  1001.2 20.0 gather_fusion.2
  1021.2 32.6 %all-to-all-done = bf16[8,256,2048]{2,1,0:T(8,128)(2,1)} async-done(((bf16[8,256,2048]{2,1,0:T(8,128)(2,1)}), bf16[8,256,2048]{2,1,0:T(8,128)(2,1)}, u32[]{:S(2)}, u32[]{:S(2)}) %all-to-all-start) | async-done | bytes 8388640 | tf_op jit(solution)/shard_map/all_to_all | solution.py:215
  1058.8 18.6 fusion.49
  1077.4 66.2 %all-gather.10.cloned.1.call-done = bf16[1,2048,1408]{2,1,0:T(8,128)(2,1)} async-done(((bf16[1,512,1408]{2,1,0:T(8,128)(2,1)}), bf16[1,2048,1408]{2,1,0:T(8,128)(2,1)}) %all-gather.10.cloned.1.call-update) | async-done | bytes 5767184 | tf_op jit(solution)/shard_map/all_gather | solution.py:119
  1143.6 18.5 fusion.45
  1162.1 88.1 %all-gather.12.cloned.1.call-done = bf16[1,1408,2048]{2,1,0:T(8,128)(2,1)} async-done(((bf16[1,1408,512]{2,1,0:T(8,128)(2,1)}), bf16[1,1408,2048]{2,1,0:T(8,128)(2,1)}) %all-gather.12.cloned.1.call-update) | async-done | bytes 5767184 | tf_op jit(solution)/shard_map/all_gather | solution.py:120
  1250.2 25.8 multiply_convert_fusion.3
  1276.0 19.3 fusion.47
  1295.3 21.6 add_convert_fusion
  1321.9 18.4 convolution_convert_fusion.3
  1340.2 75.7 %all-to-all-done.3 = bf16[8,256,2048]{2,1,0:T(8,128)(2,1)} async-done(((bf16[8,256,2048]{2,1,0:T(8,128)(2,1)}), bf16[8,256,2048]{2,1,0:T(8,128)(2,1)}, u32[]{:S(2)}, u32[]{:S(2)}) %all-to-all-start.3) | async-done | bytes 8388640 | tf_op jit(solution)/shard_map/all_to_all | solution.py:248
  1424.8 16.3 fusion.111
  1441.0 16.1 convolution_add_fusion
  1457.2 17.1 gather_fusion.3
  1474.3 12.0 reshape.487
  1486.3 28.8 all-to-all-done.1
  1515.1 17.4 gather_fusion.1
  1532.5 11.9 reshape.486
  1544.5 15.7 multiply_reduce_fusion.2
  1560.4 11.8 reduce_sum.233
  1578.6 20.7 fusion.38
  1599.4 19.4 fusion.39
  1618.9 15.2 convolution_convert_fusion.2
  1634.1 18.0 fusion.40
  1652.2 349.1 %all-reduce.13.cloned.1.call-done = f32[1536,2048]{1,0:T(8,128)} async-done(((f32[1536,2048]{1,0:T(8,128)}), f32[1536,2048]{1,0:T(8,128)}) %all-reduce.13.cloned.1.call-update) | async-done | bytes 12582928 | tf_op jit(solution)/shard_map/psum | solution.py:304
  2001.3 12.0 multiply_reduce_fusion.1
  2014.3 13.0 fusion.32
  2036.5 149.9 %while.28 = (s32[]{:T(128)}, f32[1536,4,128]{0,2,1:T(8,128)}, f32[1536,4,128]{0,2,1:T(8,128)}, f32[3,512,4,128]{3,1,0,2:T(8,128)}, s32[3]{0:T(128)S(1)}, /*index...) while((s32[]{:T(128)}, f32[1536,4,128]{0,2,1:T(8,128)}, ...), condition=%wide.region_28.29_spmd.clone, body=%wide.region_26.28_spmd.clone.sunk | while | flops 4061394944 | bytes 254870064 | solution.py:344
  2229.1 13.6 add_convert_fusion.1
  2243.4 15.0 convolution_convert_fusion
  2258.5 15.2 convolution_convert_fusion.1
  2318.3 14.1 all-reduce.3
  2340.4 200.8 %all-reduce.15.cloned.1.call-done = bf16[1536,2048]{1,0:T(8,128)(2,1)} async-done(((bf16[1536,2048]{1,0:T(8,128)(2,1)}), bf16[1536,2048]{1,0:T(8,128)(2,1)}) %all-reduce.15.cloned.1.call-update) | async-done | bytes 6291472 | tf_op jit(solution)/shard_map/psum | solution.py:364
  2549.4 40.6 %all-reduce.2 = (f32[2048]{0:T(1024)}, f32[2048]{0:T(1024)}, f32[2048]{0:T(1024)}) all-reduce(f32[2048]{0:T(1024)S(1)} %get-tuple-element.282, f32[2048]{0:T(1024)S(1)} %get-tuple-element.363, f32[2048]{0:T(1024)S(1)} %copy-done.47), channel_id=1, replica_groups=mesh['expert'=8,'fsdp'=4] {'expert','fsdp'}, use_global_device_ids=true, to_apply=%region_32.33 | all-reduce | flops 6144 | bytes 49152 | tf_op jit(solution)/shard_map/psum | solution.py:368
  2590.1 274.8 %all-reduce.19.cloned.1.call-done = (bf16[2048,512]{1,0:T(8,128)(2,1)}, bf16[2048,512]{1,0:T(8,128)(2,1)}, bf16[2048,512]{1,0:T(8,128)(2,1)}, bf16[512,2048]{1,0...) async-done(((bf16[2048,512]{1,0:T(8,128)(2,1)}, bf16[2048,512]{1,0:T(8,128)(2,1)}, bf16[2048,512]{1,0:T(8,128)(2,1)}, ...) | async-done | bytes 25690128 | tf_op jit(solution)/shard_map/psum | solution.py:370
  2894.2 94.4 %all-reduce.17.cloned.1.call-done = f32[2048,8]{0,1:T(8,128)} async-done(((f32[2048,8]{0,1:T(8,128)}), f32[2048,8]{0,1:T(8,128)}) %all-reduce.17.cloned.1.call-update) | async-done | bytes 65552 | tf_op jit(solution)/shard_map/psum | solution.py:368
  (442 shorter events, 497.5 us)
Async XLA Ops:
  7.2 227.0 %copy-start = (bf16[512,2048]{1,0:T(8,128)(2,1)S(1)}, bf16[512,2048]{1,0:T(8,128)(2,1)}, u32[]{:S(2)}) copy-start(bf16[512,2048]{1,0:T(8,128)(2,1)} %param.36) | copy-start | bytes 6291460
  7.2 120.5 %all-gather.6.cloned.1.call-start = ((), (), s32[]{:S(2)}) async-start(), calls=%async_computation.8 | async-start | bytes 7864320 | tf_op jit(solution)/shard_map/all_gather | solution.py:116
  7.9 657.1 %all-reduce.11.cloned.1.call-start = ((), (), s32[]{:S(2)}) async-start(), calls=%async_computation.9 | async-start | bytes 25165824 | tf_op jit(solution)/shard_map/psum | solution.py:174
  10.2 151.3 %copy-start.45 = (f32[2048]{0:T(1024)}, f32[2048]{0:T(1024)S(1)}, u32[]{:S(2)}) copy-start(f32[2048]{0:T(1024)S(1)} %convert_element_type.257) | copy-start | bytes 24580
  16.5 155.9 %copy-start.10 = (f32[1536,64]{1,0:T(8,128)}, f32[1536,64]{1,0:T(8,128)S(1)}, u32[]{:S(2)}) copy-start(f32[1536,64]{1,0:T(8,128)S(1)} %get-tuple-element.381) | copy-start | bytes 1179652
  132.3 29.2 copy-start.61
  240.6 540.4 %all-gather.14.cloned.1.call-start = ((), (), s32[]{:S(2)}) async-start(), calls=%async_computation.14 | async-start | bytes 7864320 | tf_op jit(solution)/shard_map/all_gather | solution.py:117
  241.3 687.1 %reduce-scatter.5.cloned.1.call-start = ((), (), s32[]{:S(2)}) async-start(), calls=%async_computation.10 | async-start | bytes 7864320 | tf_op jit(solution)/shard_map/reduce_scatter | solution.py:185
  241.4 436.9 %copy-start.37 = (f32[2048]{0:T(1024)}, f32[2048]{0:T(1024)S(1)}, u32[]{:S(2)}) copy-start(f32[2048]{0:T(1024)S(1)} %convert_element_type.267) | copy-start | bytes 24580
  686.7 18.3 slice-start.16
  691.4 239.3 %copy-start.63 = (f32[1536]{0:T(1024)}, f32[1536]{0:T(1024)S(1)}, u32[]{:S(2)}) copy-start(f32[1536]{0:T(1024)S(1)} %add_divide_fusion.2) | copy-start | bytes 18436
  691.5 13.6 slice-start.17
  819.3 239.5 %all-gather.8.cloned.1.call-start = ((), (), s32[]{:S(2)}) async-start(), calls=%async_computation.11 | async-start | bytes 7208960 | tf_op jit(solution)/shard_map/all_gather | solution.py:118
  819.9 323.7 %all-gather.10.cloned.1.call-start = ((), (), s32[]{:S(2)}) async-start(), calls=%async_computation.12 | async-start | bytes 7208960 | tf_op jit(solution)/shard_map/all_gather | solution.py:119
  931.4 23.3 copy-start.53
  954.8 99.0 %all-to-all-start = ((bf16[8,256,2048]{2,1,0:T(8,128)(2,1)}), bf16[8,256,2048]{2,1,0:T(8,128)(2,1)}, u32[]{:S(2)}, u32[]{:S(2)}) async-start(bf16[8,256,2048]{2,1,0:T(8,128)(2,1)} %bitcast.188), calls=%async_computation.1 | async-start | bytes 16777216 | tf_op jit(solution)/shard_map/all_to_all | solution.py:215
  959.7 290.5 %all-gather.12.cloned.1.call-start = ((), (), s32[]{:S(2)}) async-start(), calls=%async_computation.13 | async-start | bytes 7208960 | tf_op jit(solution)/shard_map/all_gather | solution.py:120
  968.3 14.8 copy-start.39
  1053.8 196.4 %all-to-all-start.2 = ((bf16[8,256,2048]{2,1,0:T(8,128)(2,1)}), bf16[8,256,2048]{2,1,0:T(8,128)(2,1)}, u32[]{:S(2)}, u32[]{:S(2)}) async-start(bf16[8,256,2048]{2,1,0:T(8,128)(2,1)} %bitcast.189), calls=%async_computation.3 | async-start | bytes 16777216 | tf_op jit(solution)/shard_map/all_to_all | solution.py:233
  1316.9 99.1 %all-to-all-start.3 = ((bf16[8,256,2048]{2,1,0:T(8,128)(2,1)}), bf16[8,256,2048]{2,1,0:T(8,128)(2,1)}, u32[]{:S(2)}, u32[]{:S(2)}) async-start(bf16[8,256,2048]{2,1,0:T(8,128)(2,1)} %bitcast.197), calls=%async_computation.4 | async-start | bytes 16777216 | tf_op jit(solution)/shard_map/all_to_all | solution.py:248
  1415.9 99.2 %all-to-all-start.1 = ((bf16[8,256,2048]{2,1,0:T(8,128)(2,1)}), bf16[8,256,2048]{2,1,0:T(8,128)(2,1)}, u32[]{:S(2)}, u32[]{:S(2)}) async-start(bf16[8,256,2048]{2,1,0:T(8,128)(2,1)} %bitcast.196), calls=%async_computation.2 | async-start | bytes 16777216 | tf_op jit(solution)/shard_map/all_to_all | solution.py:220
  1421.0 580.3 %all-reduce.13.cloned.1.call-start = ((), (), s32[]{:S(2)}) async-start(), calls=%async_computation.15 | async-start | bytes 25165824 | tf_op jit(solution)/shard_map/psum | solution.py:304
  1421.1 19.9 slice-start.18
  1424.7 16.3 slice-start.19
  1544.4 15.8 copy-start.42
  1544.4 15.9 copy-start.36
  1544.5 15.9 copy-start.50
  1544.5 15.9 copy-start.58
  1578.6 720.5 %reduce-scatter.7.cloned.1.call-start = ((), (), s32[]{:S(2)}) async-start(), calls=%async_computation.18 | async-start | bytes 7208960 | tf_op jit(solution)/shard_map/reduce_scatter | solution.py:250
  1599.4 702.9 %reduce-scatter.9.cloned.1.call-start = ((), (), s32[]{:S(2)}) async-start(), calls=%async_computation.19 | async-start | bytes 7208960 | tf_op jit(solution)/shard_map/reduce_scatter | solution.py:256
  1618.8 696.1 %reduce-scatter.11.cloned.1.call-start = ((), (), s32[]{:S(2)}) async-start(), calls=%async_computation.20 | async-start | bytes 7208960 | tf_op jit(solution)/shard_map/reduce_scatter | solution.py:262
  1652.1 349.2 %copy-start.38 = (f32[2048]{0:T(1024)S(1)}, f32[2048]{0:T(1024)}, u32[]{:S(2)}) copy-start(f32[2048]{0:T(1024)} %copy-done.37) | copy-start | bytes 24580
  1652.1 361.3 %copy-start.44 = (f32[1536]{0:T(1024)S(1)}, f32[1536]{0:T(1024)}, u32[]{:S(2)}) copy-start(f32[1536]{0:T(1024)} %copy-done.43) | copy-start | bytes 18436
  1652.1 361.3 %copy-start.48 = (f32[1536]{0:T(1024)S(1)}, f32[1536]{0:T(1024)}, u32[]{:S(2)}) copy-start(f32[1536]{0:T(1024)} %get-tuple-element.383) | copy-start | bytes 18436
  1652.1 889.0 %all-reduce.15.cloned.1.call-start = ((), (), s32[]{:S(2)}) async-start(), calls=%async_computation.16 | async-start | bytes 12582912 | tf_op jit(solution)/shard_map/psum | solution.py:364
  2001.3 12.9 copy-start.4
  2118.4 13.8 slice-start.3
  2169.0 13.9 slice-start.3
  2211.3 17.8 copy-start.12
  2242.8 622.1 %all-reduce.19.cloned.1.call-start = ((), (), s32[]{:S(2)}) async-start(), calls=%async_computation.21 | async-start | bytes 51380224 | tf_op jit(solution)/shard_map/psum | solution.py:370
  2243.4 30.2 %slice-start.5 = ((s8[6291456]{0:T(1024)(128)(4,1)}), s8[2097152]{0:T(1024)(128)(4,1)S(1)}, s32[]{:S(2)}) async-start(s8[6291456]{0:T(1024)(128)(4,1)} %bitcast.190), calls=%async_computation.27 | async-start | bytes 4194304
  2258.5 15.2 slice-start.6
  2258.5 15.2 copy-start.23
  2258.5 15.2 copy-start.46
  2258.5 15.2 copy-start.62
  2295.3 693.2 %all-reduce.17.cloned.1.call-start = ((), (), s32[]{:S(2)}) async-start(), calls=%async_computation.17 | async-start | bytes 131072 | tf_op jit(solution)/shard_map/psum | solution.py:368
  2299.0 35.0 %copy-start.65 = (f32[384]{0:T(512)S(1)}, f32[384]{0:T(512)}, u32[]{:S(2)}) copy-start(f32[384]{0:T(512)} %get-tuple-element.350) | copy-start | bytes 4612
  2340.4 209.1 %copy-start.47 = (f32[2048]{0:T(1024)S(1)}, f32[2048]{0:T(1024)}, u32[]{:S(2)}) copy-start(f32[2048]{0:T(1024)} %get-tuple-element.347) | copy-start | bytes 24580
  (82 other events, 510.1 us)
Sparse Core Ops, SparseCore 0:
  9.6 118.0 all-gather.5
  240.7 424.3 all-reduce.10
  666.6 114.2 all-gather.13
  819.4 108.9 reduce-scatter.4
  929.8 107.2 all-gather.7
  1038.5 104.9 all-gather.9
  1145.2 104.9 all-gather.11
  1578.7 422.5 all-reduce.12
  2003.6 101.1 reduce-scatter.6
  2107.0 102.7 reduce-scatter.8
  2212.1 102.7 reduce-scatter.10
  2317.7 223.3 all-reduce.14
  2547.4 317.3 all-reduce.18
  2870.9 117.6 all-reduce.16
where the time goes:
time: 3010 us; the launch traced here: 3000 us
  waiting for transfers between devices  1920 us (64%)
  matrix products  552 us (18%)
  other arithmetic  232 us (8%)
  local copies, waits for them, and re-layouts  193 us (6%)
  blocking collectives  54.7 us (2%)
    psum x1, waiting for transfers between devices, shards(): attn_out = lax.psum(attn_partial, 'fsdp')  424 us
    psum x1, waiting for transfers between devices, shards(): dh_second = lax.psum(dh_partial, 'fsdp')  349 us
    psum x1, waiting for transfers between devices, shards(): lax.psum(matmul_tn(normed_first, d_query_pre).astype(jnp.bfloat16), 'expe...  275 us
    psum x1, waiting for transfers between devices, shards(): lax.psum(dh_first_part.astype(jnp.bfloat16), 'fsdp').astype(jnp.float32)  201 us
    dot_general x10, matrix products, matmul_nt(): lax.dot_general(left_matrix, right_matrix, (((1,), (1,)), ((), ())), pref...  163 us
    dot_general x12, matrix products, matmul(): jnp.dot(left_matrix, right_matrix, preferred_element_type=jnp.float32)  130 us
    dot_general x10, matrix products, matmul_tn(): lax.dot_general(left_matrix, right_matrix, (((0,), (0,)), ((), ())), pref...  125 us
    all_gather x1, waiting for transfers between devices, shards(): lax.all_gather(tokens, 'fsdp', axis=0, tiled=True)  111 us
  transfers between devices with their start and end apart: 18, of which 14 were waited for; matrix products, arithmetic and copies ran while one was open for 23% of the time, Pallas kernels for 0%

commit v1 on v0

v1 whole, which is shorter than its diff:
```python
import math

import jax
import jax.numpy as jnp
from jax import lax
from jax.sharding import PartitionSpec as P

HEAD_DIM = 128
TOP = 4


EPSILON = 1e-06
THETA = 1000000.0
MASKED = -1e30
PRECISE = lax.Precision.HIGHEST


def rms_rate(values):
    return lax.rsqrt(jnp.mean(values * values, axis=-1, keepdims=True) + EPSILON)


def token_layout(lengths, count):
    ends = jnp.cumsum(lengths)
    places = jnp.arange(count, dtype=jnp.int32)
    passed = (places[:, None] >= ends[None, :]).astype(jnp.int32)
    segment = jnp.sum(passed, axis=1)
    start = jnp.sum(passed * lengths[None, :], axis=1)
    return (segment, places - start)


def rotary_tables(positions, width):
    half_width = width // 2
    inverse = THETA ** (-2.0 * jnp.arange(half_width, dtype=jnp.float32) / width)
    angle = positions.astype(jnp.float32)[:, None] * inverse[None, :]
    return (jnp.cos(angle)[:, None, :], jnp.sin(angle)[:, None, :])


def rotate(values, cosine, sine):
    half_width = values.shape[-1] // 2
    first_half = values[..., :half_width]
    second_half = values[..., half_width:]
    return jnp.concatenate(
        [first_half * cosine - second_half * sine, second_half * cosine + first_half * sine],
        axis=-1,
    )


def rotate_back(grads, cosine, sine):
    half_width = grads.shape[-1] // 2
    first_half = grads[..., :half_width]
    second_half = grads[..., half_width:]
    return jnp.concatenate(
        [first_half * cosine + second_half * sine, second_half * cosine - first_half * sine],
        axis=-1,
    )


def matmul(left_matrix, right_matrix):
    return jnp.dot(left_matrix, right_matrix, preferred_element_type=jnp.float32)


def matmul_tn(left_matrix, right_matrix):
    return lax.dot_general(
        left_matrix, right_matrix, (((0,), (0,)), ((), ())), preferred_element_type=jnp.float32
    )


def matmul_nt(left_matrix, right_matrix):
    return lax.dot_general(
        left_matrix, right_matrix, (((1,), (1,)), ((), ())), preferred_element_type=jnp.float32
    )


def silu_parts(pre_values):
    sigma_values = jax.nn.sigmoid(pre_values)
    return (pre_values * sigma_values, sigma_values * (1.0 + pre_values * (1.0 - sigma_values)))


def norm_back(upstream, dh_values, values, rate, gain):
    gained = dh_values * gain
    return (
        upstream
        + rate * gained
        - values * rate**3 * jnp.mean(gained * values, axis=-1, keepdims=True)
    )


def shards(
    tokens,
    routes,
    seq_lengths,
    cotangent,
    norm1_gain,
    query_weight,
    query_bias,
    key_weight,
    key_bias,
    value_weight,
    value_bias,
    out_weight,
    norm2_gain,
    router_weight,
    shared_switch,
    shared_gate,
    shared_up,
    shared_down,
    expert_gate,
    expert_up,
    expert_down,
):
    own_count = tokens.shape[0]
    width = tokens.shape[1]
    members = lax.axis_size("fsdp")
    columns = lax.axis_size("expert")
    member = lax.axis_index("fsdp")
    own_start = member * own_count
    count = own_count * members
    experts_count = router_weight.shape[1]
    local_experts = experts_count // members
    capacity = 4 * own_count * TOP // (3 * experts_count)

    def own_rows(values):
        return lax.dynamic_slice_in_dim(values, own_start, own_count, 0)

    def over_members(pieces):
        return lax.all_to_all(pieces, "fsdp", split_axis=0, concat_axis=0, tiled=True)

    def over_columns(pieces):
        return lax.all_to_all(pieces, "expert", split_axis=0, concat_axis=0, tiled=True)

    def weights_in(chunk):
        rows, cols = chunk.shape
        mixed = over_columns(chunk.reshape(columns, rows // columns, cols))
        crossed = over_members(mixed.reshape(members, local_experts, rows // columns, cols))
        return lax.all_gather(crossed, "expert", axis=0, tiled=False)

    def grads_out(parts):
        merged = parts.reshape((columns * members,) + parts.shape[2:])
        summed_part = lax.psum_scatter(merged, "expert", scatter_dimension=0, tiled=True)
        crossed = over_members(summed_part)
        rows, cols = crossed.shape[2:]
        mixed = over_columns(crossed.reshape(experts_count, rows, cols))
        return mixed.reshape(1, columns * rows, cols).astype(jnp.float32)

    def rows_full(gathered):
        return gathered.transpose(2, 1, 0, 3, 4).reshape(local_experts, width, -1)

    def cols_full(gathered):
        return gathered.transpose(2, 0, 3, 1, 4).reshape(local_experts, -1, width)

    group_tokens = lax.all_gather(tokens, "fsdp", axis=0, tiled=True)
    group_routes = lax.all_gather(routes, "fsdp", axis=0, tiled=True)
    column = lax.axis_index("expert")
    out_piece_rows = out_weight.shape[0] // columns
    out_piece = lax.dynamic_slice_in_dim(out_weight, column * out_piece_rows, out_piece_rows, 0)
    out_full = lax.all_gather(out_piece, ("fsdp", "expert"), axis=0, tiled=True)
    gate_mats = rows_full(weights_in(expert_gate[0]))
    up_mats = rows_full(weights_in(expert_up[0]))
    down_mats = cols_full(weights_in(expert_down[0]))
    group_cot = lax.all_gather(cotangent, "fsdp", axis=0, tiled=True)

    local_heads = query_weight.shape[1] // HEAD_DIM
    segment, positions = token_layout(seq_lengths[0], count)
    cosine, sine = rotary_tables(positions, HEAD_DIM)
    tokens_wide = group_tokens.astype(jnp.float32)
    tokens_own_wide = tokens.astype(jnp.float32)
    rate_first = rms_rate(tokens_wide)
    gain_first = norm1_gain.astype(jnp.float32)
    normed_first = (tokens_wide * rate_first * gain_first).astype(jnp.bfloat16)
    query_pre = matmul(normed_first, query_weight) + query_bias.astype(jnp.float32)
    key_pre = matmul(normed_first, key_weight) + key_bias.astype(jnp.float32)
    value_pre = matmul(normed_first, value_weight) + value_bias.astype(jnp.float32)
    queries = rotate(query_pre.reshape(count, local_heads, HEAD_DIM), cosine, sine).astype(
        jnp.bfloat16
    )
    keys_all = rotate(key_pre.reshape(count, local_heads, HEAD_DIM), cosine, sine).astype(
        jnp.bfloat16
    )
    values_all = value_pre.reshape(count, local_heads, HEAD_DIM).astype(jnp.bfloat16)
    block_rows = math.gcd(count, 512)
    block_count = count // block_rows
    factor = 1.0 / math.sqrt(HEAD_DIM)

    def block_scores(start):
        query_rows = lax.dynamic_slice_in_dim(queries, start, block_rows, 0)
        segment_rows = lax.dynamic_slice_in_dim(segment, start, block_rows, 0)
        position_rows = lax.dynamic_slice_in_dim(positions, start, block_rows, 0)
        allowed = (segment_rows[:, None] == segment[None, :]) & (
            position_rows[:, None] >= positions[None, :]
        )
        scores = (
            jnp.einsum("qhd,khd->hqk", query_rows, keys_all, preferred_element_type=jnp.float32)
            * factor
        )
        return (query_rows, jnp.where(allowed[None], scores, MASKED))

    def forward_block(block_index):
        query_rows, scores = block_scores(block_index * block_rows)
        peak = jnp.max(scores, axis=-1, keepdims=True)
        raised = jnp.exp(scores - peak)
        total_mass = jnp.sum(raised, axis=-1, keepdims=True)
        soft_low = (raised / total_mass).astype(jnp.bfloat16)
        context = jnp.einsum(
            "hqk,khd->qhd", soft_low, values_all, preferred_element_type=jnp.float32
        )
        return (context, (peak + jnp.log(total_mass))[..., 0])

    contexts, log_mass = lax.map(forward_block, jnp.arange(block_count, dtype=jnp.int32))
    attended = contexts.reshape(count, local_heads * HEAD_DIM).astype(jnp.bfloat16)
    attended_full = lax.all_gather(attended, "fsdp", axis=1, tiled=True)
    resid_mid = tokens_wide + matmul(attended_full, out_full)
    gain_second = norm2_gain.astype(jnp.float32)
    rate_second = rms_rate(resid_mid)
    normed_second = (resid_mid * rate_second * gain_second).astype(jnp.bfloat16)
    resid_own = own_rows(resid_mid)
    rate_own = own_rows(rate_second)

    small_weight = jnp.concatenate([router_weight, shared_switch[:, None]], axis=1)
    small_pre = matmul(normed_second, small_weight)
    router_probs = jax.nn.softmax(small_pre[:, :experts_count], axis=-1)
    switch_all = jax.nn.sigmoid(small_pre[:, experts_count:])
    own_ids = member * local_experts + jnp.arange(local_experts, dtype=jnp.int32)
    gates = lax.dynamic_slice_in_dim(router_probs, member * local_experts, local_experts, 1)
    hot = jnp.sum(
        (group_routes[:, :, None] == own_ids[None, None, :]).astype(jnp.float32), axis=1
    ).reshape(members, own_count, local_experts)
    places = jnp.arange(own_count, dtype=jnp.int32)
    before = (places[:, None] > places[None, :]).astype(jnp.bfloat16)
    ranks = jnp.einsum(
        "ut,btj->bju", before, hot.astype(jnp.bfloat16), preferred_element_type=jnp.float32
    ).astype(jnp.int32)
    slots = jnp.arange(capacity, dtype=jnp.int32)
    picks = (ranks[:, :, None, :] == slots[None, None, :, None]) & (
        hot.transpose(0, 2, 1)[:, :, None, :] > 0.0
    )
    picks_low = picks.astype(jnp.bfloat16)
    gates_by_block = gates.reshape(members, own_count, local_experts).transpose(0, 2, 1)
    slot_gates = jnp.sum(jnp.where(picks, gates_by_block[:, :, None, :], 0.0), axis=-1)

    def dispatch(values, which):
        return (
            jnp.einsum(
                "bst,btd->bsd",
                picks_low[:, which],
                values.reshape(members, own_count, width),
                preferred_element_type=jnp.float32,
            )
            .astype(jnp.bfloat16)
            .reshape(members * capacity, width)
        )

    def collect(values, which):
        return jnp.einsum(
            "bst,bsd->btd",
            picks_low[:, which],
            values.reshape(members, capacity, width),
            preferred_element_type=jnp.float32,
        ).reshape(count, width)

    shared_gate_pre = matmul(normed_second, shared_gate)
    shared_up_pre = matmul(normed_second, shared_up)
    shared_silu, shared_slope = silu_parts(shared_gate_pre)
    shared_mid = (shared_silu * shared_up_pre).astype(jnp.bfloat16)
    shared_out = matmul(shared_mid, shared_down)
    grad_wide = group_cot.astype(jnp.float32)
    block_part = switch_all * shared_out
    switch_logit = (
        jnp.sum(grad_wide * shared_out, axis=-1, keepdims=True) * switch_all * (1.0 - switch_all)
    )

    d_shared_out = (switch_all * grad_wide).astype(jnp.bfloat16)
    d_shared_mid = matmul_nt(d_shared_out, shared_down)
    d_shared_gate = (d_shared_mid * shared_up_pre * shared_slope).astype(jnp.bfloat16)
    d_shared_up = (d_shared_mid * shared_silu).astype(jnp.bfloat16)
    dh_partial = matmul_nt(d_shared_gate, shared_gate) + matmul_nt(d_shared_up, shared_up)

    expert_parts = []
    d_gate_columns = []
    for which in range(local_experts):
        gate_mat, up_mat, down_mat = gate_mats[which], up_mats[which], down_mats[which]
        rows = dispatch(normed_second, which)
        expert_gate_pre = matmul(rows, gate_mat)
        expert_up_pre = matmul(rows, up_mat)
        expert_silu, expert_slope = silu_parts(expert_gate_pre)
        expert_mid = (expert_silu * expert_up_pre).astype(jnp.bfloat16)
        result = matmul(expert_mid, down_mat).astype(jnp.bfloat16)
        row_gates = slot_gates[:, which].reshape(members * capacity, 1)
        result_wide = result.astype(jnp.float32)
        block_part = block_part + collect((row_gates * result_wide).astype(jnp.bfloat16), which)
        grad_rows = dispatch(group_cot, which).astype(jnp.float32)
        d_slot_gates = jnp.sum(grad_rows * result_wide, axis=-1).reshape(members, capacity)
        d_gate_columns.append(
            jnp.sum(jnp.where(picks[:, which], d_slot_gates[:, :, None], 0.0), axis=1).reshape(count)
        )
        d_rows = (row_gates * grad_rows).astype(jnp.bfloat16)
        d_expert_mid = matmul_nt(d_rows, down_mat)
        d_expert_gate = (d_expert_mid * expert_up_pre * expert_slope).astype(jnp.bfloat16)
        d_expert_up = (d_expert_mid * expert_silu).astype(jnp.bfloat16)
        d_in = (matmul_nt(d_expert_gate, gate_mat) + matmul_nt(d_expert_up, up_mat)).astype(
            jnp.bfloat16
        )
        dh_partial = dh_partial + collect(d_in, which)
        expert_parts.append((rows, d_expert_gate, d_expert_up, expert_mid, d_rows))

    d_gates = jnp.stack(d_gate_columns, axis=1)
    d_choice = lax.dynamic_update_slice_in_dim(
        jnp.zeros_like(router_probs), d_gates, member * local_experts, 1
    )
    d_logits = router_probs * (d_choice - jnp.sum(gates * d_gates, axis=-1, keepdims=True))
    d_small = jnp.concatenate([d_logits, switch_logit], axis=1)
    d_small_high = d_small.astype(jnp.bfloat16)
    d_small_low = (d_small - d_small_high.astype(jnp.float32)).astype(jnp.bfloat16)
    d_small_both = jnp.concatenate([d_small_high, d_small_low], axis=1)
    small_both = jnp.concatenate([small_weight, small_weight], axis=1)
    dh_partial = dh_partial + matmul_nt(d_small_both, small_both)
    small_part = matmul_tn(normed_second, d_small_both)
    small_part = small_part[:, : experts_count + 1] + small_part[:, experts_count + 1 :]

    block_own = lax.psum_scatter(
        block_part.astype(jnp.bfloat16), "fsdp", scatter_dimension=0, tiled=True
    ).astype(jnp.float32)
    block_out = (resid_own + block_own).astype(jnp.bfloat16)
    dh_second_own = lax.psum_scatter(
        dh_partial.astype(jnp.bfloat16), "fsdp", scatter_dimension=0, tiled=True
    ).astype(jnp.float32)

    def pieces_rows(grads):
        return (
            jnp.stack(grads)
            .astype(jnp.bfloat16)
            .reshape(local_experts, members, columns, -1, grads[0].shape[1])
            .transpose(2, 1, 0, 3, 4)
        )

    def pieces_cols(grads):
        return (
            jnp.stack(grads)
            .astype(jnp.bfloat16)
            .reshape(local_experts, columns, -1, members, width // members)
            .transpose(1, 3, 0, 2, 4)
        )

    expert_gate_grad = grads_out(pieces_rows([matmul_tn(p[0], p[1]) for p in expert_parts]))
    expert_up_grad = grads_out(pieces_rows([matmul_tn(p[0], p[2]) for p in expert_parts]))
    expert_down_grad = grads_out(pieces_cols([matmul_tn(p[3], p[4]) for p in expert_parts]))
    shared_down_grad = matmul_tn(shared_mid, d_shared_out)
    shared_gate_grad = matmul_tn(normed_second, d_shared_gate)
    shared_up_grad = matmul_tn(normed_second, d_shared_up)

    grad_own = cotangent.astype(jnp.float32)
    d_resid_own = norm_back(grad_own, dh_second_own, resid_own, rate_own, gain_second)
    d_attn_own = d_resid_own.astype(jnp.bfloat16)
    norm2_part = jnp.sum(dh_second_own * resid_own * rate_own, axis=0)
    d_attended_own = matmul_nt(d_attn_own, out_full).astype(jnp.bfloat16)
    d_context = over_members(
        d_attended_own.reshape(own_count, members, -1).transpose(1, 0, 2)
    ).reshape(count, local_heads, HEAD_DIM)
    d_attn_out = lax.all_gather(d_attn_own, "fsdp", axis=0, tiled=True)
    out_grad = matmul_tn(attended, d_attn_out)

    def backward_block(carry, block_index):
        key_acc, value_acc = carry
        start = block_index * block_rows
        query_rows, scores = block_scores(start)
        grad_rows = lax.dynamic_slice_in_dim(d_context, start, block_rows, 0)
        soft_weights = jnp.exp(scores - log_mass[block_index][..., None])
        d_soft = jnp.einsum(
            "qhd,khd->hqk", grad_rows, values_all, preferred_element_type=jnp.float32
        )
        inner = jnp.sum(soft_weights * d_soft, axis=-1, keepdims=True)
        d_scores = (soft_weights * (d_soft - inner)).astype(jnp.bfloat16)
        d_query = (
            jnp.einsum("hqk,khd->qhd", d_scores, keys_all, preferred_element_type=jnp.float32)
            * factor
        )
        key_acc = (
            key_acc
            + jnp.einsum("hqk,qhd->khd", d_scores, query_rows, preferred_element_type=jnp.float32)
            * factor
        )
        value_acc = value_acc + jnp.einsum(
            "hqk,qhd->khd",
            soft_weights.astype(jnp.bfloat16),
            grad_rows,
            preferred_element_type=jnp.float32,
        )
        return ((key_acc, value_acc), d_query)

    zero_heads = jnp.zeros((count, local_heads, HEAD_DIM), jnp.float32)
    (key_grad, value_grad), query_blocks = lax.scan(
        backward_block, (zero_heads, zero_heads), jnp.arange(block_count, dtype=jnp.int32)
    )
    query_grad = query_blocks.reshape(count, local_heads, HEAD_DIM)
    d_query_pre = (
        rotate_back(query_grad, cosine, sine)
        .astype(jnp.bfloat16)
        .reshape(count, local_heads * HEAD_DIM)
    )
    d_key_pre = (
        rotate_back(key_grad, cosine, sine)
        .astype(jnp.bfloat16)
        .reshape(count, local_heads * HEAD_DIM)
    )
    d_value_pre = value_grad.astype(jnp.bfloat16).reshape(count, local_heads * HEAD_DIM)
    dh_first_part = (
        matmul_nt(d_query_pre, query_weight)
        + matmul_nt(d_key_pre, key_weight)
        + matmul_nt(d_value_pre, value_weight)
    )
    norm1_part = jnp.sum(dh_first_part * (tokens_wide * rate_first), axis=0)
    dh_first_own = lax.psum_scatter(
        dh_first_part.astype(jnp.bfloat16), "fsdp", scatter_dimension=0, tiled=True
    ).astype(jnp.float32)
    grad_tokens = norm_back(
        d_resid_own, dh_first_own, tokens_own_wide, own_rows(rate_first), gain_first
    )

    biases = jnp.concatenate(
        [
            jnp.sum(d_pre.astype(jnp.float32), axis=0)
            for d_pre in (d_query_pre, d_key_pre, d_value_pre)
        ]
    )
    all_biases = lax.dynamic_update_slice_in_dim(
        jnp.zeros((members, biases.shape[0]), jnp.float32), biases[None], member, 0
    )
    stats = lax.psum(
        jnp.concatenate(
            [norm1_part, norm2_part, small_part.T.reshape(-1), all_biases.reshape(-1)]
        ),
        ("expert", "fsdp"),
    )
    small_sum = stats[2 * width : (3 + experts_count) * width].reshape(-1, width)
    bias_sums = lax.dynamic_index_in_dim(
        stats[(3 + experts_count) * width :].reshape(members, 3, -1), member, 0, keepdims=False
    )

    def over_groups(grad):
        return lax.psum(grad.astype(jnp.bfloat16), "expert").astype(jnp.float32)

    return (
        block_out,
        grad_tokens,
        stats[:width],
        over_groups(matmul_tn(normed_first, d_query_pre)),
        bias_sums[0],
        over_groups(matmul_tn(normed_first, d_key_pre)),
        bias_sums[1],
        over_groups(matmul_tn(normed_first, d_value_pre)),
        bias_sums[2],
        over_groups(out_grad),
        stats[width : 2 * width],
        small_sum[:experts_count].T,
        small_sum[experts_count],
        over_groups(shared_gate_grad),
        over_groups(shared_up_grad),
        over_groups(shared_down_grad),
        expert_gate_grad,
        expert_up_grad,
        expert_down_grad,
    )


def solution(mesh):
    placed = (
        P(("expert", "fsdp"), None),
        P(("expert", "fsdp"), None),
        P("expert", None),
        P(("expert", "fsdp"), None),
        P(),
        P(None, "fsdp"),
        P("fsdp"),
        P(None, "fsdp"),
        P("fsdp"),
        P(None, "fsdp"),
        P("fsdp"),
        P("fsdp", None),
        P(),
        P(),
        P(),
        P(None, "fsdp"),
        P(None, "fsdp"),
        P("fsdp", None),
        P("expert", "fsdp", None),
        P("expert", "fsdp", None),
        P("expert", None, "fsdp"),
    )
    return jax.shard_map(
        shards,
        mesh=mesh,
        in_specs=placed,
        out_specs=(
            P(("expert", "fsdp"), None),
            P(("expert", "fsdp"), None),
            P(),
            P(None, "fsdp"),
            P("fsdp"),
            P(None, "fsdp"),
            P("fsdp"),
            P(None, "fsdp"),
            P("fsdp"),
            P("fsdp", None),
            P(),
            P(),
            P(),
            P(None, "fsdp"),
            P(None, "fsdp"),
            P("fsdp", None),
            P("expert", "fsdp", None),
            P("expert", "fsdp", None),
            P("expert", None, "fsdp"),
        ),
        check_vma=False,
    )
```

time: 3010 us -> 2230 us (0.74)
  waiting for transfers between devices: 1920 us -> 756 us
  blocking collectives: 54.7 us -> 363 us
  matrix products: 552 us -> 647 us
  other arithmetic: 232 us -> 197 us
    psum x5 -> x2, waiting for transfers between devices: 1340 us -> 317 us  [the longest x1 317 us: over_groups(): return lax.psum(grad.astype(jnp.bfloat16), 'expert').astype(jnp.float32)]
    all_to_all x0 -> x7, blocking collectives: none -> 290 us  [the longest x3 187 us: over_members(): lax.all_to_all(pieces, 'fsdp', split_axis=0, concat_axis=0, tiled=True)]
    all_gather x5 -> x8, waiting for transfers between devices: 329 us -> 125 us  [the longest x1 109 us: shards(): group_tokens = lax.all_gather(tokens, 'fsdp', axis=0, tiled=True)]
    slice x1 -> x14, local copies, waits for them, and re-layouts: 0.29 us -> 75.1 us  [the longest x3 24 us: shards(): down_mats[which]]
    gather x4 -> x0, local copies, waits for them, and re-layouts: 73 us -> none  [the longest x1 20 us: shards(): send_grads = padded_grads[slot_pair].reshape(experts_count, capacity, width)]
    all_gather x0 -> x1, blocking collectives: none -> 72.8 us  [shards(): group_routes = lax.all_gather(routes, 'fsdp', axis=0, tiled=True)]
    reduce_scatter x4 -> x6, waiting for transfers between devices: 107 us -> 179 us  [the longest x1 110 us: shards(): lax.psum_scatter(dh_partial.astype(jnp.bfloat16), 'fsdp', scatter_dimensi...]
    psum x2 -> x0, blocking collectives: 54.7 us -> none  [the longest x1 40.6 us: shards(): lax.psum((norm1_part, norm2_part, router_part, switch_part), ('expert', '...]
  transfers between devices with their start and end apart: 18 -> 22, of which waited for: 14 -> 10; matrix products, arithmetic and copies ran while one was open for 23% -> 35% of each run, Pallas kernels for 0% -> 0%
where the time goes in v1:
time: 2230 us; the launch traced here: 2220 us
  waiting for transfers between devices  756 us (34%)
  matrix products  647 us (29%)
  blocking collectives  363 us (16%)
  local copies, waits for them, and re-layouts  204 us (9%)
  other arithmetic  197 us (9%)
  starting transfers between devices  26.8 us (1%)
    psum x1, waiting for transfers between devices, over_groups(): return lax.psum(grad.astype(jnp.bfloat16), 'expert').astype(jnp.float32)  317 us
    all_to_all x3, blocking collectives, over_members(): lax.all_to_all(pieces, 'fsdp', split_axis=0, concat_axis=0, tiled=True)  187 us
    dot_general x14, matrix products, matmul_nt(): lax.dot_general(left_matrix, right_matrix, (((1,), (1,)), ((), ())), pref...  180 us
    dot_general x14, matrix products, matmul(): jnp.dot(left_matrix, right_matrix, preferred_element_type=jnp.float32)  153 us
    dot_general x14, matrix products, matmul_tn(): lax.dot_general(left_matrix, right_matrix, (((0,), (0,)), ((), ())), pref...  120 us
    reduce_scatter x1, waiting for transfers between devices, shards(): lax.psum_scatter(dh_partial.astype(jnp.bfloat16), 'fsdp', scatter_dimensi...  110 us
    all_gather x1, waiting for transfers between devices, shards(): group_tokens = lax.all_gather(tokens, 'fsdp', axis=0, tiled=True)  109 us
    all_to_all x4, waiting for transfers between devices, over_members(): lax.all_to_all(pieces, 'fsdp', split_axis=0, concat_axis=0, tiled=True)  107 us
  transfers between devices with their start and end apart: 22, of which 10 were waited for; matrix products, arithmetic and copies ran while one was open for 35% of the time, Pallas kernels for 0%

profile of v1, /device:TPU:0, one launch (start us, length us, event | category | flops | bytes accessed | tf_op | source)
XLA Modules:
  0.0 2220.0 jit_solution(3053894943959940099)
XLA Ops:
  19.0 108.7 %all-gather.12.cloned.1.call-done = bf16[1536,2048]{1,0:T(8,128)(2,1)} async-done(((bf16[384,2048]{1,0:T(8,128)(2,1)}), bf16[1536,2048]{1,0:T(8,128)(2,1)}) %all-gather.12.cloned.1.call-update) | async-done | bytes 6291472 | tf_op jit(solution)/shard_map/all_gather | solution.py:151
  181.5 48.5 %while.27 = (s32[]{:T(128)}, bf16[3,512,4,128]{3,1,2,0:T(8,128)(2,1)}, f32[3,4,512]{2,1,0:T(4,128)}, s32[3]{0:T(128)S(1)}, s32[1536]{0:T(1024)S(1)}, /*index=5*/...) while((s32[]{:T(128)}, ...), condition=%wide.region_7.8_spmd, body=%wide.region_4.7_spmd.sunk | while | flops 1650718720 | bytes 51995872 | solution.py:208
  235.4 25.1 %all_to_all.65 = bf16[8,64,1408]{2,1,0:T(8,128)(2,1)S(1)} all-to-all(bf16[8,64,1408]{2,1,0:T(8,128)(2,1)} %bitcast.489), channel_id=1, replica_groups=mesh['expert'=8,'fsdp'=4] {'expert'}, dimensions={0} | all-to-all | bytes 2883584 | tf_op jit(solution)/shard_map/all_to_all | solution.py:129
  260.4 48.2 %all_to_all.66 = bf16[4,2,64,1408]{3,2,1,0:T(8,128)(2,1)} all-to-all(bf16[4,2,64,1408]{3,2,1,0:T(8,128)(2,1)S(1)} %bitcast.467), channel_id=1, replica_groups=mesh['expert'=8,'fsdp'=4] {'fsdp'}, dimensions={0} | all-to-all | bytes 2883584 | tf_op jit(solution)/shard_map/all_to_all | solution.py:126
  308.7 31.2 %all_to_all.67 = bf16[8,64,1408]{2,1,0:T(8,128)(2,1)S(1)} all-to-all(bf16[8,64,1408]{2,1,0:T(8,128)(2,1)} %bitcast.490), channel_id=1, replica_groups=mesh['expert'=8,'fsdp'=4] {'expert'}, dimensions={0} | all-to-all | bytes 2883584 | tf_op jit(solution)/shard_map/all_to_all | solution.py:129
  339.9 64.2 %all_to_all.68 = bf16[4,2,64,1408]{3,2,1,0:T(8,128)(2,1)} all-to-all(bf16[4,2,64,1408]{3,2,1,0:T(8,128)(2,1)S(1)} %bitcast.468), channel_id=1, replica_groups=mesh['expert'=8,'fsdp'=4] {'fsdp'}, dimensions={0} | all-to-all | bytes 2883584 | tf_op jit(solution)/shard_map/all_to_all | solution.py:126
  404.2 24.2 %all_to_all.69 = bf16[8,176,512]{2,1,0:T(8,128)(2,1)} all-to-all(bf16[8,176,512]{2,1,0:T(8,128)(2,1)S(1)} %bitcast.491), channel_id=1, replica_groups=mesh['expert'=8,'fsdp'=4] {'expert'}, dimensions={0} | all-to-all | bytes 2883584 | tf_op jit(solution)/shard_map/all_to_all | solution.py:129
  432.8 72.8 %all_gather.39 = s32[1536,4]{0,1:T(4,128)S(1)} all-gather(s32[384,4]{0,1:T(4,128)S(1)} %copy-done.78), channel_id=1, replica_groups=mesh['expert'=8,'fsdp'=4] {'fsdp'}, dimensions={0}, use_global_device_ids=true | all-gather | bytes 30720 | tf_op jit(solution)/shard_map/all_gather | solution.py:152
  518.7 22.2 multiply_reduce_fusion.1
  554.5 13.6 fusion.129
  568.1 15.7 multiply_convert_fusion.4
  583.9 16.9 fusion.34
  617.2 22.8 %multiply_convert_fusion.2 = (bf16[1536,1408]{1,0:T(8,128)(2,1)}, bf16[1536,1408]{1,0:T(8,128)(2,1)}) fusion(f32[1536,1408]{1,0:T(8,128)} %fusion.129, f32[1536,1408]{1,0:T(8,128)} %get-tuple-element.407, bf16[1408,2048]{1,0:T(8,128)(2,1)} %param.42, bf16[1536,2048]{1,0:T(8,128)(2,1)} %all-gather.18.cloned.1.call-done, f32[1536]{0:T(1024)S(1)} %reduce.3), kind=kOutput, calls=%fused_computation.67 | convolution fusion | flops 8895922176 | bytes 38017024 | tf_op jit(solution)/shard_map/dot_general | solution.py:69
  640.0 16.5 fusion.132
  656.5 14.9 fusion.133
  671.4 10.0 fusion.123
  688.2 10.0 fusion.124
  703.9 16.7 all-gather.26.cloned.1.call-done
  720.6 9.9 fusion.125
  761.6 13.3 fusion.43
  815.1 13.0 fusion.41
  835.6 15.9 multiply_convert_fusion.7
  854.3 14.5 multiply_convert_fusion.5
  868.8 10.9 fusion.134
  879.7 11.3 add_convert_fusion.1
  919.3 19.3 fusion.37
  939.7 109.9 %reduce-scatter.9.cloned.1.call-done = bf16[384,2048]{1,0:T(8,128)(2,1)} async-done(((bf16[1536,2048]{1,0:T(8,128)(2,1)}), bf16[384,2048]{1,0:T(8,128)(2,1)}) %reduce-scatter.9.cloned.1.call-update) | async-done | bytes 1572880 | tf_op jit(solution)/shard_map/reduce_scatter | solution.py:323
  1153.1 11.0 convert_bitcast_fusion.5
  1200.1 14.2 all-to-all-done.6
  1217.9 168.9 %while.28 = (s32[]{:T(128)}, f32[1536,4,128]{0,2,1:T(8,128)}, f32[1536,4,128]{0,2,1:T(8,128)}, f32[3,512,4,128]{3,1,0,2:T(8,128)}, s32[3]{0:T(128)S(1)}, /*index...) while((s32[]{:T(128)}, f32[1536,4,128]{0,2,1:T(8,128)}, ...), condition=%wide.region_24.25_spmd.clone, body=%wide.region_22.24_spmd.clone.sunk | while | flops 4061394944 | bytes 224461360 | solution.py:390
  1231.7 12.2 multiply_reduce_fusion.4
  1273.9 10.6 fusion.251
  1287.1 12.0 multiply_reduce_fusion.4
  1342.7 12.0 multiply_reduce_fusion.4
  1413.2 10.3 fusion.137
  1430.1 15.5 fusion.32
  1458.1 12.0 fusion.38
  1470.2 14.7 convolution_convert_fusion
  1484.9 15.2 convolution_convert_fusion.1
  1500.1 12.4 convolution_convert_fusion.2
  1541.5 34.5 %all-to-all-done.11 = bf16[4,2,176,512]{3,2,1,0:T(8,128)(2,1)S(1)} async-done(((bf16[4,2,176,512]{3,2,1,0:T(8,128)(2,1)}), bf16[4,2,176,512]{3,2,1,0:T(8,128)(2,1)S(1)}, u32[]{:S(2)}, u32[]{:S(2)}) %all-to-all-start.11) | async-done | bytes 1441824 | tf_op jit(solution)/shard_map/all_to_all | solution.py:126
  1580.7 58.5 %all-to-all-done.9 = bf16[4,2,64,1408]{3,2,1,0:T(8,128)(2,1)S(1)} async-done(((bf16[4,2,64,1408]{3,2,1,0:T(8,128)(2,1)}), bf16[4,2,64,1408]{3,2,1,0:T(8,128)(2,1)S(1)}, u32[]{:S(2)}, u32[]{:S(2)}) %all-to-all-start.9) | async-done | bytes 1441824 | tf_op jit(solution)/shard_map/all_to_all | solution.py:126
  1639.2 74.2 %all_to_all.70 = bf16[4,2,64,1408]{3,2,1,0:T(8,128)(2,1)} all-to-all(bf16[4,2,64,1408]{3,2,1,0:T(8,128)(2,1)} %reduce-scatter.13.cloned.1.call-done), channel_id=1, replica_groups=mesh['expert'=8,'fsdp'=4] {'fsdp'}, dimensions={0} | all-to-all | bytes 2883584 | tf_op jit(solution)/shard_map/all_to_all | solution.py:126
  1713.4 23.4 %all_to_all.71 = bf16[8,176,512]{2,1,0:T(8,128)(2,1)S(1)} all-to-all(bf16[8,176,512]{2,1,0:T(8,128)(2,1)} %bitcast.466), channel_id=1, replica_groups=mesh['expert'=8,'fsdp'=4] {'expert'}, dimensions={0} | all-to-all | bytes 2883584 | tf_op jit(solution)/shard_map/all_to_all | solution.py:129
  1745.9 14.9 all-to-all-done.10
  1774.5 10.1 all-to-all-done.8
  1790.3 68.9 %reduce-scatter.7.cloned.1.call-done = bf16[384,2048]{1,0:T(8,128)(2,1)} async-done(((bf16[1536,2048]{1,0:T(8,128)(2,1)}), bf16[384,2048]{1,0:T(8,128)(2,1)}) %reduce-scatter.7.cloned.1.call-update) | async-done | bytes 1572880 | tf_op jit(solution)/shard_map/reduce_scatter | solution.py:319
  1865.8 317.2 %all-reduce.6.cloned.1.call-done = (bf16[2048,512]{1,0:T(8,128)(2,1)}, bf16[2048,512]{1,0:T(8,128)(2,1)}, bf16[2048,512]{1,0:T(8,128)(2,1)}, bf16[512,2048]{1,0:...) async-done(((bf16[2048,512]{1,0:T(8,128)(2,1)}, bf16[2048,512]{1,0:T(8,128)(2,1)}, bf16[2048,512]{1,0:T(8,128)(2,1)}, ...) | async-done | bytes 25690128 | tf_op jit(solution)/shard_map/psum | solution.py:439
  (570 shorter events, 688.7 us)
Async XLA Ops:
  7.2 154.8 %copy-start = (bf16[2048,512]{1,0:T(8,128)(2,1)S(1)}, bf16[2048,512]{1,0:T(8,128)(2,1)}, u32[]{:S(2)}) copy-start(bf16[2048,512]{1,0:T(8,128)(2,1)} %param.34) | copy-start | bytes 6291460
  7.2 120.5 %all-gather.12.cloned.1.call-start = ((), (), s32[]{:S(2)}) async-start(), calls=%async_computation.19 | async-start | bytes 7864320 | tf_op jit(solution)/shard_map/all_gather | solution.py:151
  7.9 498.7 %all-gather.18.cloned.1.call-start = ((), (), s32[]{:S(2)}) async-start(), calls=%async_computation.23 | async-start | bytes 7864320 | tf_op jit(solution)/shard_map/all_gather | solution.py:160
  8.7 510.0 %all-gather.16.cloned.1.call-start = ((), (), s32[]{:S(2)}) async-start(), calls=%async_computation.21 | async-start | bytes 8650752 | tf_op jit(solution)/shard_map/all_gather | solution.py:156
  10.4 508.2 %all-gather.14.cloned.1.call-start = ((), (), s32[]{:S(2)}) async-start(), calls=%async_computation.20 | async-start | bytes 7864320 | tf_op jit(solution)/shard_map/all_gather | solution.py:210
  11.2 150.8 %copy-start.53 = (f32[2048]{0:T(1024)}, f32[2048]{0:T(1024)S(1)}, u32[]{:S(2)}) copy-start(f32[2048]{0:T(1024)S(1)} %convert_element_type.345) | copy-start | bytes 24580
  19.0 153.4 %copy-start.19 = (f32[1536,64]{1,0:T(8,128)}, f32[1536,64]{1,0:T(8,128)S(1)}, u32[]{:S(2)}) copy-start(f32[1536,64]{1,0:T(8,128)S(1)} %get-tuple-element.388) | copy-start | bytes 1179652
  132.3 29.7 %copy-start.64 = (f32[1536]{0:T(1024)}, f32[1536]{0:T(1024)S(1)}, u32[]{:S(2)}) copy-start(f32[1536]{0:T(1024)S(1)} %add_rsqrt_fusion.1) | copy-start | bytes 18436
  230.1 30.4 %copy-start.38 = (s32[1536]{0:T(1024)}, s32[1536]{0:T(1024)S(1)}, u32[]{:S(2)}) copy-start(s32[1536]{0:T(1024)S(1)} %get-tuple-element.729) | copy-start | bytes 18436
  230.1 30.3 %copy-start.40 = (s32[1536]{0:T(1024)}, s32[1536]{0:T(1024)S(1)}, u32[]{:S(2)}) copy-start(s32[1536]{0:T(1024)S(1)} %get-tuple-element.730) | copy-start | bytes 18436
  235.3 436.0 %all-gather.22.cloned.1.call-start = ((), (), s32[]{:S(2)}) async-start(), calls=%async_computation.31 | async-start | bytes 12976128 | tf_op jit(solution)/shard_map/all_gather | solution.py:135
  308.6 95.5 %copy-start.42 = (bf16[1,1408,512]{2,1,0:T(8,128)(2,1)S(1)}, bf16[1,1408,512]{2,1,0:T(8,128)(2,1)}, u32[]{:S(2)}) copy-start(bf16[1,1408,512]{2,1,0:T(8,128)(2,1)} %param.45) | copy-start | bytes 4325380
  308.7 379.5 %all-gather.24.cloned.1.call-start = ((), (), s32[]{:S(2)}) async-start(), calls=%async_computation.32 | async-start | bytes 12976128 | tf_op jit(solution)/shard_map/all_gather | solution.py:135
  404.1 28.6 %copy-start.80 = (bf16[2048]{0:T(1024)(128)(2,1)S(1)}, bf16[2048]{0:T(1024)(128)(2,1)}, u32[]{:S(2)}) copy-start(bf16[2048]{0:T(1024)(128)(2,1)} %param.39) | copy-start | bytes 12292
  404.1 28.7 %copy-start.78 = (s32[384,4]{0,1:T(4,128)S(1)}, s32[384,4]{0,1:T(4,128)}, u32[]{:S(2)}) copy-start(s32[384,4]{0,1:T(4,128)} %param.26) | copy-start | bytes 18436
  428.3 78.2 %all-to-all-start.5 = ((bf16[4,2,176,512]{3,2,1,0:T(8,128)(2,1)}), bf16[4,2,176,512]{3,2,1,0:T(8,128)(2,1)}, u32[]{:S(2)}, u32[]{:S(2)}) async-start(bf16[4,2,176,512]{3,2,1,0:T(8,128)(2,1)} %bitcast.27), calls=%async_computation.5 | async-start | bytes 2883584 | tf_op jit(solution)/shard_map/all_to_all | solution.py:126
  432.7 288.0 %all-gather.26.cloned.1.call-start = ((), (), s32[]{:S(2)}) async-start(), calls=%async_computation.33 | async-start | bytes 12976128 | tf_op jit(solution)/shard_map/all_gather | solution.py:135
  432.7 108.1 %copy-start.46 = (f32[2048]{0:T(1024)}, f32[2048]{0:T(1024)S(1)}, u32[]{:S(2)}) copy-start(f32[2048]{0:T(1024)S(1)} %convert_element_type.355) | copy-start | bytes 24580
  432.8 117.1 %copy-start.57 = (bf16[2048,1]{0,1:T(2,128)(2,1)}, bf16[2048,1]{0,1:T(2,128)(2,1)S(1)}, u32[]{:S(2)}) copy-start(bf16[2048,1]{0,1:T(2,128)(2,1)S(1)} %broadcast_in_dim.126) | copy-start | bytes 12292
  506.6 102.9 %copy-start.7 = (pred[4,2,256,384]{3,2,0,1:T(32,128)(4,1)}, pred[4,2,256,384]{3,2,0,1:T(32,128)(4,1)S(1)}, u32[]{:S(2)}) copy-start(pred[4,2,256,384]{3,2,0,1:T(32,128)(4,1)S(1)} %fusion.68) | copy-start | bytes 2359300
  506.6 542.9 %reduce-scatter.9.cloned.1.call-start = ((), (), s32[]{:S(2)}) async-start(), calls=%async_computation.24 | async-start | bytes 7864320 | tf_op jit(solution)/shard_map/reduce_scatter | solution.py:323
  554.5 47.0 %copy-start.43 = (f32[1536,9]{0,1:T(8,128)}, f32[1536,9]{0,1:T(8,128)S(1)}, u32[]{:S(2)}) copy-start(f32[1536,9]{0,1:T(8,128)S(1)} %fusion.96) | copy-start | bytes 165892
  554.5 29.3 %slice-start.12 = ((s8[6291456]{0:T(1024)(128)(4,1)}), s8[4194304]{0:T(1024)(128)(4,1)S(1)}, s32[]{:S(2)}) async-start(s8[6291456]{0:T(1024)(128)(4,1)} %bitcast.412), calls=%async_computation.47 | async-start | bytes 8388608
  868.8 28.7 %slice-start.16 = ((s8[5767168]{0:T(1024)(128)(4,1)}), s8[4194304]{0:T(1024)(128)(4,1)S(1)}, s32[]{:S(2)}) async-start(s8[5767168]{0:T(1024)(128)(4,1)} %bitcast.439), calls=%async_computation.51 | async-start | bytes 8388608
  938.6 110.9 %copy-start.47 = (f32[2048]{0:T(1024)S(1)}, f32[2048]{0:T(1024)}, u32[]{:S(2)}) copy-start(f32[2048]{0:T(1024)} %copy-done.46) | copy-start | bytes 24580
  938.6 590.5 %all-gather.20.cloned.1.call-start = ((), (), s32[]{:S(2)}) async-start(), calls=%async_computation.27 | async-start | bytes 7864320 | tf_op jit(solution)/shard_map/all_gather | solution.py:358
  939.6 117.9 %copy-start.60 = (f32[384]{0:T(512)}, f32[384]{0:T(512)S(1)}, u32[]{:S(2)}) copy-start(f32[384]{0:T(512)S(1)} %dynamic-slice.6) | copy-start | bytes 4612
  939.6 117.9 %copy-start.72 = (f32[384]{0:T(512)}, f32[384]{0:T(512)S(1)}, u32[]{:S(2)}) copy-start(f32[384]{0:T(512)S(1)} %fusion.107) | copy-start | bytes 4612
  1057.6 479.7 %reduce-scatter.17.cloned.1.call-start = ((), (), s32[]{:S(2)}) async-start(), calls=%async_computation.30 | async-start | bytes 12976128 | tf_op jit(solution)/shard_map/reduce_scatter | solution.py:139
  1116.3 425.2 %reduce-scatter.15.cloned.1.call-start = ((), (), s32[]{:S(2)}) async-start(), calls=%async_computation.29 | async-start | bytes 12976128 | tf_op jit(solution)/shard_map/reduce_scatter | solution.py:139
  1172.2 42.0 %all-to-all-start.6 = ((bf16[4,384,512]{2,1,0:T(8,128)(2,1)}), bf16[4,384,512]{2,1,0:T(8,128)(2,1)}, u32[]{:S(2)}, u32[]{:S(2)}) async-start(bf16[4,384,512]{2,1,0:T(8,128)(2,1)} %bitcast.435), calls=%async_computation.8 | async-start | bytes 3145728 | tf_op jit(solution)/shard_map/all_to_all | solution.py:126
  1176.6 404.1 %reduce-scatter.13.cloned.1.call-start = ((), (), s32[]{:S(2)}) async-start(), calls=%async_computation.28 | async-start | bytes 12976128 | tf_op jit(solution)/shard_map/reduce_scatter | solution.py:139
  1199.9 541.9 %all-reduce.4.cloned.1.call-start = ((), (), s32[]{:S(2)}) async-start(), calls=%async_computation.26 | async-start | bytes 229376 | tf_op jit(solution)/shard_map/psum | solution.py:427
  1446.2 341.5 %reduce-scatter.11.cloned.1.call-start = ((), (), s32[]{:S(2)}) async-start(), calls=%async_computation.25 | async-start | bytes 7864320 | tf_op jit(solution)/shard_map/reduce_scatter | solution.py:411
  1446.8 412.4 %reduce-scatter.7.cloned.1.call-start = ((), (), s32[]{:S(2)}) async-start(), calls=%async_computation.22 | async-start | bytes 7864320 | tf_op jit(solution)/shard_map/reduce_scatter | solution.py:319
  1470.1 713.0 %all-reduce.6.cloned.1.call-start = ((), (), s32[]{:S(2)}) async-start(), calls=%async_computation.34 | async-start | bytes 51380224 | tf_op jit(solution)/shard_map/psum | solution.py:439
  1470.2 29.9 %slice-start.8 = ((s8[6291456]{0:T(1024)(128)(4,1)}), s8[2097152]{0:T(1024)(128)(4,1)S(1)}, s32[]{:S(2)}) async-start(s8[6291456]{0:T(1024)(128)(4,1)} %bitcast.403), calls=%async_computation.43 | async-start | bytes 4194304
  1470.2 29.9 %slice-start.30 = ((s8[4325376]{0:T(1024)(128)(4,1)}), s8[4194304]{0:T(1024)(128)(4,1)S(1)}, s32[]{:S(2)}) async-start(s8[4325376]{0:T(1024)(128)(4,1)} %bitcast.511), calls=%async_computation.65 | async-start | bytes 8388608
  1537.3 38.7 %all-to-all-start.11 = ((bf16[4,2,176,512]{3,2,1,0:T(8,128)(2,1)}), bf16[4,2,176,512]{3,2,1,0:T(8,128)(2,1)S(1)}, u32[]{:S(2)}, u32[]{:S(2)}) async-start(bf16[4,2,176,512]{3,2,1,0:T(8,128)(2,1)} %reduce-scatter.17.cloned.1.call-done), calls=%async_computation.17 | async-start | bytes 2883584 | tf_op jit(solution)/shard_map/all_to_all | solution.py:126
  1577.1 62.1 %all-to-all-start.9 = ((bf16[4,2,64,1408]{3,2,1,0:T(8,128)(2,1)}), bf16[4,2,64,1408]{3,2,1,0:T(8,128)(2,1)S(1)}, u32[]{:S(2)}, u32[]{:S(2)}) async-start(bf16[4,2,64,1408]{3,2,1,0:T(8,128)(2,1)} %reduce-scatter.15.cloned.1.call-done), calls=%async_computation.14 | async-start | bytes 2883584 | tf_op jit(solution)/shard_map/all_to_all | solution.py:126
  1639.2 74.2 %copy-start.26 = (bf16[4,2,64,1408]{3,2,1,0:T(8,128)(2,1)}, bf16[4,2,64,1408]{3,2,1,0:T(8,128)(2,1)S(1)}, u32[]{:S(2)}) copy-start(bf16[4,2,64,1408]{3,2,1,0:T(8,128)(2,1)S(1)} %all-to-all-done.9) | copy-start | bytes 4325380
  1736.8 23.9 %all-to-all-start.10 = ((bf16[8,64,1408]{2,1,0:T(8,128)(2,1)}), bf16[8,64,1408]{2,1,0:T(8,128)(2,1)}, u32[]{:S(2)}, u32[]{:S(2)}) async-start(bf16[8,64,1408]{2,1,0:T(8,128)(2,1)} %bitcast.465), calls=%async_computation.15 | async-start | bytes 2883584 | tf_op jit(solution)/shard_map/all_to_all | solution.py:129
  1760.7 23.9 %all-to-all-start.8 = ((bf16[8,64,1408]{2,1,0:T(8,128)(2,1)}), bf16[8,64,1408]{2,1,0:T(8,128)(2,1)}, u32[]{:S(2)}, u32[]{:S(2)}) async-start(bf16[8,64,1408]{2,1,0:T(8,128)(2,1)} %bitcast.77), calls=%async_computation.12 | async-start | bytes 2883584 | tf_op jit(solution)/shard_map/all_to_all | solution.py:129
  1774.5 84.7 %copy-start.48 = (f32[2048]{0:T(1024)S(1)}, f32[2048]{0:T(1024)}, u32[]{:S(2)}) copy-start(f32[2048]{0:T(1024)} %copy-done.46) | copy-start | bytes 24580
  1774.5 84.7 %copy-start.61 = (f32[384]{0:T(512)S(1)}, f32[384]{0:T(512)}, u32[]{:S(2)}) copy-start(f32[384]{0:T(512)} %copy-done.60) | copy-start | bytes 4612
  1774.5 84.7 %copy-start.73 = (f32[384]{0:T(512)S(1)}, f32[384]{0:T(512)}, u32[]{:S(2)}) copy-start(f32[384]{0:T(512)} %copy-done.72) | copy-start | bytes 4612
  1774.5 84.7 %copy-start.75 = (f32[384]{0:T(512)S(1)}, f32[384]{0:T(512)}, u32[]{:S(2)}) copy-start(f32[384]{0:T(512)} %copy-done.74) | copy-start | bytes 4612
  1774.5 84.7 %copy-start.77 = (f32[384]{0:T(512)S(1)}, f32[384]{0:T(512)}, u32[]{:S(2)}) copy-start(f32[384]{0:T(512)} %copy-done.76) | copy-start | bytes 4612
  (117 other events, 1158.7 us)
Sparse Core Ops, SparseCore 0:
  9.6 118.0 all-gather.11
  129.3 113.5 all-gather.17
  246.3 105.7 all-gather.15
  354.1 158.3 all-gather.13
  514.3 67.1 all-gather.21
  583.2 67.7 all-gather.23
  652.9 67.6 all-gather.25
  938.7 110.7 reduce-scatter.8
  1057.7 115.8 all-gather.19
  1177.5 85.0 reduce-scatter.16
  1266.7 86.7 reduce-scatter.14
  1357.4 86.7 reduce-scatter.12
  1450.4 133.3 all-reduce.3
  1585.9 151.3 reduce-scatter.10
  1739.5 119.6 reduce-scatter.6
  1865.3 317.6 all-reduce.5

commit v2 on v1

v2 whole, which is shorter than its diff:
```python
import functools
import math

import jax
import jax.numpy as jnp
from jax import lax
from jax.experimental import pallas as pl
from jax.experimental.pallas import tpu as pltpu
from jax.sharding import PartitionSpec as P

HEAD_DIM = 128
TOP = 4


EPSILON = 1e-06
THETA = 1000000.0
MASKED = -1e30
KERNEL_VMEM = 40 * 1024 * 1024
BIG_VMEM = 58 * 1024 * 1024
NO_COST = pl.CostEstimate(flops=0, bytes_accessed=0, transcendentals=0)


def rms_rate(values):
    return lax.rsqrt(jnp.mean(values * values, axis=-1, keepdims=True) + EPSILON)


def token_layout(lengths, count):
    ends = jnp.cumsum(lengths)
    places = jnp.arange(count, dtype=jnp.int32)
    passed = (places[:, None] >= ends[None, :]).astype(jnp.int32)
    segment = jnp.sum(passed, axis=1)
    start = jnp.sum(passed * lengths[None, :], axis=1)
    return (segment, places - start)


def rotary_tables(positions, width):
    half_width = width // 2
    inverse = THETA ** (-2.0 * jnp.arange(half_width, dtype=jnp.float32) / width)
    angle = positions.astype(jnp.float32)[:, None] * inverse[None, :]
    cosine, sine = jnp.cos(angle), jnp.sin(angle)
    return (
        jnp.concatenate([cosine, cosine], axis=1),
        jnp.concatenate([-sine, sine], axis=1),
    )


def matmul(left_matrix, right_matrix):
    return jnp.dot(left_matrix, right_matrix, preferred_element_type=jnp.float32)


def matmul_tn(left_matrix, right_matrix):
    return lax.dot_general(
        left_matrix, right_matrix, (((0,), (0,)), ((), ())), preferred_element_type=jnp.float32
    )


def matmul_nt(left_matrix, right_matrix):
    return lax.dot_general(
        left_matrix, right_matrix, (((1,), (1,)), ((), ())), preferred_element_type=jnp.float32
    )


def silu_parts(pre_values):
    sigma_values = jax.nn.sigmoid(pre_values)
    return (pre_values * sigma_values, sigma_values * (1.0 + pre_values * (1.0 - sigma_values)))


def norm_back(upstream, dh_values, values, rate, gain):
    gained = dh_values * gain
    return (
        upstream
        + rate * gained
        - values * rate**3 * jnp.mean(gained * values, axis=-1, keepdims=True)
    )


def lane_turn(values):
    return pltpu.roll(values, HEAD_DIM // 2, 1)


def project_body(tokens_ref, gain_ref, weight_refs, bias_refs, cos_ref, sin_ref, outs):
    normed_ref, rate_ref, query_ref, key_ref, value_ref = outs
    wide = tokens_ref[...].astype(jnp.float32)
    rate = rms_rate(wide)
    normed = (wide * rate * gain_ref[...]).astype(jnp.bfloat16)
    normed_ref[...] = normed
    rate_ref[...] = rate
    cosine, sine = cos_ref[...], sin_ref[...]
    for place, out_ref in enumerate((query_ref, key_ref, value_ref)):
        pre = (
            jnp.dot(normed, weight_refs[place][...], preferred_element_type=jnp.float32)
            + bias_refs[place][...]
        )
        if place == 2:
            out_ref[...] = pre.astype(jnp.bfloat16)
            continue
        for head in range(pre.shape[1] // HEAD_DIM):
            part = pre[:, head * HEAD_DIM : (head + 1) * HEAD_DIM]
            turned = part * cosine + lane_turn(part) * sine
            out_ref[:, head * HEAD_DIM : (head + 1) * HEAD_DIM] = turned.astype(jnp.bfloat16)


def project(tokens, gain, weights, biases, cosine, sine, rows):
    count, width = tokens.shape
    features = weights[0].shape[1]

    def body(t, g, w0, w1, w2, b0, b1, b2, c, s, *outs):
        project_body(t, g, (w0, w1, w2), (b0, b1, b2), c, s, outs)

    def by_rows(cols):
        return pl.BlockSpec((rows, cols), lambda i: (i, 0))

    def whole(*shape):
        return pl.BlockSpec(shape, lambda i: (0, 0))

    return pl.pallas_call(
        body,
        grid=(count // rows,),
        in_specs=[by_rows(width), whole(1, width)]
        + [whole(width, features)] * 3
        + [whole(1, features)] * 3
        + [by_rows(HEAD_DIM)] * 2,
        out_specs=[by_rows(width), by_rows(1)] + [by_rows(features)] * 3,
        out_shape=[
            jax.ShapeDtypeStruct((count, width), jnp.bfloat16),
            jax.ShapeDtypeStruct((count, 1), jnp.float32),
        ]
        + [jax.ShapeDtypeStruct((count, features), jnp.bfloat16)] * 3,
        compiler_params=pltpu.CompilerParams(vmem_limit_bytes=KERNEL_VMEM),
        cost_estimate=pl.CostEstimate(
            flops=6 * count * width * features,
            bytes_accessed=4 * count * width + 6 * (count + width) * features,
            transcendentals=0,
        ),
        name="project",
    )(tokens, gain, *weights, *biases, cosine, sine)


def scores_of(lows_ref, starts_ref, query, key_ref, wide, block):
    index = pl.program_id(1)
    low = lows_ref[index]
    rows = pl.ds(pl.multiple_of(low * block, block), wide * block)
    keys = key_ref[rows, :]
    scores = lax.dot_general(
        keys, query, (((1,), (1,)), ((), ())), preferred_element_type=jnp.float32
    ) * (1.0 / math.sqrt(HEAD_DIM))
    key_place = low * block + lax.broadcasted_iota(jnp.int32, scores.shape, 0)
    query_place = index * block + lax.broadcasted_iota(jnp.int32, scores.shape, 1)
    allowed = (key_place <= query_place) & (key_place >= starts_ref[...])
    return rows, keys, jnp.where(allowed, scores, MASKED)


def attend_body(lows_ref, starts_ref, query_ref, key_ref, value_ref, out_ref, mass_ref):
    block = query_ref.shape[0]
    index = pl.program_id(1)

    def run(wide):
        rows, _, scores = scores_of(lows_ref, starts_ref, query_ref[...], key_ref, wide, block)
        peak = jnp.max(scores, axis=0, keepdims=True)
        raised = jnp.exp(scores - peak)
        total = jnp.sum(raised, axis=0, keepdims=True)
        soft = (raised * (1.0 / total)).astype(jnp.bfloat16)
        mixed = lax.dot_general(
            value_ref[rows, :], soft, (((0,), (0,)), ((), ())), preferred_element_type=jnp.float32
        )
        out_ref[...] = mixed.T.astype(jnp.bfloat16)
        mass_ref[0] = peak + jnp.log(total)

    for wide in range(1, key_ref.shape[0] // block + 1):
        pl.when(index - lows_ref[index] + 1 == wide)(functools.partial(run, wide))


def attend(lows, starts, queries, keys, values, block):
    count, features = queries.shape
    heads = features // HEAD_DIM
    by_block = pl.BlockSpec((block, HEAD_DIM), lambda h, i, *_: (i, h))
    by_head = pl.BlockSpec((count, HEAD_DIM), lambda h, i, *_: (0, h))
    return pl.pallas_call(
        attend_body,
        grid_spec=pltpu.PrefetchScalarGridSpec(
            num_scalar_prefetch=1,
            grid=(heads, count // block),
            in_specs=[
                pl.BlockSpec((1, block), lambda h, i, *_: (0, i)),
                by_block,
                by_head,
                by_head,
            ],
            out_specs=[by_block, pl.BlockSpec((1, 1, block), lambda h, i, *_: (h, 0, i))],
        ),
        out_shape=[
            jax.ShapeDtypeStruct((count, features), jnp.bfloat16),
            jax.ShapeDtypeStruct((heads, 1, count), jnp.float32),
        ],
        compiler_params=pltpu.CompilerParams(vmem_limit_bytes=KERNEL_VMEM),
        cost_estimate=pl.CostEstimate(
            flops=2 * count * count * features,
            bytes_accessed=8 * count * features,
            transcendentals=count * count * heads // 2,
        ),
        name="attend",
    )(lows, starts, queries, keys, values)


def attend_back_body(
    lows_ref, starts_ref, query_ref, key_ref, value_ref, grad_ref, mass_ref, *rest
):
    cos_ref, sin_ref, d_query_ref, d_key_ref, d_value_ref, key_sum, value_sum = rest
    block = query_ref.shape[0]
    index = pl.program_id(1)
    blocks = key_ref.shape[0] // block
    factor = 1.0 / math.sqrt(HEAD_DIM)

    def rope_back(values, rows):
        return (
            values * cos_ref[rows, :] + lane_turn(values) * -sin_ref[rows, :]
        ).astype(jnp.bfloat16)

    @pl.when(index == 0)
    def _():
        key_sum[...] = jnp.zeros_like(key_sum)
        value_sum[...] = jnp.zeros_like(value_sum)

    def run(wide):
        query, grad = query_ref[...], grad_ref[...]
        rows, keys, scores = scores_of(lows_ref, starts_ref, query, key_ref, wide, block)
        soft = jnp.exp(scores - mass_ref[0])
        d_soft = lax.dot_general(
            value_ref[rows, :], grad, (((1,), (1,)), ((), ())), preferred_element_type=jnp.float32
        )
        inner = jnp.sum(soft * d_soft, axis=0, keepdims=True)
        d_scores = (soft * (d_soft - inner)).astype(jnp.bfloat16)
        value_sum[rows, :] += jnp.dot(
            soft.astype(jnp.bfloat16), grad, preferred_element_type=jnp.float32
        )
        key_sum[rows, :] += jnp.dot(d_scores, query, preferred_element_type=jnp.float32) * factor
        d_query = lax.dot_general(
            keys, d_scores, (((0,), (0,)), ((), ())), preferred_element_type=jnp.float32
        ).T * factor
        here = pl.ds(pl.multiple_of(index * block, block), block)
        d_query_ref[...] = rope_back(d_query, here)

    for wide in range(1, blocks + 1):
        pl.when(index - lows_ref[index] + 1 == wide)(functools.partial(run, wide))

    @pl.when(index == blocks - 1)
    def _():
        d_key_ref[...] = rope_back(key_sum[...], slice(None))
        d_value_ref[...] = value_sum[...].astype(jnp.bfloat16)


def attend_back(lows, starts, queries, keys, values, grads, mass, cosine, sine, block):
    count, features = queries.shape
    heads = features // HEAD_DIM
    by_block = pl.BlockSpec((block, HEAD_DIM), lambda h, i, *_: (i, h))
    by_head = pl.BlockSpec((count, HEAD_DIM), lambda h, i, *_: (0, h))
    whole = pl.BlockSpec((count, HEAD_DIM), lambda h, i, *_: (0, 0))
    return pl.pallas_call(
        attend_back_body,
        grid_spec=pltpu.PrefetchScalarGridSpec(
            num_scalar_prefetch=1,
            grid=(heads, count // block),
            in_specs=[
                pl.BlockSpec((1, block), lambda h, i, *_: (0, i)),
                by_block,
                by_head,
                by_head,
                by_block,
                pl.BlockSpec((1, 1, block), lambda h, i, *_: (h, 0, i)),
                whole,
                whole,
            ],
            out_specs=[by_block, by_head, by_head],
            scratch_shapes=[pltpu.VMEM((count, HEAD_DIM), jnp.float32)] * 2,
        ),
        out_shape=[jax.ShapeDtypeStruct((count, features), jnp.bfloat16)] * 3,
        compiler_params=pltpu.CompilerParams(vmem_limit_bytes=KERNEL_VMEM),
        cost_estimate=NO_COST,
        name="attend_back",
    )(lows, starts, queries, keys, values, grads, mass, cosine, sine)


def settle_body(tokens_ref, attended_ref, weight_ref, gain_ref, small_ref, *outs):
    resid_ref, rate_ref, normed_ref, logit_ref = outs
    total = tokens_ref[...].astype(jnp.float32)
    members, _, features = attended_ref.shape
    for member in range(members):
        total = total + jnp.dot(
            attended_ref[member],
            weight_ref[member * features : (member + 1) * features, :],
            preferred_element_type=jnp.float32,
        )
    rate = rms_rate(total)
    normed = (total * rate * gain_ref[...]).astype(jnp.bfloat16)
    resid_ref[...] = total
    rate_ref[...] = rate
    normed_ref[...] = normed
    logit_ref[...] = jnp.dot(normed, small_ref[...], preferred_element_type=jnp.float32)


def settle(tokens, attended, weight, gain, small, rows):
    count, width = tokens.shape
    members, _, features = attended.shape

    def by_rows(cols):
        return pl.BlockSpec((rows, cols), lambda i: (i, 0))

    def whole(*shape):
        return pl.BlockSpec(shape, lambda i: (0,) * len(shape))

    return pl.pallas_call(
        settle_body,
        grid=(count // rows,),
        in_specs=[
            by_rows(width),
            pl.BlockSpec((members, rows, features), lambda i: (0, i, 0)),
            whole(width, width),
            whole(1, width),
            whole(*small.shape),
        ],
        out_specs=[by_rows(width), by_rows(1), by_rows(width), by_rows(small.shape[1])],
        out_shape=[
            jax.ShapeDtypeStruct((count, width), jnp.float32),
            jax.ShapeDtypeStruct((count, 1), jnp.float32),
            jax.ShapeDtypeStruct((count, width), jnp.bfloat16),
            jax.ShapeDtypeStruct((count, small.shape[1]), jnp.float32),
        ],
        compiler_params=pltpu.CompilerParams(vmem_limit_bytes=KERNEL_VMEM),
        cost_estimate=pl.CostEstimate(
            flops=2 * count * width * width, bytes_accessed=12 * count * width, transcendentals=0
        ),
        name="settle",
    )(tokens, attended, weight, gain, small)


def mixed_places(members, rows):
    for z in range(members):
        for q in range(members):
            yield (z * members + q) * rows, (q * members + z) * rows


def dispatch_body(members, places_ref, source_ref, target_ref):
    slots = target_ref.shape[2]
    quarter = source_ref.shape[1] // members // members
    for which in range(target_ref.shape[0]):
        place = places_ref[0, which : which + 1, :]
        picks = lax.broadcasted_iota(jnp.int32, (slots, place.shape[1]), 0) == place
        picks = picks.astype(jnp.float32).astype(jnp.bfloat16)
        values = jnp.dot(picks, source_ref[...], preferred_element_type=jnp.float32).astype(
            jnp.bfloat16
        )
        for plain, mixed in mixed_places(members, quarter):
            target_ref[which, 0, :, mixed : mixed + quarter] = values[:, plain : plain + quarter]


def dispatch(places, source, slots, members):
    experts, width = places.shape[1], source.shape[1]
    own = source.shape[0] // members
    return pl.pallas_call(
        functools.partial(dispatch_body, members),
        grid=(members,),
        in_specs=[
            pl.BlockSpec((1, experts, own), lambda b: (b, 0, 0)),
            pl.BlockSpec((own, width), lambda b: (b, 0)),
        ],
        out_specs=pl.BlockSpec((experts, 1, slots, width), lambda b: (0, b, 0, 0)),
        out_shape=jax.ShapeDtypeStruct((experts, members, slots, width), jnp.bfloat16),
        compiler_params=pltpu.CompilerParams(vmem_limit_bytes=KERNEL_VMEM),
        cost_estimate=NO_COST,
        name="dispatch",
    )(places, source).reshape(experts, members * slots, width)


def collect_body(members, scaled, places_ref, values_ref, extra_ref, *rest):
    *rest, out_ref = rest
    slots = values_ref.shape[2]
    total = 0.0
    for which in range(values_ref.shape[0]):
        place = places_ref[:, which : which + 1]
        picks = lax.broadcasted_iota(jnp.int32, (place.shape[0], slots), 1) == place
        total = total + jnp.dot(
            picks.astype(jnp.float32).astype(jnp.bfloat16),
            values_ref[which, 0],
            preferred_element_type=jnp.float32,
        )
    extra = extra_ref[...]
    if scaled:
        extra = extra * rest[0][...]
    else:
        extra = extra + jnp.dot(rest[0][...], rest[1][...], preferred_element_type=jnp.float32)
    quarter = extra.shape[1] // members // members
    for plain, mixed in mixed_places(members, quarter):
        out_ref[:, plain : plain + quarter] = (
            extra[:, plain : plain + quarter] + total[:, mixed : mixed + quarter]
        ).astype(out_ref.dtype)


def collect(places, values, extra, members, left, right=None):
    experts, _, slots, width = values.shape
    own = extra.shape[0] // members
    by_block = pl.BlockSpec((own, width), lambda b: (b, 0))
    operands = [places, values, extra]
    in_specs = [
        pl.BlockSpec((own, experts), lambda b: (b, 0)),
        pl.BlockSpec((experts, 1, slots, width), lambda b: (0, b, 0, 0)),
        by_block,
    ]
    operands.append(left)
    in_specs.append(pl.BlockSpec((own, left.shape[1]), lambda b: (b, 0)))
    if right is not None:
        operands.append(right)
        in_specs.append(pl.BlockSpec(right.shape, lambda b: (0, 0)))
    return pl.pallas_call(
        functools.partial(collect_body, members, right is None),
        grid=(members,),
        in_specs=in_specs,
        out_specs=by_block,
        out_shape=jax.ShapeDtypeStruct(extra.shape, jnp.bfloat16),
        compiler_params=pltpu.CompilerParams(vmem_limit_bytes=KERNEL_VMEM),
        cost_estimate=NO_COST,
        name="collect",
    )(*operands)


def expert_specs(experts, count, width, features, rows):
    def by_rows(cols):
        return pl.BlockSpec((1, rows, cols), lambda e, i: (e, i, 0))

    def whole(array):
        return pl.BlockSpec(
            (1,) + array.shape[1:], lambda e, i: (e, 0, 0), pipeline_mode=pl.Buffered(1)
        )

    def out(cols, kind):
        return jax.ShapeDtypeStruct((experts, count, cols), kind)

    return by_rows, whole, out


def expert_body(turned, values_ref, scale_ref, gate_ref, up_ref, down_ref, *outs):
    result_ref, mid_ref, silu_ref, up_slope_ref, *scaled_ref = outs
    values = values_ref[0]
    gate_pre = jnp.dot(values, gate_ref[0], preferred_element_type=jnp.float32)
    up_pre = jnp.dot(values, up_ref[0], preferred_element_type=jnp.float32)
    silu, slope = silu_parts(gate_pre)
    mid = (silu * up_pre).astype(jnp.bfloat16)
    mid_ref[0] = mid
    silu_ref[0] = silu
    up_slope_ref[0] = up_pre * slope
    if turned:
        result = matmul_nt(mid, down_ref[0]).astype(jnp.bfloat16)
        scaled_ref[0][0] = (scale_ref[0] * result.astype(jnp.float32)).astype(jnp.bfloat16)
    else:
        result = matmul(mid, down_ref[0])
    result_ref[0] = result


def expert(values, scales, gate, up, down, turned, rows):
    experts, count, width = values.shape
    features = gate.shape[2]
    by_rows, whole, out = expert_specs(experts, count, width, features, rows)
    low, wide = jnp.bfloat16, jnp.float32
    cols = (width, features, features, features) + (width,) * turned
    kinds = (low if turned else wide, low, wide, wide) + (low,) * turned
    return pl.pallas_call(
        functools.partial(expert_body, turned),
        grid=(experts, count // rows),
        in_specs=[by_rows(width), by_rows(1), whole(gate), whole(up), whole(down)],
        out_specs=[by_rows(c) for c in cols],
        out_shape=[out(c, kind) for c, kind in zip(cols, kinds)],
        compiler_params=pltpu.CompilerParams(vmem_limit_bytes=BIG_VMEM),
        cost_estimate=pl.CostEstimate(
            flops=6 * experts * count * width * features,
            bytes_accessed=6 * experts * (count + width) * features,
            transcendentals=experts * count * features,
        ),
        name="expert",
    )(values, scales, gate, up, down)


def expert_back_body(turned, grad_ref, result_ref, scale_ref, silu_ref, up_slope_ref, *rest):
    gate_ref, up_ref, down_ref, dot_ref, d_out_ref, d_gate_ref, d_up_ref, d_in_ref = rest
    grad = grad_ref[0].astype(jnp.float32)
    dot_ref[0] = jnp.sum(grad * result_ref[0].astype(jnp.float32), axis=1, keepdims=True)
    d_out = (scale_ref[0] * grad).astype(jnp.bfloat16)
    d_out_ref[0] = d_out
    d_mid = (matmul if turned else matmul_nt)(d_out, down_ref[0])
    d_gate = (d_mid * up_slope_ref[0]).astype(jnp.bfloat16)
    d_up = (d_mid * silu_ref[0]).astype(jnp.bfloat16)
    d_gate_ref[0] = d_gate
    d_up_ref[0] = d_up
    d_in_ref[0] = (matmul_nt(d_gate, gate_ref[0]) + matmul_nt(d_up, up_ref[0])).astype(
        d_in_ref.dtype
    )


def expert_back(grads, results, scales, silu, up_slope, gate, up, down, turned, rows):
    experts, count, width = grads.shape
    features = gate.shape[2]
    by_rows, whole, out = expert_specs(experts, count, width, features, rows)
    low = jnp.bfloat16
    return pl.pallas_call(
        functools.partial(expert_back_body, turned),
        grid=(experts, count // rows),
        in_specs=[by_rows(width), by_rows(width), by_rows(1), by_rows(features), by_rows(features)]
        + [whole(gate), whole(up), whole(down)],
        out_specs=[by_rows(c) for c in (1, width, features, features, width)],
        out_shape=[
            out(1, jnp.float32),
            out(width, low),
            out(features, low),
            out(features, low),
            out(width, results.dtype),
        ],
        compiler_params=pltpu.CompilerParams(vmem_limit_bytes=BIG_VMEM),
        cost_estimate=NO_COST,
        name="expert_back",
    )(grads, results, scales, silu, up_slope, gate, up, down)


def weight_grads_body(rows_ref, d_out_ref, d_gate_ref, d_up_ref, mid_ref, out_ref):
    rows = rows_ref[0].T
    out_ref[0, 0, 0] = matmul(rows, d_gate_ref[0]).astype(jnp.bfloat16)
    out_ref[0, 0, 1] = matmul(rows, d_up_ref[0]).astype(jnp.bfloat16)
    out_ref[0, 0, 2] = matmul(d_out_ref[0].T, mid_ref[0]).astype(jnp.bfloat16)


def weight_grads(rows, d_out, d_gate, d_up, mid, members):
    experts, count, width = rows.shape
    features = mid.shape[2]
    cut = width // members
    by_cols = pl.BlockSpec((1, count, cut), lambda e, i: (e, 0, i))
    whole = pl.BlockSpec((1, count, features), lambda e, i: (e, 0, 0))
    return pl.pallas_call(
        weight_grads_body,
        grid=(experts, members),
        in_specs=[by_cols, by_cols, whole, whole, whole],
        out_specs=pl.BlockSpec((1, 1, 3, cut, features), lambda e, i: (e, i, 0, 0, 0)),
        out_shape=jax.ShapeDtypeStruct((experts, members, 3, cut, features), jnp.bfloat16),
        compiler_params=pltpu.CompilerParams(vmem_limit_bytes=KERNEL_VMEM),
        cost_estimate=NO_COST,
        name="weight_grads",
    )(rows, d_out, d_gate, d_up, mid)


MESH = pl.DeviceIdType.MESH


class Line:
    def __init__(self, source, out, send_sems, recv_sems, pieces):
        self.source, self.out = source, out
        self.send_sems, self.recv_sems = send_sems, recv_sems
        self.members, self.rows, self.pieces = out.shape[0], out.shape[1] // pieces, pieces
        self.member = lax.axis_index("fsdp")

    def origin(self, step, way):
        return self.member - step if way == 0 else self.member + step

    def inside(self, place):
        return (place >= 0) & (place < self.members)

    def target(self, way):
        return self.member + 1 if way == 0 else self.member - 1

    def sends(self, step, way):
        return self.inside(self.origin(step - 1, way)) & self.inside(self.target(way))

    def copy(self, origin, step, way, piece, first):
        rows = pl.ds(piece * self.rows, self.rows)
        return pltpu.make_async_remote_copy(
            src_ref=self.source.at[rows] if first else self.out.at[origin, rows],
            dst_ref=self.out.at[origin, rows],
            send_sem=self.send_sems.at[way, step - 1, piece],
            recv_sem=self.recv_sems.at[way, step - 1, piece],
            device_id={"fsdp": self.target(way)},
            device_id_type=MESH,
        )

    def send(self, step, way, piece):
        copy = self.copy(self.origin(step - 1, way), step, way, piece, step == 1)
        pl.when(self.sends(step, way))(copy.start)

    def start(self):
        for piece in range(self.pieces):
            for way in range(2):
                self.send(1, way, piece)

    def hand_on(self, step):
        for piece in range(self.pieces):
            for way in range(2):
                origin = self.origin(step, way)
                came = self.copy(origin, step, way, piece, False)
                pl.when(self.inside(origin))(came.wait_recv)
                if step < self.members - 1:
                    self.send(step + 1, way, piece)

    def finish(self):
        for step in range(1, self.members):
            for piece in range(self.pieces):
                for way in range(2):
                    copy = self.copy(self.origin(step - 1, way), step, way, piece, step == 1)
                    pl.when(self.sends(step, way))(copy.wait_send)


def arrive_body(members, local_experts, pieces, *refs):
    tokens_ref, routes_ref, *refs = refs
    chunk_refs, refs = refs[:3], refs[3:]
    group_ref, routes_out, *refs = refs
    mixed_refs, crossed_refs, refs = refs[:3], refs[3:6], refs[6:]
    line_send, line_recv, routes_send, routes_recv, mix_send, mix_recv, refs = *refs[:6], refs[6:]
    cross_send, cross_recv, own_sems = refs
    columns = members * local_experts
    column, member = lax.axis_index("expert"), lax.axis_index("fsdp")
    plane, j = column // local_experts, column % local_experts
    rows = chunk_refs[0].shape[0] // members

    barrier = pltpu.get_barrier_semaphore()
    for other in range(1, columns):
        pl.semaphore_signal(
            barrier, inc=1, device_id={"expert": (column + other) % columns}, device_id_type=MESH
        )
    for other in range(1, members):
        pl.semaphore_signal(
            barrier, inc=1, device_id={"fsdp": (member + other) % members}, device_id_type=MESH
        )
    pl.semaphore_wait(barrier, columns + members - 2)

    line = Line(tokens_ref, group_ref, line_send, line_recv, pieces)
    line.start()
    own_copies = [
        pltpu.make_async_copy(tokens_ref, group_ref.at[member], own_sems.at[0]),
        pltpu.make_async_copy(routes_ref, routes_out.at[member], own_sems.at[1]),
    ]
    for copy in own_copies:
        copy.start()

    def mix(turn, kind):
        part = (plane + turn) % members
        target = j * members + part
        source = chunk_refs[kind].at[pl.ds(pl.multiple_of(part * rows, rows), rows)]
        remote = pltpu.make_async_remote_copy(
            src_ref=source,
            dst_ref=mixed_refs[kind].at[plane],
            send_sem=mix_send.at[turn, kind],
            recv_sem=mix_recv.at[turn, kind],
            device_id={"expert": target},
            device_id_type=MESH,
        )
        local = pltpu.make_async_copy(
            source, mixed_refs[kind].at[plane], mix_send.at[turn, kind]
        )
        return target == column, remote, local

    turns = [(turn, kind) for turn in range(members) for kind in range(3)]
    for turn, kind in turns:
        here, remote, local = mix(turn, kind)
        pl.when(here)(local.start)
        pl.when(jnp.logical_not(here))(remote.start)

    def route(other):
        return pltpu.make_async_remote_copy(
            src_ref=routes_ref,
            dst_ref=routes_out.at[member],
            send_sem=routes_send.at[other - 1],
            recv_sem=routes_recv.at[other - 1],
            device_id={"fsdp": (member + other) % members},
            device_id_type=MESH,
        )

    for other in range(1, members):
        route(other).start()
    for step in range(1, members - 1):
        line.hand_on(step)
    for turn, kind in turns:
        here, remote, local = mix(turn, kind)
        pl.when(here)(local.wait)
        pl.when(jnp.logical_not(here))(remote.wait)

    def cross(other, kind):
        target = (member + other) % members
        return pltpu.make_async_remote_copy(
            src_ref=mixed_refs[kind].at[target],
            dst_ref=crossed_refs[kind].at[member],
            send_sem=cross_send.at[other - 1, kind],
            recv_sem=cross_recv.at[other - 1, kind],
            device_id={"fsdp": target},
            device_id_type=MESH,
        )

    for kind in range(3):
        own_copies.append(
            pltpu.make_async_copy(
                mixed_refs[kind].at[member], crossed_refs[kind].at[member], own_sems.at[2 + kind]
            )
        )
        own_copies[-1].start()
        for other in range(1, members):
            cross(other, kind).start()
    line.hand_on(members - 1)
    line.finish()
    for other in range(1, members):
        route(other).wait()
        for kind in range(3):
            cross(other, kind).wait()
    for copy in own_copies:
        copy.wait()


def arrive(tokens, routes, chunks, members, local_experts):
    own, width = tokens.shape
    pieces = 3 if own % 48 == 0 else 1
    rows, cols = chunks[0].shape
    piece = jax.ShapeDtypeStruct((members, rows // members, cols), jnp.bfloat16)
    anywhere = pl.BlockSpec(memory_space=pl.ANY)
    sems = pltpu.SemaphoreType.DMA
    out_shape = [
        jax.ShapeDtypeStruct((members, own, width), jnp.bfloat16),
        jax.ShapeDtypeStruct((members,) + routes.shape, jnp.int32),
    ] + [piece] * 6
    group, group_routes, *rest = pl.pallas_call(
        functools.partial(arrive_body, members, local_experts, pieces),
        in_specs=[anywhere] * 5,
        out_specs=[anywhere] * len(out_shape),
        out_shape=out_shape,
        scratch_shapes=[sems((2, members - 1, pieces))] * 2
        + [sems((members - 1,))] * 2
        + [sems((members, 3))] * 2
        + [sems((members - 1, 3))] * 2
        + [sems((5,))],
        compiler_params=pltpu.CompilerParams(collective_id=0, has_side_effects=True),
        name="arrive",
    )(tokens, routes, *chunks)
    return group.reshape(members * own, width), group_routes, rest[3:]


def greet(members):
    member = lax.axis_index("fsdp")
    barrier = pltpu.get_barrier_semaphore()
    for other in range(1, members):
        pl.semaphore_signal(
            barrier, inc=1, device_id={"fsdp": (member + other) % members}, device_id_type=MESH
        )
    pl.semaphore_wait(barrier, members - 1)


def gather_body(pieces, block_ref, out_ref, send_sems, recv_sems, own_sem):
    members = out_ref.shape[0]
    member = lax.axis_index("fsdp")
    greet(members)
    line = Line(block_ref, out_ref, send_sems, recv_sems, pieces)
    line.start()
    own = pltpu.make_async_copy(block_ref, out_ref.at[member], own_sem)
    own.start()
    for step in range(1, members):
        line.hand_on(step)
    line.finish()
    own.wait()


def gather(block, members, pieces, collective_id):
    sems = pltpu.SemaphoreType.DMA
    return pl.pallas_call(
        functools.partial(gather_body, pieces),
        in_specs=[pl.BlockSpec(memory_space=pl.ANY)],
        out_specs=pl.BlockSpec(memory_space=pl.ANY),
        out_shape=jax.ShapeDtypeStruct((members,) + block.shape, block.dtype),
        scratch_shapes=[sems((2, members - 1, pieces))] * 2 + [sems],
        compiler_params=pltpu.CompilerParams(collective_id=collective_id, has_side_effects=True),
        name="gather",
    )(block)


def scatter_body(pieces, parts_ref, out_ref, came, send_sems, recv_sems):
    members, rows = parts_ref.shape[0], parts_ref.shape[1] // pieces
    member = lax.axis_index("fsdp")
    greet(members)

    def copy(way, block, piece, first):
        here = pl.ds(piece * rows, rows)
        source = parts_ref.at[block, here] if first else came.at[way, block, here]
        return pltpu.make_async_remote_copy(
            src_ref=source,
            dst_ref=came.at[way, block, here],
            send_sem=send_sems.at[way, block, piece],
            recv_sem=recv_sems.at[way, block, piece],
            device_id={"fsdp": member + 1 if way == 0 else member - 1},
            device_id_type=MESH,
        )

    def passes(way, block):
        starts = (member == 0) & (block > 0) if way == 0 else (member == members - 1)
        if way == 0:
            return starts, (member > 0) & (block > member), (member > 0) & (block == member)
        starts = starts & (block < members - 1)
        last = member < members - 1
        return starts, last & (block < member), last & (block == member)

    turns = [
        (way, members - 1 - turn if way == 0 else turn, piece)
        for turn in range(members)
        for piece in range(pieces)
        for way in range(2)
    ]
    for way, block, piece in turns:
        starts, hands_on, ends = passes(way, block)
        pl.when(starts)(copy(way, block, piece, True).start)

        @pl.when(hands_on)
        def _():
            copy(way, block, piece, False).wait_recv()
            here = pl.ds(piece * rows, rows)
            came[way, block, here] = (
                came[way, block, here].astype(jnp.float32)
                + parts_ref[block, here].astype(jnp.float32)
            ).astype(came.dtype)
            copy(way, block, piece, False).start()

    for way, block, piece in turns:
        pl.when(passes(way, block)[2])(copy(way, block, piece, False).wait_recv)

    for block in range(members):

        @pl.when(member == block)
        def _():
            total = parts_ref[block].astype(jnp.float32)
            if block > 0:
                total = total + came[0, block].astype(jnp.float32)
            if block < members - 1:
                total = total + came[1, block].astype(jnp.float32)
            out_ref[...] = total

    for way, block, piece in turns:
        starts, hands_on, _ = passes(way, block)
        pl.when(starts)(copy(way, block, piece, True).wait_send)
        pl.when(hands_on)(copy(way, block, piece, False).wait_send)


def scatter(parts, members, collective_id):
    count, width = parts.shape
    own = count // members
    pieces = 6 if own % 96 == 0 else 1
    sems = pltpu.SemaphoreType.DMA((2, members, pieces))
    return pl.pallas_call(
        functools.partial(scatter_body, pieces),
        in_specs=[pl.BlockSpec(memory_space=pltpu.VMEM)],
        out_specs=pl.BlockSpec(memory_space=pltpu.VMEM),
        out_shape=jax.ShapeDtypeStruct((own, width), jnp.float32),
        scratch_shapes=[pltpu.VMEM((2, members, own, width), parts.dtype), sems, sems],
        compiler_params=pltpu.CompilerParams(
            collective_id=collective_id, has_side_effects=True, vmem_limit_bytes=KERNEL_VMEM
        ),
        name="scatter",
    )(parts.reshape(members, own, width))


def unproject_body(*refs):
    grad_refs, weight_refs, refs = refs[:3], refs[3:6], refs[6:]
    tokens_ref, rate_ref, out_ref, sum_ref = refs
    total = 0.0
    for grad_ref, weight_ref in zip(grad_refs, weight_refs):
        total = total + matmul_nt(grad_ref[...], weight_ref[...])
    out_ref[...] = total.astype(jnp.bfloat16)
    part = total * (tokens_ref[...].astype(jnp.float32) * rate_ref[...])

    @pl.when(pl.program_id(0) == 0)
    def _():
        sum_ref[...] = jnp.zeros_like(sum_ref)

    sum_ref[...] += jnp.sum(part, axis=0, keepdims=True)


def unproject(grads, weights, tokens, rates, rows):
    count, width = tokens.shape
    features = grads[0].shape[1]

    def by_rows(cols):
        return pl.BlockSpec((rows, cols), lambda i: (i, 0))

    def whole(*shape):
        return pl.BlockSpec(shape, lambda i: (0, 0))

    return pl.pallas_call(
        unproject_body,
        grid=(count // rows,),
        in_specs=[by_rows(features)] * 3
        + [whole(width, features)] * 3
        + [by_rows(width), by_rows(1)],
        out_specs=[by_rows(width), whole(1, width)],
        out_shape=[
            jax.ShapeDtypeStruct((count, width), jnp.bfloat16),
            jax.ShapeDtypeStruct((1, width), jnp.float32),
        ],
        compiler_params=pltpu.CompilerParams(vmem_limit_bytes=KERNEL_VMEM),
        cost_estimate=NO_COST,
        name="unproject",
    )(*grads, *weights, tokens, rates)


def turn_body(piece_ref, out_ref):
    out_ref[...] = piece_ref[0].astype(jnp.float32).T


def turn(pieces):
    members, rows, features = pieces.shape
    if rows % 128:
        return pieces.reshape(members * rows, features).astype(jnp.float32).T
    return pl.pallas_call(
        turn_body,
        grid=(members,),
        in_specs=[pl.BlockSpec((1, rows, features), lambda i: (i, 0, 0))],
        out_specs=pl.BlockSpec((features, rows), lambda i: (0, i)),
        out_shape=jax.ShapeDtypeStruct((features, members * rows), jnp.float32),
        compiler_params=pltpu.CompilerParams(vmem_limit_bytes=KERNEL_VMEM),
        name="turn",
    )(pieces)


def shards(
    tokens,
    routes,
    seq_lengths,
    cotangent,
    norm1_gain,
    query_weight,
    query_bias,
    key_weight,
    key_bias,
    value_weight,
    value_bias,
    out_weight,
    norm2_gain,
    router_weight,
    shared_switch,
    shared_gate,
    shared_up,
    shared_down,
    expert_gate,
    expert_up,
    expert_down,
):
    own_count = tokens.shape[0]
    width = tokens.shape[1]
    members = lax.axis_size("fsdp")
    columns = lax.axis_size("expert")
    member = lax.axis_index("fsdp")
    own_start = member * own_count
    count = own_count * members
    experts_count = router_weight.shape[1]
    local_experts = experts_count // members
    capacity = 4 * own_count * TOP // (3 * experts_count)

    def own_rows(values):
        return lax.dynamic_slice_in_dim(values, own_start, own_count, 0)

    def take(pieces, place):
        return lax.dynamic_index_in_dim(pieces, place, 0, keepdims=False)

    def put(pieces, piece, place):
        return lax.dynamic_update_index_in_dim(pieces, piece, place, 0)

    def after(value, other):
        return lax.optimization_barrier((value, other))[0]

    def exchange(pieces):
        result = pieces
        for step in range(1, members):
            sent = take(pieces, (member + step) % members)
            came = lax.ppermute(sent, "fsdp", [(m, (m + step) % members) for m in range(members)])
            result = put(result, came, (member - step) % members)
        return result

    def line_gather(block, ties=(), last=()):
        from_low, from_high = [block], [block]
        for step in range(1, members):
            if step > 1 and ties:
                from_low[-1], from_high[-1] = after(
                    (from_low[-1], from_high[-1]), ties[min(step - 2, len(ties) - 1)]
                )
            upward = [(m, m + 1) for m in range(step - 1, members - 1)]
            downward = [(members - 1 - m, members - 2 - m) for m in range(step - 1, members - 1)]
            from_low.append(lax.ppermute(from_low[-1], "fsdp", upward))
            from_high.append(lax.ppermute(from_high[-1], "fsdp", downward))
        from_low[-1], from_high[-1] = after((from_low[-1], from_high[-1]), last)
        window = jnp.concatenate(from_low[:0:-1] + [block] + from_high[1:], axis=0)
        size = block.shape[0]
        return lax.dynamic_slice_in_dim(window, (members - 1 - member) * size, members * size, 0)

    def line_scatter(parts, ties=()):
        blocks = parts.reshape((members, -1) + parts.shape[1:])
        up_sum = down_sum = None
        for step in range(1, members):
            up_block = take(blocks, jnp.minimum(members - step + member, members - 1))
            down_block = take(blocks, jnp.maximum(member - (members - step), 0))
            if up_sum is not None:
                if ties:
                    up_sum, down_sum = after(
                        (up_sum, down_sum), ties[min(step - 2, len(ties) - 1)]
                    )
                up_block = (up_block.astype(jnp.float32) + up_sum.astype(jnp.float32)).astype(
                    parts.dtype
                )
                down_block = (down_block.astype(jnp.float32) + down_sum.astype(jnp.float32)).astype(
                    parts.dtype
                )
            up_sum = lax.ppermute(up_block, "fsdp", [(m, m + 1) for m in range(step)])
            down_sum = lax.ppermute(
                down_block, "fsdp", [(members - 1 - m, members - 2 - m) for m in range(step)]
            )
        if ties:
            up_sum, down_sum = after((up_sum, down_sum), ties[-1])
        own = take(blocks, member).astype(jnp.float32)
        return own + up_sum.astype(jnp.float32) + down_sum.astype(jnp.float32)

    column = lax.axis_index("expert")
    plane_of, j_of = column // local_experts, column % local_experts
    quarter_of = column % members

    def pairs_to_quarters(turn):
        return [
            (plane * local_experts + j, j * members + (plane + turn) % members)
            for plane in range(members)
            for j in range(local_experts)
        ]

    def weights_whole(piece):
        gathered = lax.all_gather(piece, "expert", axis=0, tiled=False)
        return gathered.reshape(local_experts, width, -1)

    def grads_out(crossed, tie):
        came = [
            lax.ppermute(
                take(crossed, (quarter_of - turn) % members),
                "expert",
                [(b, a) for a, b in pairs_to_quarters(turn)],
            )
            for turn in range(members)
        ]
        mixed = jnp.zeros_like(crossed)
        for turn, piece in enumerate(after(came, tie)):
            mixed = put(mixed, piece, (plane_of + turn) % members)
        return lax.optimization_barrier([mixed[:, kind] for kind in range(3)])

    group_tokens, group_routes, crossed = arrive(
        tokens,
        routes.T,
        (expert_gate[0], expert_up[0], expert_down[0].T),
        members,
        local_experts,
    )
    out_piece_rows = out_weight.shape[0] // columns
    out_piece = lax.dynamic_slice_in_dim(out_weight, column * out_piece_rows, out_piece_rows, 0)
    out_full = lax.all_gather(out_piece, ("fsdp", "expert"), axis=0, tiled=True)
    gate_mats, up_mats, down_mats = (weights_whole(piece) for piece in crossed)

    segment, positions = token_layout(seq_lengths[0], count)
    block = math.gcd(count, 256)
    starts = jnp.arange(count, dtype=jnp.int32) - positions
    lows = starts[::block] // block
    starts = starts[None]
    cosine, sine = rotary_tables(positions, HEAD_DIM)
    tokens_own_wide = tokens.astype(jnp.float32)
    gain_first = norm1_gain.astype(jnp.float32)
    normed_first, rate_first, queries, keys_all, values_all = project(
        group_tokens,
        gain_first[None],
        (query_weight, key_weight, value_weight),
        [bias.astype(jnp.float32)[None] for bias in (query_bias, key_bias, value_bias)],
        cosine,
        sine,
        block,
    )
    attended, log_mass = attend(lows, starts, queries, keys_all, values_all, block)
    attended_by_member = gather(attended, members, math.gcd(count // 16, 4), 1)
    tokens_wide = group_tokens.astype(jnp.float32)
    gain_second = norm2_gain.astype(jnp.float32)
    small_count = experts_count + 1
    small_weight = jnp.concatenate([router_weight, shared_switch[:, None]], axis=1)
    small_wide = jnp.pad(small_weight, ((0, 0), (0, 128 - small_count)))
    resid_mid, rate_second, normed_second, small_pre = settle(
        group_tokens, attended_by_member, out_full, gain_second[None], small_wide, block
    )
    resid_own = own_rows(resid_mid)
    rate_own = own_rows(rate_second)

    router_probs = jax.nn.softmax(small_pre[:, :experts_count], axis=-1)
    switch_all = jax.nn.sigmoid(small_pre[:, experts_count:small_count])
    own_ids = member * local_experts + jnp.arange(local_experts, dtype=jnp.int32)
    gates = lax.dynamic_slice_in_dim(router_probs, member * local_experts, local_experts, 1)
    hot = jnp.sum(
        (group_routes[:, :, None, :] == own_ids[None, None, :, None]).astype(jnp.float32), axis=1
    )
    order = jnp.arange(own_count, dtype=jnp.int32)
    before = (order[:, None] > order[None, :]).astype(jnp.bfloat16)
    ranks = jnp.einsum(
        "ut,bjt->bju", before, hot.astype(jnp.bfloat16), preferred_element_type=jnp.float32
    ).astype(jnp.int32)
    places_turned = jnp.where(hot > 0.0, ranks, -1)
    places = places_turned.transpose(0, 2, 1)
    slots = jnp.arange(capacity, dtype=jnp.int32)
    picks = places_turned[:, :, None, :] == slots[None, None, :, None]
    gates_turned = gates.reshape(members, own_count, local_experts).transpose(0, 2, 1)
    slot_gates = jnp.sum(jnp.where(picks, gates_turned[:, :, None, :], 0.0), axis=-1)
    slot_gates = slot_gates.transpose(1, 0, 2).reshape(local_experts, members * capacity, 1)
    places = places.reshape(count, local_experts)

    shared_weights = (shared_gate[None], shared_up[None], shared_down[None])
    shared_out, shared_mid, shared_silu, shared_slope = expert(
        normed_second[None], switch_all[None], *shared_weights, False, block
    )
    row_count = members * capacity
    row_block = math.gcd(row_count, 256)
    rows = dispatch(places_turned, after(normed_second, shared_mid), capacity, members)
    result, expert_mid, expert_silu, expert_slope, scaled = expert(
        rows, slot_gates, gate_mats, up_mats, down_mats, True, row_block
    )
    by_block = (local_experts, members, capacity, width)
    block_low = collect(places, scaled.reshape(by_block), shared_out[0], members, switch_all)

    group_cot = line_gather(
        after(cotangent, attended_by_member), (normed_second, shared_mid), block_low
    )

    grad_wide = group_cot.astype(jnp.float32)
    down_grad = matmul_tn(shared_mid[0], (switch_all * grad_wide).astype(jnp.bfloat16)).astype(
        jnp.bfloat16
    )
    down_sum = lax.psum(down_grad, "expert")
    slot_dot, d_rows, d_expert_gate, d_expert_up, d_in = expert_back(
        dispatch(places_turned, after(group_cot, down_grad), capacity, members),
        result,
        slot_gates,
        expert_silu,
        expert_slope,
        gate_mats,
        up_mats,
        down_mats,
        True,
        row_block,
    )
    expert_grads = weight_grads(rows, d_rows, d_expert_gate, d_expert_up, expert_mid, members)
    expert_pieces = lax.psum_scatter(
        expert_grads.reshape((columns, 3) + expert_grads.shape[3:]),
        "expert",
        scatter_dimension=0,
        tiled=True,
    ).reshape(3, members, -1, expert_grads.shape[-1])
    switch_dot, _, d_shared_gate, d_shared_up, dh_shared = expert_back(
        after(group_cot, (expert_grads, down_sum))[None],
        shared_out,
        switch_all[None],
        shared_silu,
        shared_slope,
        *shared_weights,
        False,
        block,
    )
    switch_logit = switch_dot[0] * switch_all * (1.0 - switch_all)
    shared_grads = tuple(
        grad.astype(jnp.bfloat16)
        for grad in (
            matmul_tn(normed_second, d_shared_gate[0]),
            matmul_tn(normed_second, d_shared_up[0]),
        )
    )
    shared_sums = lax.psum(shared_grads, "expert")
    slot_dots = slot_dot.reshape(local_experts, members, capacity).transpose(1, 0, 2)
    d_gates = jnp.sum(jnp.where(picks, slot_dots[:, :, :, None], 0.0), axis=2)
    d_gates = d_gates.transpose(0, 2, 1).reshape(count, local_experts)
    d_choice = lax.dynamic_update_slice_in_dim(
        jnp.zeros_like(router_probs), d_gates, member * local_experts, 1
    )
    d_logits = router_probs * (d_choice - jnp.sum(gates * d_gates, axis=-1, keepdims=True))
    d_small = jnp.concatenate([d_logits, switch_logit], axis=1)
    d_small_high = d_small.astype(jnp.bfloat16)
    d_small_low = (d_small - d_small_high.astype(jnp.float32)).astype(jnp.bfloat16)
    d_small_both = jnp.pad(
        jnp.concatenate([d_small_high, d_small_low], axis=1),
        ((0, 0), (0, 128 - 2 * small_count)),
    )
    small_both = jnp.pad(
        jnp.concatenate([small_weight.T, small_weight.T], axis=0),
        ((0, 128 - 2 * small_count), (0, 0)),
    )
    dh_low = collect(
        places, d_in.reshape(by_block), dh_shared[0], members, d_small_both, small_both
    )
    small_part = matmul_tn(normed_second, d_small_both)
    small_part = small_part[:, :small_count] + small_part[:, small_count : 2 * small_count]

    block_own = line_scatter(block_low, (d_in, dh_shared, shared_grads))
    block_out = (resid_own + block_own).astype(jnp.bfloat16)
    dh_second_own = scatter(after(dh_low, shared_grads), members, 2)

    grad_own = cotangent.astype(jnp.float32)
    d_resid_own = norm_back(grad_own, dh_second_own, resid_own, rate_own, gain_second)
    d_attn_own = d_resid_own.astype(jnp.bfloat16)
    norm2_part = jnp.sum(dh_second_own * resid_own * rate_own, axis=0)
    d_attn_out = gather(d_attn_own, members, 3 if own_count % 48 == 0 else 1, 3)
    d_attn_out = d_attn_out.reshape(count, width)
    d_context = matmul_nt(d_attn_out, out_weight).astype(jnp.bfloat16)
    d_query_pre, d_key_pre, d_value_pre = attend_back(
        lows,
        starts,
        queries,
        keys_all,
        values_all,
        d_context,
        log_mass,
        cosine,
        sine,
        block,
    )

    d_query_pre, d_key_pre, d_value_pre = after(
        (d_query_pre, d_key_pre, d_value_pre), shared_sums
    )
    dh_first_low, norm1_part = unproject(
        (d_query_pre, d_key_pre, d_value_pre),
        (query_weight, key_weight, value_weight),
        group_tokens,
        rate_first,
        block,
    )
    norm1_part = norm1_part[0]
    attn_grads = tuple(
        matmul_tn(normed_first, d_pre).astype(jnp.bfloat16)
        for d_pre in (d_query_pre, d_key_pre, d_value_pre)
    ) + (matmul_tn(attended, d_attn_out).astype(jnp.bfloat16),)
    crossed_grads = exchange(after(expert_pieces, d_attn_out).transpose(1, 0, 2, 3))
    dh_first_own = scatter(
        after(dh_first_low, (attn_grads, crossed_grads)), members, 4
    )
    grad_tokens = norm_back(
        d_resid_own, dh_first_own, tokens_own_wide, own_rows(rate_first), gain_first
    )

    def pair_sum(values, axis, size):
        if size & (size - 1):
            return lax.psum(values, axis)
        for bit in range(size.bit_length() - 1):
            pairs = [(place, place ^ (1 << bit)) for place in range(size)]
            values = values + lax.ppermute(values, axis, pairs)
        return values

    biases = [
        jnp.sum(d_pre.astype(jnp.float32), axis=0)
        for d_pre in (d_query_pre, d_key_pre, d_value_pre)
    ]
    stats = pair_sum(
        jnp.concatenate([norm1_part, norm2_part, small_part.T.reshape(-1)]), "fsdp", members
    )
    stats = pair_sum(jnp.concatenate([stats] + biases), "expert", columns)
    small_sum = stats[2 * width : (2 + small_count) * width].reshape(-1, width)
    bias_sums = stats[(2 + small_count) * width :].reshape(3, -1)

    attn_sums = lax.psum(attn_grads, "expert")
    expert_sums = grads_out(crossed_grads, dh_first_own)

    return (
        block_out,
        grad_tokens,
        stats[:width],
        attn_sums[0].astype(jnp.float32),
        bias_sums[0],
        attn_sums[1].astype(jnp.float32),
        bias_sums[1],
        attn_sums[2].astype(jnp.float32),
        bias_sums[2],
        attn_sums[3].astype(jnp.float32),
        stats[width : 2 * width],
        small_sum[:experts_count].T,
        small_sum[experts_count],
        shared_sums[0].astype(jnp.float32),
        shared_sums[1].astype(jnp.float32),
        down_sum.astype(jnp.float32),
        expert_sums[0].reshape(1, width // members, -1).astype(jnp.float32),
        expert_sums[1].reshape(1, width // members, -1).astype(jnp.float32),
        turn(expert_sums[2])[None],
    )


def solution(mesh):
    placed = (
        P(("expert", "fsdp"), None),
        P(("expert", "fsdp"), None),
        P("expert", None),
        P(("expert", "fsdp"), None),
        P(),
        P(None, "fsdp"),
        P("fsdp"),
        P(None, "fsdp"),
        P("fsdp"),
        P(None, "fsdp"),
        P("fsdp"),
        P("fsdp", None),
        P(),
        P(),
        P(),
        P(None, "fsdp"),
        P(None, "fsdp"),
        P("fsdp", None),
        P("expert", "fsdp", None),
        P("expert", "fsdp", None),
        P("expert", None, "fsdp"),
    )
    return jax.shard_map(
        shards,
        mesh=mesh,
        in_specs=placed,
        out_specs=(
            P(("expert", "fsdp"), None),
            P(("expert", "fsdp"), None),
            P(),
            P(None, "fsdp"),
            P("fsdp"),
            P(None, "fsdp"),
            P("fsdp"),
            P(None, "fsdp"),
            P("fsdp"),
            P("fsdp", None),
            P(),
            P(),
            P(),
            P(None, "fsdp"),
            P(None, "fsdp"),
            P("fsdp", None),
            P("expert", "fsdp", None),
            P("expert", "fsdp", None),
            P("expert", None, "fsdp"),
        ),
        check_vma=False,
    )
```

time: 2230 us -> 1540 us (0.69)
  Pallas kernels: 0 us -> 1030 us
  waiting for transfers between devices: 756 us -> 158 us
  matrix products: 647 us -> 74.7 us
  blocking collectives: 363 us -> 0 us
  other arithmetic: 197 us -> 81 us
  local copies, waits for them, and re-layouts: 204 us -> 113 us
  starting transfers between devices: 26.8 us -> 60.6 us
    pallas_call x0 -> x20, Pallas kernels: none -> 1030 us  [the longest x2 230 us: scatter(): pl.pallas_call(functools.partial(scatter_body, pieces), in_specs=[pl.Bloc...]
    dot_general x44 -> x1, matrix products: 347 us -> 0.2 us  [shards(): jnp.einsum('ut,bjt->bju', before, hot.astype(jnp.bfloat16), preferred_ele...]
    all_to_all x7 -> x0, blocking collectives: 290 us -> none  [the longest x3 187 us: over_members(): lax.all_to_all(pieces, 'fsdp', split_axis=0, concat_axis=0, tiled=True)]
    psum x2 -> x3, waiting for transfers between devices: 317 us -> 32 us  [the longest x1 32 us: shards(): attn_sums = lax.psum(attn_grads, 'expert')]
    dot_general x14 -> x1, matrix products: 180 us -> 6.69 us  [matmul_nt(): lax.dot_general(left_matrix, right_matrix, (((1,), (1,)), ((), ())), pref...]
    all_to_all x6 -> x0, waiting for transfers between devices: 132 us -> none  [the longest x4 107 us: over_members(): lax.all_to_all(pieces, 'fsdp', split_axis=0, concat_axis=0, tiled=True)]
    reduce_scatter x6 -> x1, waiting for transfers between devices: 179 us -> 50.6 us  [shards(): lax.psum_scatter(expert_grads.reshape((columns, 3) + expert_grads.shape[3...]
    all_gather x7 -> x3, waiting for transfers between devices: 125 us -> 0.06 us  [weights_whole(): gathered = lax.all_gather(piece, 'expert', axis=0, tiled=False)]
  transfers between devices with their start and end apart: 22 -> 32, of which waited for: 10 -> 8; matrix products, arithmetic and copies ran while one was open for 35% -> 11% of each run, Pallas kernels for 0% -> 67%
where the time goes in v2:
time: 1540 us; the launch traced here: 1530 us
  Pallas kernels  1030 us (67%)
  waiting for transfers between devices  158 us (10%)
  local copies, waits for them, and re-layouts  113 us (7%)
  other arithmetic  81 us (5%)
  matrix products  74.7 us (5%)
  starting transfers between devices  60.6 us (4%)
  between operations  16.3 us (1%)
    pallas_call x2, Pallas kernels, scatter(): pl.pallas_call(functools.partial(scatter_body, pieces), in_specs=[pl.Bloc...  230 us
    pallas_call x1, Pallas kernels, arrive(): pl.pallas_call(functools.partial(arrive_body, members, local_experts, pie...  218 us
    pallas_call x2, Pallas kernels, gather(): pl.pallas_call(functools.partial(gather_body, pieces), in_specs=[pl.Block...  201 us
    pallas_call x2, Pallas kernels, expert_back(): pl.pallas_call(functools.partial(expert_back_body, turned), grid=(experts...  103 us
    pallas_call x2, Pallas kernels, expert(): pl.pallas_call(functools.partial(expert_body, turned), grid=(experts, cou...  94.8 us
    dot_general x8, matrix products, matmul_tn(): lax.dot_general(left_matrix, right_matrix, (((0,), (0,)), ((), ())), pref...  67.8 us
    unnamed x175, local copies, waits for them, and re-layouts  63.7 us
    reduce_scatter x1, waiting for transfers between devices, shards(): lax.psum_scatter(expert_grads.reshape((columns, 3) + expert_grads.shape[3...  50.6 us
  transfers between devices with their start and end apart: 32, of which 8 were waited for; matrix products, arithmetic and copies ran while one was open for 11% of the time, Pallas kernels for 67%

profile of v2, /device:TPU:0, one launch (start us, length us, event | category | flops | bytes accessed | tf_op | source)
XLA Modules:
  0.0 1533.0 jit_solution(11402334004300698665)
XLA Ops:
  12.1 218.1 %arrive.1 = (bf16[4,384,2048]{2,1,0:T(8,128)(2,1)}, s32[4,4,384]{2,1,0:T(4,128)}, bf16[4,128,1408]{2,1,0:T(8,128)(2,1)}, bf16[4,128,1408]{2,1,0:T(8,128)(2,1)}, ...) custom-call(bf16[384,2048]{1,0:T(8,128)(2,1)} %refs_0_.1, ...), custom_call_target="tpu_custom_call" | custom-call | tf_op jit(solution)/shard_map/arrive/pallas_call | solution.py:720
  235.6 14.4 project.1
  250.1 23.0 %attend.1 = (bf16[1536,512]{1,0:T(8,128)(2,1)S(1)}, f32[4,1,1536]{2,1,0:T(1,128)S(1)}) custom-call(s32[6]{0:T(128)S(1)} %and_select_fusion.lows_ref, s32[1,1536]{1,0:T(1,128)S(1)} %subtract_subtract_fusion.starts_ref, bf16[1536,512]{1,0:T(8,128)(2,1)S(1)} %get-tuple-element.88.query_ref, bf16[1536,512]{1,0:T(8,128)(2,1)S(1)} %get-tuple-element.89.key_ref, ...), custom_call_target="tpu_custom_call" | custom-call | flops 2415919104 | bytes 6291456 | tf_op jit(solution)/shard_map/attend/pallas_call | solution.py:178
  274.3 102.7 %gather.2.attended_ref = bf16[4,1536,512]{2,1,0:T(8,128)(2,1)} custom-call(bf16[1536,512]{1,0:T(8,128)(2,1)} %copy-done.40), custom_call_target="tpu_custom_call" | custom-call | tf_op jit(solution)/shard_map/gather/pallas_call | solution.py:762
  383.2 22.3 %settle.1 = (f32[1536,2048]{1,0:T(8,128)}, f32[1536,1]{1,0:T(8,128)S(1)}, bf16[1536,2048]{1,0:T(8,128)(2,1)S(1)}, f32[1536,128]{1,0:T(8,128)S(1)}) custom-call(bf16[1536,2048]{1,0:T(8,128)(2,1)} %bitcast.186, bf16[4,1536,512]{2,1,0:T(8,128)(2,1)} %gather.2.attended_ref, bf16[2048,2048]{1,0:T(8,128)(2,1)} %all-gather.8.cloned.1.call-done.weight_ref, ...), custom_call_target="tpu_custom_call" | custom-call | flops 12884901888 | bytes 37748736 | tf_op jit(solution)/shard_map/settle/pallas_call | solution.py:311
  419.7 38.8 %expert.2 = (f32[1,1536,2048]{2,1,0:T(8,128)}, bf16[1,1536,1408]{2,1,0:T(8,128)(2,1)}, f32[1,1536,1408]{2,1,0:T(8,128)}, f32[1,1536,1408]{2,1,0:T(8,128)}) custom-call(bf16[1,1536,2048]{2,1,0:T(8,128)(2,1)} %bitcast.151, f32[1,1536,1]{2,1,0:T(8,128)} %bitcast.155, bf16[1,2048,1408]{2,1,0:T(8,128)(2,1)} %bitcast.190, bf16[1,2048,1408]{2,1,0:T(8,128)(2,1)} %bitcast.192, ...), custom_call_target="tpu_custom_call" | custom-call | flops 26575110144 | bytes 30277632 | tf_op jit(solution)/shard_map/expert/pallas_call | solution.py:465
  461.2 6.5 dispatch.2
  471.3 56.0 %expert.3 = (bf16[2,1024,2048]{2,1,0:T(8,128)(2,1)}, bf16[2,1024,1408]{2,1,0:T(8,128)(2,1)}, f32[2,1024,1408]{2,1,0:T(8,128)}, f32[2,1024,1408]{2,1,0:T(8,128)}, bf16[2,1024,2048]{2,1,0:T(8,128)(2,1)}) custom-call(bf16[2,1024,2048]{2,1,0:T(8,128)(2,1)} %bitcast.171, f32[2,1024,1]{2,1,0:T(8,128)} %copy.93.scale_ref, bf16[2,2048,1408]{2,1,0:T(8,128)(2,1)} %bitcast.176, ...), custom_call_target="tpu_custom_call" | custom-call | flops 35433480192 | bytes 51904512 | tf_op jit(solution)/shard_map/expert/pallas_call | solution.py:465
  527.4 9.0 collect.2
  560.4 11.4 convolution_convert_fusion.2
  574.4 4.0 dynamic-slice_bitcast_fusion
  578.5 8.8 collective-permute-start
  592.3 6.4 dispatch.3
  598.8 60.3 %expert_back.2 = (f32[2,1024,1]{2,1,0:T(8,128)}, bf16[2,1024,2048]{2,1,0:T(8,128)(2,1)}, bf16[2,1024,1408]{2,1,0:T(8,128)(2,1)}, bf16[2,1024,1408]{2,1,0:T(8,128)(2,1)}, bf16[2,1024,2048]{2,1,0:T(8,128)(2,1)}) custom-call(bf16[2,1024,2048]{2,1,0:T(8,128)(2,1)} %bitcast.170, bf16[2,1024,2048]{2,1,0:T(8,128)(2,1)} %get-tuple-element.111.result_ref, ...), custom_call_target="tpu_custom_call" | custom-call | tf_op jit(solution)/shard_map/expert_back/pallas_call | solution.py:502
  663.3 4.3 dynamic_update_slice.25
  677.7 45.3 %weight_grads.1 = bf16[2,4,3,512,1408]{4,3,2,1,0:T(8,128)(2,1)} custom-call(bf16[2,1024,2048]{2,1,0:T(8,128)(2,1)} %bitcast.172, bf16[2,1024,2048]{2,1,0:T(8,128)(2,1)} %get-tuple-element.117.d_out_ref, bf16[2,1024,1408]{2,1,0:T(8,128)(2,1)S(1)} %copy-done.22, bf16[2,1024,1408]{2,1,0:T(8,128)(2,1)S(1)} %copy-done.23, ...), custom_call_target="tpu_custom_call" | custom-call | tf_op jit(solution)/shard_map/weight_grads/pallas_call | solution.py:534
  723.0 6.1 fusion.8
  733.8 42.6 %expert_back.3 = (f32[1,1536,1]{2,1,0:T(8,128)}, bf16[1,1536,2048]{2,1,0:T(8,128)(2,1)}, bf16[1,1536,1408]{2,1,0:T(8,128)(2,1)}, bf16[1,1536,1408]{2,1,0:T(8,128)(2,1)}, f32[1,1536,2048]{2,1,0:T(8,128)}) custom-call(bf16[1,1536,2048]{2,1,0:T(8,128)(2,1)} %bitcast.144, f32[1,1536,2048]{2,1,0:T(8,128)} %get-tuple-element.102.result_ref, ...), custom_call_target="tpu_custom_call" | custom-call | tf_op jit(solution)/shard_map/expert_back/pallas_call | solution.py:502
  782.3 9.9 collect.3
  794.9 14.4 convolution_convert_fusion
  809.4 4.9 fusion.7
  814.3 4.6 collective-permute-start.10
  820.2 12.0 convolution_convert_fusion.1
  832.3 15.0 collective-permute-done.10
  847.3 5.3 collective-permute-done.11
  857.9 105.7 %scatter.2 = f32[384,2048]{1,0:T(8,128)S(1)} custom-call(bf16[4,384,2048]{2,1,0:T(8,128)(2,1)S(1)} %bitcast.154), custom_call_target="tpu_custom_call" | custom-call | tf_op jit(solution)/shard_map/scatter/pallas_call | solution.py:843
  963.6 5.0 fusion.34
  968.7 9.7 convert_element_type.256
  981.3 6.0 fusion.36
  987.4 98.6 %gather.3 = bf16[4,384,2048]{2,1,0:T(8,128)(2,1)} custom-call(bf16[384,2048]{1,0:T(8,128)(2,1)} %get-tuple-element.167.block_ref), custom_call_target="tpu_custom_call" | custom-call | tf_op jit(solution)/shard_map/gather/pallas_call | solution.py:762
  1086.1 6.7 convolution_convert_fusion.7.grad_ref
  1092.9 29.3 %attend_back.1 = (bf16[1536,512]{1,0:T(8,128)(2,1)S(1)}, bf16[1536,512]{1,0:T(8,128)(2,1)S(1)}, bf16[1536,512]{1,0:T(8,128)(2,1)S(1)}) custom-call(s32[6]{0:T(128)S(1)} %copy-done.50, s32[1,1536]{1,0:T(1,128)S(1)} %copy-done.48, bf16[1536,512]{1,0:T(8,128)(2,1)S(1)} %copy-done.35, bf16[1536,512]{1,0:T(8,128)(2,1)S(1)} %copy-done.37, ...), custom_call_target="tpu_custom_call" | custom-call | tf_op jit(solution)/shard_map/attend_back/pallas_call | solution.py:258
  1125.6 4.8 convolution_convert_fusion.3
  1139.6 13.9 unproject.1
  1158.5 5.5 collective-permute-done.16
  1164.1 8.0 convolution_convert_fusion.4
  1175.2 4.6 convolution_convert_fusion.5
  1179.8 4.8 collective-permute-start.19
  1184.6 50.6 %reduce-scatter.2.cloned.1.call-done = bf16[1,3,512,1408]{3,2,1,0:T(8,128)(2,1)} async-done(((bf16[8,3,512,1408]{3,2,1,0:T(8,128)(2,1)}), bf16[1,3,512,1408]{3,2,1,0:T(8,128)(2,1)}) %reduce-scatter.2.cloned.1.call-update) | async-done | bytes 4325392 | tf_op jit(solution)/shard_map/reduce_scatter | solution.py:1141
  1242.3 7.6 convolution_convert_fusion.6
  1249.9 7.8 convert_element_type.254
  1257.8 7.8 convert_element_type.255
  1270.5 42.5 %collective-permute-done.13 = bf16[3,128,1408]{2,1,0:T(8,128)(2,1)S(1)} collective-permute-done((bf16[3,128,1408]{2,1,0:T(8,128)(2,1)}, bf16[3,128,1408]{2,1,0:T(8,128)(2,1)S(1)}, u32[]{:S(2)}, u32[]{:S(2)}) %collective-permute-start.13) | collective-permute-done | bytes 1081376 | tf_op jit(solution)/shard_map/ppermute | solution.py:968
  1321.1 9.7 collective-permute-start.20
  1333.2 4.1 collective-permute-start.23
  1340.1 124.8 %scatter.3 = f32[384,2048]{1,0:T(8,128)S(1)} custom-call(bf16[4,384,2048]{2,1,0:T(8,128)(2,1)S(1)} %bitcast.159), custom_call_target="tpu_custom_call" | custom-call | tf_op jit(solution)/shard_map/scatter/pallas_call | solution.py:843
  1481.6 32.0 %all-reduce.11.cloned.1.call-done = (bf16[2048,512]{1,0:T(8,128)(2,1)}, bf16[2048,512]{1,0:T(8,128)(2,1)}, bf16[2048,512]{1,0:T(8,128)(2,1)}, bf16[512,2048]{1,0:T(8,128)(2,1)}) async-done(((bf16[2048,512]{1,0:T(8,128)(2,1)}, bf16[2048,512]{1,0:T(8,128)(2,1)}, bf16[2048,512]{1,0:T(8,128)(2,1)}, bf16[512,2048]{1,0:T(8,128)(2,1)}), (bf16[2048,512]{1,0:T(8,128)(2,1)}, bf16[2048,512]{1,0:T(8,128)(2,1)}, ...) | async-done | bytes 8388624 | tf_op jit(solution)/shard_map/psum | solution.py:1256
  1513.6 4.3 convert_element_type.250
  (333 shorter events, 176.8 us)
Async XLA Ops:
  7.2 376.0 %all-gather.8.cloned.1.call-start = ((), (), s32[]{:S(2)}) async-start(), calls=%async_computation.1 | async-start | bytes 8650752 | tf_op jit(solution)/shard_map/all_gather | solution.py:1052
  9.5 461.7 %all-gather.10.cloned.1.call-start = ((), (), s32[]{:S(2)}) async-start(), calls=%async_computation.4 | async-start | bytes 12976128 | tf_op jit(solution)/shard_map/all_gather | solution.py:1026
  230.3 241.0 %all-gather.12.cloned.1.call-start = ((), (), s32[]{:S(2)}) async-start(), calls=%async_computation.5 | async-start | bytes 12976128 | tf_op jit(solution)/shard_map/all_gather | solution.py:1026
  231.0 240.3 %all-gather.14.cloned.1.call-start = ((), (), s32[]{:S(2)}) async-start(), calls=%async_computation.6 | async-start | bytes 12976128 | tf_op jit(solution)/shard_map/all_gather | solution.py:1026
  231.6 502.2 %all-reduce.9.cloned.1.call-start = ((), (), s32[]{:S(2)}) async-start(), calls=%async_computation.2 | async-start | bytes 11534336 | tf_op jit(solution)/shard_map/psum | solution.py:1127
  274.3 106.8 %copy-start.65 = (bf16[2048]{0:T(1024)(128)(2,1)S(1)}, bf16[2048]{0:T(1024)(128)(2,1)}, u32[]{:S(2)}) copy-start(bf16[2048]{0:T(1024)(128)(2,1)} %param.33) | copy-start | bytes 12292
  274.3 106.9 %copy-start.62 = (bf16[2048,8]{0,1:T(8,128)(2,1)S(1)}, bf16[2048,8]{0,1:T(8,128)(2,1)}, u32[]{:S(2)}) copy-start(bf16[2048,8]{0,1:T(8,128)(2,1)} %param.34) | copy-start | bytes 98308
  274.3 106.9 %copy-start.66 = (bf16[2048]{0:T(1024)(128)(2,1)S(1)}, bf16[2048]{0:T(1024)(128)(2,1)}, u32[]{:S(2)}) copy-start(bf16[2048]{0:T(1024)(128)(2,1)} %param.35) | copy-start | bytes 12292
  274.3 107.2 %copy-start.63 = (s32[4,4,384]{2,1,0:T(4,128)S(1)}, s32[4,4,384]{2,1,0:T(4,128)}, u32[]{:S(2)}) copy-start(s32[4,4,384]{2,1,0:T(4,128)} %get-tuple-element.93) | copy-start | bytes 73732
  376.9 38.5 %collective-permute-start.2 = (bf16[384,2048]{1,0:T(8,128)(2,1)}, bf16[384,2048]{1,0:T(8,128)(2,1)}, u32[]{:S(2)}, u32[]{:S(2)}) collective-permute-start(bf16[384,2048]{1,0:T(8,128)(2,1)} %param.24), channel_id=1, source_target_pairs={{0,1},{1,2},{2,3},{4,5},{5,6},{6,7},{8,9},{9,10},{10,11},{12,13},{... | collective-permute-start | bytes 4718600 | tf_op jit(solution)/shard_map/ppermute | solution.py:981
  379.6 35.8 %collective-permute-start.3 = (bf16[384,2048]{1,0:T(8,128)(2,1)}, bf16[384,2048]{1,0:T(8,128)(2,1)}, u32[]{:S(2)}, u32[]{:S(2)}) collective-permute-start(bf16[384,2048]{1,0:T(8,128)(2,1)} %param.24), channel_id=1, source_target_pairs={{3,2},{2,1},{1,0},{7,6},{6,5},{5,4},{11,10},{10,9},{9,8},{15,14},{... | collective-permute-start | bytes 4718600 | tf_op jit(solution)/shard_map/ppermute | solution.py:982
  415.4 52.3 %collective-permute-start.4 = (bf16[384,2048]{1,0:T(8,128)(2,1)}, bf16[384,2048]{1,0:T(8,128)(2,1)}, u32[]{:S(2)}, u32[]{:S(2)}) collective-permute-start(bf16[384,2048]{1,0:T(8,128)(2,1)} %collective-permute-done.2), channel_id=1, source_target_pairs={{1,2},{2,3},{5,6},{6,7},{9,10},{10,11},{13,14},{14,15},{17,18},{18... | collective-permute-start | bytes 4718600 | tf_op jit(solution)/shard_map/ppermute | solution.py:981
  417.2 50.5 %collective-permute-start.5 = (bf16[384,2048]{1,0:T(8,128)(2,1)}, bf16[384,2048]{1,0:T(8,128)(2,1)}, u32[]{:S(2)}, u32[]{:S(2)}) collective-permute-start(bf16[384,2048]{1,0:T(8,128)(2,1)} %collective-permute-done.3), channel_id=1, source_target_pairs={{2,1},{1,0},{6,5},{5,4},{10,9},{9,8},{14,13},{13,12},{18,17},{17,1... | collective-permute-start | bytes 4718600 | tf_op jit(solution)/shard_map/ppermute | solution.py:982
  467.7 71.3 %collective-permute-start.6 = (bf16[384,2048]{1,0:T(8,128)(2,1)}, bf16[384,2048]{1,0:T(8,128)(2,1)}, u32[]{:S(2)}, u32[]{:S(2)}) collective-permute-start(bf16[384,2048]{1,0:T(8,128)(2,1)} %collective-permute-done.4), channel_id=1, source_target_pairs={{2,3},{6,7},{10,11},{14,15},{18,19},{22,23},{26,27},{30,31}} | collective-permute-start | bytes 4718600 | tf_op jit(solution)/shard_map/ppermute | solution.py:981
  469.5 69.5 %collective-permute-start.7 = (bf16[384,2048]{1,0:T(8,128)(2,1)}, bf16[384,2048]{1,0:T(8,128)(2,1)}, u32[]{:S(2)}, u32[]{:S(2)}) collective-permute-start(bf16[384,2048]{1,0:T(8,128)(2,1)} %collective-permute-done.5), channel_id=1, source_target_pairs={{1,0},{5,4},{9,8},{13,12},{17,16},{21,20},{25,24},{29,28}} | collective-permute-start | bytes 4718600 | tf_op jit(solution)/shard_map/ppermute | solution.py:982
  471.3 56.1 %copy-start.10 = (f32[1536,1]{1,0:T(8,128)S(1)}, f32[1536,1]{1,0:T(8,128)}, u32[]{:S(2)}) copy-start(f32[1536,1]{1,0:T(8,128)} %get-tuple-element.170.rest_0_) | copy-start | bytes 18436
  471.3 56.0 %copy-start.12 = (s32[4,384,2]{2,1,0:T(8,128)S(1)}, s32[4,384,2]{2,1,0:T(8,128)}, u32[]{:S(2)}) copy-start(s32[4,384,2]{2,1,0:T(8,128)} %copy.89) | copy-start | bytes 36868
  574.4 556.1 %all-reduce.13.cloned.1.call-start = ((), (), s32[]{:S(2)}) async-start(), calls=%async_computation.8 | async-start | bytes 23068672 | tf_op jit(solution)/shard_map/psum | solution.py:1165
  578.5 144.5 %collective-permute-start = (bf16[384,2048]{1,0:T(8,128)(2,1)}, bf16[384,2048]{1,0:T(8,128)(2,1)}, u32[]{:S(2)}, u32[]{:S(2)}) collective-permute-start(bf16[384,2048]{1,0:T(8,128)(2,1)} %get-tuple-element.177), channel_id=1, source_target_pairs={{0,1},{4,5},{8,9},{12,13},{16,17},{20,21},{24,25},{28,29}} | collective-permute-start | bytes 4718600 | tf_op jit(solution)/shard_map/ppermute | solution.py:1005
  587.2 135.8 %collective-permute-start.1 = (bf16[384,2048]{1,0:T(8,128)(2,1)}, bf16[384,2048]{1,0:T(8,128)(2,1)}, u32[]{:S(2)}, u32[]{:S(2)}) collective-permute-start(bf16[384,2048]{1,0:T(8,128)(2,1)} %get-tuple-element.176), channel_id=1, source_target_pairs={{3,2},{7,6},{11,10},{15,14},{19,18},{23,22},{27,26},{31,30}} | collective-permute-start | bytes 4718600 | tf_op jit(solution)/shard_map/ppermute | solution.py:1006
  729.1 80.3 %collective-permute-start.8 = (bf16[384,2048]{1,0:T(8,128)(2,1)}, bf16[384,2048]{1,0:T(8,128)(2,1)}, u32[]{:S(2)}, u32[]{:S(2)}) collective-permute-start(bf16[384,2048]{1,0:T(8,128)(2,1)} %get-tuple-element.175), channel_id=1, source_target_pairs={{0,1},{1,2},{4,5},{5,6},{8,9},{9,10},{12,13},{13,14},{16,17},{17,1... | collective-permute-start | bytes 4718600 | tf_op jit(solution)/shard_map/ppermute | solution.py:1005
  731.8 77.6 %collective-permute-start.9 = (bf16[384,2048]{1,0:T(8,128)(2,1)}, bf16[384,2048]{1,0:T(8,128)(2,1)}, u32[]{:S(2)}, u32[]{:S(2)}) collective-permute-start(bf16[384,2048]{1,0:T(8,128)(2,1)} %get-tuple-element.174), channel_id=1, source_target_pairs={{3,2},{2,1},{7,6},{6,5},{11,10},{10,9},{15,14},{14,13},{19,18},{18... | collective-permute-start | bytes 4718600 | tf_op jit(solution)/shard_map/ppermute | solution.py:1006
  733.8 42.6 %copy-start.11 = (f32[1536,1]{1,0:T(8,128)S(1)}, f32[1536,1]{1,0:T(8,128)}, u32[]{:S(2)}) copy-start(f32[1536,1]{1,0:T(8,128)} %get-tuple-element.170.rest_0_) | copy-start | bytes 18436
  782.3 27.1 %slice-start = ((s8[6291456]{0:T(1024)(128)(4,1)}), s8[2097152]{0:T(1024)(128)(4,1)S(1)}, s32[]{:S(2)}) async-start(s8[6291456]{0:T(1024)(128)(4,1)} %bitcast.148), calls=%async_computation.9 | async-start | bytes 4194304
  794.9 25.3 %slice-start.2 = ((s8[6291456]{0:T(1024)(128)(4,1)}), s8[4194304]{0:T(1024)(128)(4,1)S(1)}, s32[]{:S(2)}) async-start(s8[6291456]{0:T(1024)(128)(4,1)} %bitcast.152), calls=%async_computation.11 | async-start | bytes 8388608
  794.9 25.3 %slice-start.4 = ((s8[4325376]{0:T(1024)(128)(4,1)}), s8[4194304]{0:T(1024)(128)(4,1)S(1)}, s32[]{:S(2)}) async-start(s8[4325376]{0:T(1024)(128)(4,1)} %bitcast.213), calls=%async_computation.13 | async-start | bytes 8388608
  794.9 25.3 %slice-start.3 = ((s8[6291456]{0:T(1024)(128)(4,1)}), s8[2097152]{0:T(1024)(128)(4,1)S(1)}, s32[]{:S(2)}) async-start(s8[6291456]{0:T(1024)(128)(4,1)} %bitcast.152), calls=%async_computation.12 | async-start | bytes 4194304
  814.3 33.0 %collective-permute-start.10 = (bf16[384,2048]{1,0:T(8,128)(2,1)}, bf16[384,2048]{1,0:T(8,128)(2,1)}, u32[]{:S(2)}, u32[]{:S(2)}) collective-permute-start(bf16[384,2048]{1,0:T(8,128)(2,1)} %get-tuple-element.173), channel_id=1, source_target_pairs={{0,1},{1,2},{2,3},{4,5},{5,6},{6,7},{8,9},{9,10},{10,11},{12,13},{... | collective-permute-start | bytes 4718600 | tf_op jit(solution)/shard_map/ppermute | solution.py:1005
  818.9 33.7 %collective-permute-start.11 = (bf16[384,2048]{1,0:T(8,128)(2,1)}, bf16[384,2048]{1,0:T(8,128)(2,1)}, u32[]{:S(2)}, u32[]{:S(2)}) collective-permute-start(bf16[384,2048]{1,0:T(8,128)(2,1)} %get-tuple-element.172), channel_id=1, source_target_pairs={{3,2},{2,1},{1,0},{7,6},{6,5},{5,4},{11,10},{10,9},{9,8},{15,14},{... | collective-permute-start | bytes 4718600 | tf_op jit(solution)/shard_map/ppermute | solution.py:1006
  852.6 382.6 %reduce-scatter.2.cloned.1.call-start = ((), (), s32[]{:S(2)}) async-start(), calls=%async_computation.3 | async-start | bytes 38928384 | tf_op jit(solution)/shard_map/reduce_scatter | solution.py:1141
  853.4 660.2 %all-reduce.11.cloned.1.call-start = ((), (), s32[]{:S(2)}) async-start(), calls=%async_computation.7 | async-start | bytes 16777216 | tf_op jit(solution)/shard_map/psum | solution.py:1256
  857.9 105.7 %copy-start.58 = (bf16[1536,18]{1,0:T(8,128)(2,1)S(1)}, bf16[1536,18]{1,0:T(8,128)(2,1)}, u32[]{:S(2)}) copy-start(bf16[1536,18]{1,0:T(8,128)(2,1)} %copy.101) | copy-start | bytes 165892
  1092.9 32.8 %copy-start.41 = (bf16[1536,512]{1,0:T(8,128)(2,1)S(1)}, bf16[1536,512]{1,0:T(8,128)(2,1)}, u32[]{:S(2)}) copy-start(bf16[1536,512]{1,0:T(8,128)(2,1)} %copy-done.40) | copy-start | bytes 4718596
  1092.9 32.8 %copy-start.55 = (bf16[4,384,2048]{2,1,0:T(8,128)(2,1)S(1)}, bf16[4,384,2048]{2,1,0:T(8,128)(2,1)}, u32[]{:S(2)}) copy-start(bf16[4,384,2048]{2,1,0:T(8,128)(2,1)} %gather.3) | copy-start | bytes 18874372
  1153.5 4.6 collective-permute-start.15
  1158.1 5.9 collective-permute-start.16
  1164.1 8.1 collective-permute-start.17
  1172.2 7.7 collective-permute-start.18
  1179.8 85.7 %collective-permute-start.19 = (f32[24064]{0:T(1024)S(1)}, f32[24064]{0:T(1024)S(1)}, u32[]{:S(2)}, u32[]{:S(2)}) collective-permute-start(f32[24064]{0:T(1024)S(1)} %add.269), channel_id=1, source_target_pairs={{0,16},{4,20},{8,24},{12,28},{16,0},{20,4},{24,8},{28,12},{1,17},{... | collective-permute-start | bytes 288776 | tf_op jit(solution)/shard_map/ppermute | solution.py:1242
  1239.0 29.2 %collective-permute-start.12 = (bf16[3,128,1408]{2,1,0:T(8,128)(2,1)}, bf16[3,128,1408]{2,1,0:T(8,128)(2,1)}, u32[]{:S(2)}, u32[]{:S(2)}) collective-permute-start(bf16[3,128,1408]{2,1,0:T(8,128)(2,1)} %get-tuple-element.187), channel_id=1, source_target_pairs={{0,1},{1,2},{2,3},{3,0},{4,5},{5,6},{6,7},{7,4},{8,9},{9,10},{10,1... | collective-permute-start | bytes 3244040 | tf_op jit(solution)/shard_map/ppermute | solution.py:968
  1239.0 74.0 %collective-permute-start.13 = (bf16[3,128,1408]{2,1,0:T(8,128)(2,1)}, bf16[3,128,1408]{2,1,0:T(8,128)(2,1)S(1)}, u32[]{:S(2)}, u32[]{:S(2)}) collective-permute-start(bf16[3,128,1408]{2,1,0:T(8,128)(2,1)} %get-tuple-element.186), channel_id=1, source_target_pairs={{0,2},{1,3},{2,0},{3,1},{4,6},{5,7},{6,4},{7,5},{8,10},{9,11},{10,... | collective-permute-start | bytes 3244040 | tf_op jit(solution)/shard_map/ppermute | solution.py:968
  1266.2 48.6 %collective-permute-start.14 = (bf16[3,128,1408]{2,1,0:T(8,128)(2,1)}, bf16[3,128,1408]{2,1,0:T(8,128)(2,1)}, u32[]{:S(2)}, u32[]{:S(2)}) collective-permute-start(bf16[3,128,1408]{2,1,0:T(8,128)(2,1)} %get-tuple-element.185), channel_id=1, source_target_pairs={{0,3},{1,0},{2,1},{3,2},{4,7},{5,4},{6,5},{7,6},{8,11},{9,8},{10,9... | collective-permute-start | bytes 3244040 | tf_op jit(solution)/shard_map/ppermute | solution.py:968
  1321.1 148.2 %collective-permute-start.20 = (bf16[3,128,1408]{2,1,0:T(8,128)(2,1)}, bf16[3,128,1408]{2,1,0:T(8,128)(2,1)}, u32[]{:S(2)}, u32[]{:S(2)}) collective-permute-start(bf16[3,128,1408]{2,1,0:T(8,128)(2,1)} %get-tuple-element.184), channel_id=1, source_target_pairs={{0,0},{16,4},{4,8},{20,12},{8,16},{24,20},{12,24},{28,28},{1,1},{1... | collective-permute-start | bytes 3244040 | tf_op jit(solution)/shard_map/ppermute | solution.py:1031
  1330.8 138.5 %collective-permute-start.21 = (bf16[3,128,1408]{2,1,0:T(8,128)(2,1)}, bf16[3,128,1408]{2,1,0:T(8,128)(2,1)}, u32[]{:S(2)}, u32[]{:S(2)}) collective-permute-start(bf16[3,128,1408]{2,1,0:T(8,128)(2,1)} %get-tuple-element.183), channel_id=1, source_target_pairs={{4,0},{20,4},{8,8},{24,12},{12,16},{28,20},{0,24},{16,28},{5,1},{2... | collective-permute-start | bytes 3244040 | tf_op jit(solution)/shard_map/ppermute | solution.py:1031
  1332.8 136.6 %collective-permute-start.22 = (bf16[3,128,1408]{2,1,0:T(8,128)(2,1)}, bf16[3,128,1408]{2,1,0:T(8,128)(2,1)}, u32[]{:S(2)}, u32[]{:S(2)}) collective-permute-start(bf16[3,128,1408]{2,1,0:T(8,128)(2,1)} %get-tuple-element.182), channel_id=1, source_target_pairs={{8,0},{24,4},{12,8},{28,12},{0,16},{16,20},{4,24},{20,28},{9,1},{2... | collective-permute-start | bytes 3244040 | tf_op jit(solution)/shard_map/ppermute | solution.py:1031
  1333.2 136.1 %collective-permute-start.23 = (bf16[3,128,1408]{2,1,0:T(8,128)(2,1)S(1)}, bf16[3,128,1408]{2,1,0:T(8,128)(2,1)}, u32[]{:S(2)}, u32[]{:S(2)}) collective-permute-start(bf16[3,128,1408]{2,1,0:T(8,128)(2,1)S(1)} %get-tuple-element.181), channel_id=1, source_target_pairs={{12,0},{28,4},{0,8},{16,12},{4,16},{20,20},{8,24},{24,28},{13,1},{... | collective-permute-start | bytes 3244040 | tf_op jit(solution)/shard_map/ppermute | solution.py:1031
  1340.1 124.8 %copy-start.45 = (f32[2048]{0:T(1024)S(1)}, f32[2048]{0:T(1024)}, u32[]{:S(2)}) copy-start(f32[2048]{0:T(1024)} %copy-done.44) | copy-start | bytes 24580
  1340.1 124.8 %copy-start.51 = (bf16[384,2048]{1,0:T(8,128)(2,1)S(1)}, bf16[384,2048]{1,0:T(8,128)(2,1)}, u32[]{:S(2)}) copy-start(bf16[384,2048]{1,0:T(8,128)(2,1)} %refs_0_.1) | copy-start | bytes 4718596
  (67 other events, 442.7 us)
Sparse Core Ops, SparseCore 0:
  11.5 101.8 all-gather.7
  230.4 66.4 all-gather.9
  298.8 67.6 all-gather.11
  368.3 67.6 all-gather.13
  574.5 106.5 all-reduce.8
  852.8 166.1 all-reduce.12
  1022.6 212.5 reduce-scatter.1
  1337.4 176.1 all-reduce.10

commit v3 on v2

--- a/solution.py
+++ b/solution.py
@@ -18,6 +18,7 @@
 KERNEL_VMEM = 40 * 1024 * 1024
 BIG_VMEM = 58 * 1024 * 1024
 NO_COST = pl.CostEstimate(flops=0, bytes_accessed=0, transcendentals=0)
+LONG_COST = pl.CostEstimate(flops=10**11, bytes_accessed=0, transcendentals=0)
 
 
 def rms_rate(values):
@@ -127,11 +128,7 @@
         ]
         + [jax.ShapeDtypeStruct((count, features), jnp.bfloat16)] * 3,
         compiler_params=pltpu.CompilerParams(vmem_limit_bytes=KERNEL_VMEM),
-        cost_estimate=pl.CostEstimate(
-            flops=6 * count * width * features,
-            bytes_accessed=4 * count * width + 6 * (count + width) * features,
-            transcendentals=0,
-        ),
+        cost_estimate=NO_COST,
         name="project",
     )(tokens, gain, *weights, *biases, cosine, sine)
 
@@ -193,11 +190,7 @@
             jax.ShapeDtypeStruct((heads, 1, count), jnp.float32),
         ],
         compiler_params=pltpu.CompilerParams(vmem_limit_bytes=KERNEL_VMEM),
-        cost_estimate=pl.CostEstimate(
-            flops=2 * count * count * features,
-            bytes_accessed=8 * count * features,
-            transcendentals=count * count * heads // 2,
-        ),
+        cost_estimate=NO_COST,
         name="attend",
     )(lows, starts, queries, keys, values)
 
@@ -469,11 +462,7 @@
         out_specs=[by_rows(c) for c in cols],
         out_shape=[out(c, kind) for c, kind in zip(cols, kinds)],
         compiler_params=pltpu.CompilerParams(vmem_limit_bytes=BIG_VMEM),
-        cost_estimate=pl.CostEstimate(
-            flops=6 * experts * count * width * features,
-            bytes_accessed=6 * experts * (count + width) * features,
-            transcendentals=experts * count * features,
-        ),
+        cost_estimate=NO_COST if turned else None,
         name="expert",
     )(values, scales, gate, up, down)
 
@@ -543,6 +532,29 @@
     )(rows, d_out, d_gate, d_up, mid)
 
 
+def pair_grads_body(rows_ref, first_ref, second_ref, first_out, second_out):
+    rows = rows_ref[...].T
+    first_out[...] = matmul(rows, first_ref[...]).astype(jnp.bfloat16)
+    second_out[...] = matmul(rows, second_ref[...]).astype(jnp.bfloat16)
+
+
+def pair_grads(rows, first, second, cut):
+    count, width = rows.shape
+    features = first.shape[1]
+    whole = pl.BlockSpec((count, features), lambda i: (0, 0))
+    out = jax.ShapeDtypeStruct((width, features), jnp.bfloat16)
+    return pl.pallas_call(
+        pair_grads_body,
+        grid=(width // cut,),
+        in_specs=[pl.BlockSpec((count, cut), lambda i: (0, i)), whole, whole],
+        out_specs=[pl.BlockSpec((cut, features), lambda i: (i, 0))] * 2,
+        out_shape=[out, out],
+        compiler_params=pltpu.CompilerParams(vmem_limit_bytes=KERNEL_VMEM),
+        cost_estimate=NO_COST,
+        name="pair_grads",
+    )(rows, first, second)
+
+
 MESH = pl.DeviceIdType.MESH
 
 
@@ -587,12 +599,15 @@
 
     def hand_on(self, step):
         for piece in range(self.pieces):
-            for way in range(2):
-                origin = self.origin(step, way)
-                came = self.copy(origin, step, way, piece, False)
-                pl.when(self.inside(origin))(came.wait_recv)
-                if step < self.members - 1:
-                    self.send(step + 1, way, piece)
+            self.hand_on_piece(step, piece)
+
+    def hand_on_piece(self, step, piece):
+        for way in range(2):
+            origin = self.origin(step, way)
+            came = self.copy(origin, step, way, piece, False)
+            pl.when(self.inside(origin))(came.wait_recv)
+            if step < self.members - 1:
+                self.send(step + 1, way, piece)
 
     def finish(self):
         for step in range(1, self.members):
@@ -770,92 +785,282 @@
     )(block)
 
 
-def scatter_body(pieces, parts_ref, out_ref, came, send_sems, recv_sems):
-    members, rows = parts_ref.shape[0], parts_ref.shape[1] // pieces
-    member = lax.axis_index("fsdp")
-    greet(members)
-
-    def copy(way, block, piece, first):
-        here = pl.ds(piece * rows, rows)
-        source = parts_ref.at[block, here] if first else came.at[way, block, here]
+class Sums:
+    def __init__(self, parts, came, send_sems, recv_sems, pieces):
+        self.parts, self.came = parts, came
+        self.send_sems, self.recv_sems = send_sems, recv_sems
+        self.members, self.rows = parts.shape[0], parts.shape[1] // pieces
+        self.member = lax.axis_index("fsdp")
+
+    def clear(self):
+        for way, end in ((0, 0), (1, self.members - 1)):
+
+            @pl.when(self.member == end)
+            def _():
+                self.came[way, end] = jnp.zeros_like(self.came[way, end])
+
+    def copy(self, way, block, piece, first):
+        here = pl.ds(piece * self.rows, self.rows)
+        source = self.parts.at[block, here] if first else self.came.at[way, block, here]
         return pltpu.make_async_remote_copy(
             src_ref=source,
-            dst_ref=came.at[way, block, here],
-            send_sem=send_sems.at[way, block, piece],
-            recv_sem=recv_sems.at[way, block, piece],
-            device_id={"fsdp": member + 1 if way == 0 else member - 1},
+            dst_ref=self.came.at[way, block, here],
+            send_sem=self.send_sems.at[way, block, piece],
+            recv_sem=self.recv_sems.at[way, block, piece],
+            device_id={"fsdp": self.member + 1 if way == 0 else self.member - 1},
             device_id_type=MESH,
         )
 
-    def passes(way, block):
-        starts = (member == 0) & (block > 0) if way == 0 else (member == members - 1)
+    def passes(self, way, block):
+        member, last = self.member, self.members - 1
         if way == 0:
+            starts = (member == 0) & (block > 0)
             return starts, (member > 0) & (block > member), (member > 0) & (block == member)
-        starts = starts & (block < members - 1)
-        last = member < members - 1
-        return starts, last & (block < member), last & (block == member)
-
-    turns = [
-        (way, members - 1 - turn if way == 0 else turn, piece)
-        for turn in range(members)
-        for piece in range(pieces)
-        for way in range(2)
-    ]
-    for way, block, piece in turns:
-        starts, hands_on, ends = passes(way, block)
-        pl.when(starts)(copy(way, block, piece, True).start)
-
-        @pl.when(hands_on)
-        def _():
-            copy(way, block, piece, False).wait_recv()
-            here = pl.ds(piece * rows, rows)
-            came[way, block, here] = (
-                came[way, block, here].astype(jnp.float32)
-                + parts_ref[block, here].astype(jnp.float32)
-            ).astype(came.dtype)
-            copy(way, block, piece, False).start()
-
-    for way, block, piece in turns:
-        pl.when(passes(way, block)[2])(copy(way, block, piece, False).wait_recv)
-
-    for block in range(members):
-
-        @pl.when(member == block)
-        def _():
-            total = parts_ref[block].astype(jnp.float32)
-            if block > 0:
-                total = total + came[0, block].astype(jnp.float32)
-            if block < members - 1:
-                total = total + came[1, block].astype(jnp.float32)
-            out_ref[...] = total
-
-    for way, block, piece in turns:
-        starts, hands_on, _ = passes(way, block)
-        pl.when(starts)(copy(way, block, piece, True).wait_send)
-        pl.when(hands_on)(copy(way, block, piece, False).wait_send)
-
-
-def scatter(parts, members, collective_id):
+        starts = (member == last) & (block < last)
+        return starts, (member < last) & (block < member), (member < last) & (block == member)
+
+    def turns(self):
+        for turn in range(self.members):
+            for way in range(2):
+                yield way, self.members - 1 - turn if way == 0 else turn
+
+    def hand_on(self, piece):
+        here = pl.ds(piece * self.rows, self.rows)
+        for way, block in self.turns():
+            starts, hands_on, _ = self.passes(way, block)
+            pl.when(starts)(self.copy(way, block, piece, True).start)
+
+            @pl.when(hands_on)
+            def _():
+                self.copy(way, block, piece, False).wait_recv()
+                self.came[way, block, here] = (
+                    self.came[way, block, here].astype(jnp.float32)
+                    + self.parts[block, here].astype(jnp.float32)
+                ).astype(self.came.dtype)
+                self.copy(way, block, piece, False).start()
+
+    def total(self, piece):
+        for way, block in self.turns():
+            pl.when(self.passes(way, block)[2])(self.copy(way, block, piece, False).wait_recv)
+        here = pl.ds(piece * self.rows, self.rows)
+        return (
+            self.parts[self.member, here].astype(jnp.float32)
+            + self.came[0, self.member, here].astype(jnp.float32)
+            + self.came[1, self.member, here].astype(jnp.float32)
+        )
+
+    def finish(self, piece):
+        for way, block in self.turns():
+            starts, hands_on, _ = self.passes(way, block)
+            pl.when(starts)(self.copy(way, block, piece, True).wait_send)
+            pl.when(hands_on)(self.copy(way, block, piece, False).wait_send)
+
+
+def pair_stages(members, columns):
+    for size, axis in ((members, "fsdp"), (columns, "expert")):
+        for bit in range(size.bit_length() - 1):
+            yield axis, 1 << bit
+
+
+def scatter_body(pieces, columns, line_rows, parts_ref, stats_ref, crossed_ref, *refs):
+    out_ref, stats_out, mixed_ref, came, levels, stats_came, send_sems, recv_sems, *refs = refs
+    stats_send, stats_recv, mix_send, mix_recv = refs
+    members = parts_ref.shape[0]
+    stages = list(pair_stages(members, columns))
+    member, column = lax.axis_index("fsdp"), lax.axis_index("expert")
+    barrier = pltpu.get_barrier_semaphore()
+    for other in range(1, members):
+        pl.semaphore_signal(
+            barrier, inc=1, device_id={"fsdp": (member + other) % members}, device_id_type=MESH
+        )
+    for other in range(1, columns):
+        pl.semaphore_signal(
+            barrier, inc=1, device_id={"expert": (column + other) % columns}, device_id_type=MESH
+        )
+    pl.semaphore_wait(barrier, members + columns - 2)
+
+    def exchange(stage):
+        axis, distance = stages[stage]
+        place = member if axis == "fsdp" else column
+        partner = place + distance - 2 * distance * ((place // distance) % 2)
+        return pltpu.make_async_remote_copy(
+            src_ref=levels.at[stage],
+            dst_ref=stats_came.at[stage],
+            send_sem=stats_send.at[stage],
+            recv_sem=stats_recv.at[stage],
+            device_id={axis: partner},
+            device_id_type=MESH,
+        )
+
+    def settle_stage(stage):
+        exchange(stage).wait_recv()
+        value = levels[stage] + stats_came[stage]
+        if stages[stage][0] == "fsdp":
+            rows = lax.broadcasted_iota(jnp.int32, value.shape, 0)
+            value = jnp.where(rows < line_rows, value, levels[stage])
+        if stage + 1 < len(stages):
+            levels[stage + 1] = value
+            exchange(stage + 1).start()
+        else:
+            stats_out[...] = value
+
+    def mix(turn):
+        quarter, j = column % members, column // members
+        plane = (quarter - turn + members) % members
+        target = plane * (columns // members) + j
+        remote = pltpu.make_async_remote_copy(
+            src_ref=crossed_ref.at[plane],
+            dst_ref=mixed_ref.at[quarter],
+            send_sem=mix_send.at[turn],
+            recv_sem=mix_recv.at[turn],
+            device_id={"expert": target},
+            device_id_type=MESH,
+        )
+        local = pltpu.make_async_copy(
+            crossed_ref.at[plane], mixed_ref.at[quarter], mix_send.at[turn]
+        )
+        return target == column, remote, local
+
+    for turn in range(members):
+        here, remote, local = mix(turn)
+        pl.when(here)(local.start)
+        pl.when(jnp.logical_not(here))(remote.start)
+    sums = Sums(parts_ref, came, send_sems, recv_sems, pieces)
+    sums.clear()
+    levels[0] = stats_ref[...]
+    exchange(0).start()
+    for piece in range(pieces):
+        sums.hand_on(piece)
+        if piece < len(stages):
+            settle_stage(piece)
+    for stage in range(pieces, len(stages)):
+        settle_stage(stage)
+    for piece in range(pieces):
+        out_ref[piece * sums.rows : (piece + 1) * sums.rows, :] = sums.total(piece)
+    for piece in range(pieces):
+        sums.finish(piece)
+    for stage in range(len(stages)):
+        exchange(stage).wait_send()
+    for turn in range(members):
+        here, remote, local = mix(turn)
+        pl.when(here)(local.wait)
+        pl.when(jnp.logical_not(here))(remote.wait)
+
+
+def scatter(parts, stats, crossed, line_rows, members, columns, collective_id, cost):
     count, width = parts.shape
     own = count // members
     pieces = 6 if own % 96 == 0 else 1
-    sems = pltpu.SemaphoreType.DMA((2, members, pieces))
+    stages = len(list(pair_stages(members, columns)))
+    sems = pltpu.SemaphoreType.DMA
+    in_vmem = pl.BlockSpec(memory_space=pltpu.VMEM)
+    anywhere = pl.BlockSpec(memory_space=pl.ANY)
     return pl.pallas_call(
-        functools.partial(scatter_body, pieces),
-        in_specs=[pl.BlockSpec(memory_space=pltpu.VMEM)],
-        out_specs=pl.BlockSpec(memory_space=pltpu.VMEM),
-        out_shape=jax.ShapeDtypeStruct((own, width), jnp.float32),
-        scratch_shapes=[pltpu.VMEM((2, members, own, width), parts.dtype), sems, sems],
+        functools.partial(scatter_body, pieces, columns, line_rows),
+        in_specs=[in_vmem, in_vmem, anywhere],
+        out_specs=[in_vmem, in_vmem, anywhere],
+        out_shape=[
+            jax.ShapeDtypeStruct((own, width), jnp.float32),
+            jax.ShapeDtypeStruct(stats.shape, jnp.float32),
+            jax.ShapeDtypeStruct(crossed.shape, crossed.dtype),
+        ],
+        scratch_shapes=[
+            pltpu.VMEM((2, members, own, width), parts.dtype),
+            pltpu.VMEM((stages,) + stats.shape, jnp.float32),
+            pltpu.VMEM((stages,) + stats.shape, jnp.float32),
+        ]
+        + [sems((2, members, pieces))] * 2
+        + [sems((stages,))] * 2
+        + [sems((members,))] * 2,
         compiler_params=pltpu.CompilerParams(
             collective_id=collective_id, has_side_effects=True, vmem_limit_bytes=KERNEL_VMEM
         ),
+        cost_estimate=cost,
         name="scatter",
-    )(parts.reshape(members, own, width))
+    )(parts.reshape(members, own, width), stats, crossed)
+
+
+def turnaround_body(pieces, *refs):
+    parts_ref, resid_all, rate_all, grad_ref, gain_ref, d_resid_ref, sum_ref, out_ref, *refs = refs
+    came, resid_ref, rate_ref, low, send_sems, recv_sems, line_send, line_recv, own_sems = refs
+    members, own_rows = parts_ref.shape[:2]
+    greet(members)
+    here = pl.ds(pl.multiple_of(lax.axis_index("fsdp") * own_rows, own_rows), own_rows)
+    reads = [
+        pltpu.make_async_copy(resid_all.at[here], resid_ref, own_sems.at[1]),
+        pltpu.make_async_copy(rate_all.at[here], rate_ref, own_sems.at[2]),
+    ]
+    for read in reads:
+        read.start()
+    sums = Sums(parts_ref, came, send_sems, recv_sems, pieces)
+    sums.clear()
+    line = Line(low, out_ref, line_send, line_recv, pieces)
+    sum_ref[...] = jnp.zeros_like(sum_ref)
+    for read in reads:
+        read.wait()
+    for phase in range(pieces + members - 1 + 1):
+        if phase < pieces:
+            sums.hand_on(phase)
+        ready = phase - 1
+        if 0 <= ready < pieces:
+            here = slice(ready * sums.rows, (ready + 1) * sums.rows)
+            dh = sums.total(ready)
+            resid, rate = resid_ref[here, :], rate_ref[here, :]
+            sum_ref[...] += jnp.sum(dh * resid * rate, axis=0, keepdims=True)
+            d_resid = norm_back(
+                grad_ref[here, :].astype(jnp.float32), dh, resid, rate, gain_ref[...]
+            )
+            d_resid_ref[here, :] = d_resid
+            low[here, :] = d_resid.astype(low.dtype)
+            for way in range(2):
+                line.send(1, way, ready)
+        for step in range(1, members):
+            if 0 <= ready - step < pieces:
+                line.hand_on_piece(step, ready - step)
+    own = pltpu.make_async_copy(low, out_ref.at[line.member], own_sems.at[0])
+    own.start()
+    line.finish()
+    for piece in range(pieces):
+        sums.finish(piece)
+    own.wait()
+
+
+def turnaround(parts, resid, rate, grad, gain, members, collective_id):
+    count, width = parts.shape
+    own = count // members
+    pieces = 12 if own % 192 == 0 else 1
+    sems = pltpu.SemaphoreType.DMA
+    in_vmem = pl.BlockSpec(memory_space=pltpu.VMEM)
+    anywhere = pl.BlockSpec(memory_space=pl.ANY)
+    d_resid, gain_part, d_attn = pl.pallas_call(
+        functools.partial(turnaround_body, pieces),
+        in_specs=[in_vmem, anywhere, anywhere, in_vmem, in_vmem],
+        out_specs=[in_vmem, in_vmem, anywhere],
+        out_shape=[
+            jax.ShapeDtypeStruct((own, width), jnp.float32),
+            jax.ShapeDtypeStruct((1, width), jnp.float32),
+            jax.ShapeDtypeStruct((members, own, width), jnp.bfloat16),
+        ],
+        scratch_shapes=[
+            pltpu.VMEM((2, members, own, width), parts.dtype),
+            pltpu.VMEM((own, width), jnp.float32),
+            pltpu.VMEM((own, 1), jnp.float32),
+            pltpu.VMEM((own, width), jnp.bfloat16),
+        ]
+        + [sems((2, members, pieces))] * 2
+        + [sems((2, members - 1, pieces))] * 2
+        + [sems((3,))],
+        compiler_params=pltpu.CompilerParams(
+            collective_id=collective_id, has_side_effects=True, vmem_limit_bytes=KERNEL_VMEM
+        ),
+        name="turnaround",
+    )(parts.reshape(members, own, width), resid, rate, grad, gain)
+    return d_resid, gain_part[0], d_attn.reshape(count, width)
 
 
 def unproject_body(*refs):
     grad_refs, weight_refs, refs = refs[:3], refs[3:6], refs[6:]
-    tokens_ref, rate_ref, out_ref, sum_ref = refs
+    tokens_ref, rate_ref, out_ref, sum_ref, *bias_refs = refs
     total = 0.0
     for grad_ref, weight_ref in zip(grad_refs, weight_refs):
         total = total + matmul_nt(grad_ref[...], weight_ref[...])
@@ -864,9 +1069,12 @@
 
     @pl.when(pl.program_id(0) == 0)
     def _():
-        sum_ref[...] = jnp.zeros_like(sum_ref)
+        for ref in (sum_ref, *bias_refs):
+            ref[...] = jnp.zeros_like(ref)
 
     sum_ref[...] += jnp.sum(part, axis=0, keepdims=True)
+    for grad_ref, bias_ref in zip(grad_refs, bias_refs):
+        bias_ref[...] += jnp.sum(grad_ref[...].astype(jnp.float32), axis=0, keepdims=True)
 
 
 def unproject(grads, weights, tokens, rates, rows):
@@ -885,15 +1093,42 @@
         in_specs=[by_rows(features)] * 3
         + [whole(width, features)] * 3
         + [by_rows(width), by_rows(1)],
-        out_specs=[by_rows(width), whole(1, width)],
+        out_specs=[by_rows(width), whole(1, width)] + [whole(1, features)] * 3,
         out_shape=[
             jax.ShapeDtypeStruct((count, width), jnp.bfloat16),
             jax.ShapeDtypeStruct((1, width), jnp.float32),
-        ],
+        ]
+        + [jax.ShapeDtypeStruct((1, features), jnp.float32)] * 3,
         compiler_params=pltpu.CompilerParams(vmem_limit_bytes=KERNEL_VMEM),
         cost_estimate=NO_COST,
         name="unproject",
     )(*grads, *weights, tokens, rates)
+
+
+def attend_grads_body(rows_ref, d_query, d_key, d_value, attended_ref, d_out_ref, *outs):
+    rows = rows_ref[...].T
+    for d_ref, out in zip((d_query, d_key, d_value), outs):
+        out[...] = matmul(rows, d_ref[...]).astype(jnp.bfloat16)
+    outs[3][...] = matmul(attended_ref[...].T, d_out_ref[...]).astype(jnp.bfloat16)
+
+
+def attend_grads(rows, d_pres, attended, d_out, cut):
+    count, width = rows.shape
+    features = attended.shape[1]
+    by_cols = pl.BlockSpec((count, cut), lambda i: (0, i))
+    whole = pl.BlockSpec((count, features), lambda i: (0, 0))
+    tall = pl.BlockSpec((cut, features), lambda i: (i, 0))
+    return pl.pallas_call(
+        attend_grads_body,
+        grid=(width // cut,),
+        in_specs=[by_cols] + [whole] * 4 + [by_cols],
+        out_specs=[tall] * 3 + [pl.BlockSpec((features, cut), lambda i: (0, i))],
+        out_shape=[jax.ShapeDtypeStruct((width, features), jnp.bfloat16)] * 3
+        + [jax.ShapeDtypeStruct((features, width), jnp.bfloat16)],
+        compiler_params=pltpu.CompilerParams(vmem_limit_bytes=KERNEL_VMEM),
+        cost_estimate=NO_COST,
+        name="attend_grads",
+    )(rows, *d_pres, attended, d_out)
 
 
 def turn_body(piece_ref, out_ref):
@@ -969,76 +1204,46 @@
             result = put(result, came, (member - step) % members)
         return result
 
-    def line_gather(block, ties=(), last=()):
-        from_low, from_high = [block], [block]
-        for step in range(1, members):
-            if step > 1 and ties:
-                from_low[-1], from_high[-1] = after(
-                    (from_low[-1], from_high[-1]), ties[min(step - 2, len(ties) - 1)]
-                )
-            upward = [(m, m + 1) for m in range(step - 1, members - 1)]
-            downward = [(members - 1 - m, members - 2 - m) for m in range(step - 1, members - 1)]
-            from_low.append(lax.ppermute(from_low[-1], "fsdp", upward))
-            from_high.append(lax.ppermute(from_high[-1], "fsdp", downward))
+    def one_hop(low, high, step):
+        upward = [(m, m + 1) for m in range(step - 1, members - 1)]
+        downward = [(members - 1 - m, members - 2 - m) for m in range(step - 1, members - 1)]
+        return lax.ppermute(low, "fsdp", upward), lax.ppermute(high, "fsdp", downward)
+
+    def line_gather(block, first, ties, last):
+        from_low, from_high = [block, first[0]], [block, first[1]]
+        for step in range(2, members):
+            from_low[-1], from_high[-1] = after(
+                (from_low[-1], from_high[-1]), ties[min(step - 2, len(ties) - 1)]
+            )
+            low, high = one_hop(from_low[-1], from_high[-1], step)
+            from_low.append(low)
+            from_high.append(high)
         from_low[-1], from_high[-1] = after((from_low[-1], from_high[-1]), last)
         window = jnp.concatenate(from_low[:0:-1] + [block] + from_high[1:], axis=0)
         size = block.shape[0]
         return lax.dynamic_slice_in_dim(window, (members - 1 - member) * size, members * size, 0)
 
-    def line_scatter(parts, ties=()):
+    def relay(parts, step, sums=None):
         blocks = parts.reshape((members, -1) + parts.shape[1:])
-        up_sum = down_sum = None
-        for step in range(1, members):
-            up_block = take(blocks, jnp.minimum(members - step + member, members - 1))
-            down_block = take(blocks, jnp.maximum(member - (members - step), 0))
-            if up_sum is not None:
-                if ties:
-                    up_sum, down_sum = after(
-                        (up_sum, down_sum), ties[min(step - 2, len(ties) - 1)]
-                    )
-                up_block = (up_block.astype(jnp.float32) + up_sum.astype(jnp.float32)).astype(
-                    parts.dtype
-                )
-                down_block = (down_block.astype(jnp.float32) + down_sum.astype(jnp.float32)).astype(
-                    parts.dtype
-                )
-            up_sum = lax.ppermute(up_block, "fsdp", [(m, m + 1) for m in range(step)])
-            down_sum = lax.ppermute(
-                down_block, "fsdp", [(members - 1 - m, members - 2 - m) for m in range(step)]
+        up_block = take(blocks, jnp.minimum(members - step + member, members - 1))
+        down_block = take(blocks, jnp.maximum(member - (members - step), 0))
+        if sums is not None:
+            up_block, down_block = (
+                (block.astype(jnp.float32) + came.astype(jnp.float32)).astype(parts.dtype)
+                for block, came in zip((up_block, down_block), sums)
             )
-        if ties:
-            up_sum, down_sum = after((up_sum, down_sum), ties[-1])
-        own = take(blocks, member).astype(jnp.float32)
-        return own + up_sum.astype(jnp.float32) + down_sum.astype(jnp.float32)
+        up_pairs = [(m, m + 1) for m in range(step)]
+        down_pairs = [(members - 1 - m, members - 2 - m) for m in range(step)]
+        return (
+            lax.ppermute(up_block, "fsdp", up_pairs),
+            lax.ppermute(down_block, "fsdp", down_pairs),
+        )
 
     column = lax.axis_index("expert")
-    plane_of, j_of = column // local_experts, column % local_experts
-    quarter_of = column % members
-
-    def pairs_to_quarters(turn):
-        return [
-            (plane * local_experts + j, j * members + (plane + turn) % members)
-            for plane in range(members)
-            for j in range(local_experts)
-        ]
 
     def weights_whole(piece):
         gathered = lax.all_gather(piece, "expert", axis=0, tiled=False)
         return gathered.reshape(local_experts, width, -1)
-
-    def grads_out(crossed, tie):
-        came = [
-            lax.ppermute(
-                take(crossed, (quarter_of - turn) % members),
-                "expert",
-                [(b, a) for a, b in pairs_to_quarters(turn)],
-            )
-            for turn in range(members)
-        ]
-        mixed = jnp.zeros_like(crossed)
-        for turn, piece in enumerate(after(came, tie)):
-            mixed = put(mixed, piece, (plane_of + turn) % members)
-        return lax.optimization_barrier([mixed[:, kind] for kind in range(3)])
 
     group_tokens, group_routes, crossed = arrive(
         tokens,
@@ -1070,6 +1275,8 @@
         block,
     )
     attended, log_mass = attend(lows, starts, queries, keys_all, values_all, block)
+    cot_tied = after(cotangent, group_tokens)
+    attended, cot_hop = lax.optimization_barrier((attended, one_hop(cot_tied, cot_tied, 1)))
     attended_by_member = gather(attended, members, math.gcd(count // 16, 4), 1)
     tokens_wide = group_tokens.astype(jnp.float32)
     gain_second = norm2_gain.astype(jnp.float32)
@@ -1080,7 +1287,6 @@
         group_tokens, attended_by_member, out_full, gain_second[None], small_wide, block
     )
     resid_own = own_rows(resid_mid)
-    rate_own = own_rows(rate_second)
 
     router_probs = jax.nn.softmax(small_pre[:, :experts_count], axis=-1)
     switch_all = jax.nn.sigmoid(small_pre[:, experts_count:small_count])
@@ -1107,26 +1313,41 @@
     shared_out, shared_mid, shared_silu, shared_slope = expert(
         normed_second[None], switch_all[None], *shared_weights, False, block
     )
+    group_cot = line_gather(
+        cotangent, cot_hop, (attended_by_member, normed_second), shared_mid
+    )
     row_count = members * capacity
     row_block = math.gcd(row_count, 256)
     rows = dispatch(places_turned, after(normed_second, shared_mid), capacity, members)
-    result, expert_mid, expert_silu, expert_slope, scaled = expert(
-        rows, slot_gates, gate_mats, up_mats, down_mats, True, row_block
-    )
-    by_block = (local_experts, members, capacity, width)
-    block_low = collect(places, scaled.reshape(by_block), shared_out[0], members, switch_all)
-
-    group_cot = line_gather(
-        after(cotangent, attended_by_member), (normed_second, shared_mid), block_low
-    )
 
     grad_wide = group_cot.astype(jnp.float32)
     down_grad = matmul_tn(shared_mid[0], (switch_all * grad_wide).astype(jnp.bfloat16)).astype(
         jnp.bfloat16
     )
     down_sum = lax.psum(down_grad, "expert")
+    switch_dot, _, d_shared_gate, d_shared_up, dh_shared = expert_back(
+        after(group_cot, down_grad)[None],
+        shared_out,
+        switch_all[None],
+        shared_silu,
+        shared_slope,
+        *shared_weights,
+        False,
+        block,
+    )
+    switch_logit = switch_dot[0] * switch_all * (1.0 - switch_all)
+    shared_grads = tuple(
+        pair_grads(normed_second, d_shared_gate[0], d_shared_up[0], math.gcd(width, 512))
+    )
+    shared_sums = lax.psum(shared_grads, "expert")
+
+    result, expert_mid, expert_silu, expert_slope, scaled = expert(
+        after(rows, shared_grads), slot_gates, gate_mats, up_mats, down_mats, True, row_block
+    )
+    by_block = (local_experts, members, capacity, width)
+    block_low = collect(places, scaled.reshape(by_block), shared_out[0], members, switch_all)
     slot_dot, d_rows, d_expert_gate, d_expert_up, d_in = expert_back(
-        dispatch(places_turned, after(group_cot, down_grad), capacity, members),
+        dispatch(places_turned, after(group_cot, block_low), capacity, members),
         result,
         slot_gates,
         expert_silu,
@@ -1137,37 +1358,29 @@
         True,
         row_block,
     )
-    expert_grads = weight_grads(rows, d_rows, d_expert_gate, d_expert_up, expert_mid, members)
+    block_sums = relay(block_low, 1)
+    expert_grads = weight_grads(
+        after(rows, block_sums), d_rows, d_expert_gate, d_expert_up, expert_mid, members
+    )
+    block_sums = relay(block_low, 2, after(block_sums, d_in))
+    slot_dot, block_sums, expert_grads = lax.optimization_barrier(
+        (slot_dot, block_sums, expert_grads)
+    )
+    for step in range(3, members):
+        block_sums = relay(block_low, step, block_sums)
     expert_pieces = lax.psum_scatter(
         expert_grads.reshape((columns, 3) + expert_grads.shape[3:]),
         "expert",
         scatter_dimension=0,
         tiled=True,
     ).reshape(3, members, -1, expert_grads.shape[-1])
-    switch_dot, _, d_shared_gate, d_shared_up, dh_shared = expert_back(
-        after(group_cot, (expert_grads, down_sum))[None],
-        shared_out,
-        switch_all[None],
-        shared_silu,
-        shared_slope,
-        *shared_weights,
-        False,
-        block,
-    )
-    switch_logit = switch_dot[0] * switch_all * (1.0 - switch_all)
-    shared_grads = tuple(
-        grad.astype(jnp.bfloat16)
-        for grad in (
-            matmul_tn(normed_second, d_shared_gate[0]),
-            matmul_tn(normed_second, d_shared_up[0]),
-        )
-    )
-    shared_sums = lax.psum(shared_grads, "expert")
     slot_dots = slot_dot.reshape(local_experts, members, capacity).transpose(1, 0, 2)
     d_gates = jnp.sum(jnp.where(picks, slot_dots[:, :, :, None], 0.0), axis=2)
     d_gates = d_gates.transpose(0, 2, 1).reshape(count, local_experts)
-    d_choice = lax.dynamic_update_slice_in_dim(
-        jnp.zeros_like(router_probs), d_gates, member * local_experts, 1
+    ids = jnp.arange(experts_count, dtype=jnp.int32)
+    d_choice = sum(
+        jnp.where(ids[None, :] == own_ids[which], d_gates[:, which : which + 1], 0.0)
+        for which in range(local_experts)
     )
     d_logits = router_probs * (d_choice - jnp.sum(gates * d_gates, axis=-1, keepdims=True))
     d_small = jnp.concatenate([d_logits, switch_logit], axis=1)
@@ -1182,21 +1395,25 @@
         ((0, 128 - 2 * small_count), (0, 0)),
     )
     dh_low = collect(
-        places, d_in.reshape(by_block), dh_shared[0], members, d_small_both, small_both
+        places,
+        after(d_in, (expert_grads, shared_sums, down_sum, block_sums)).reshape(by_block),
+        dh_shared[0],
+        members,
+        d_small_both,
+        small_both,
     )
     small_part = matmul_tn(normed_second, d_small_both)
     small_part = small_part[:, :small_count] + small_part[:, small_count : 2 * small_count]
 
-    block_own = line_scatter(block_low, (d_in, dh_shared, shared_grads))
-    block_out = (resid_own + block_own).astype(jnp.bfloat16)
-    dh_second_own = scatter(after(dh_low, shared_grads), members, 2)
-
-    grad_own = cotangent.astype(jnp.float32)
-    d_resid_own = norm_back(grad_own, dh_second_own, resid_own, rate_own, gain_second)
-    d_attn_own = d_resid_own.astype(jnp.bfloat16)
-    norm2_part = jnp.sum(dh_second_own * resid_own * rate_own, axis=0)
-    d_attn_out = gather(d_attn_own, members, 3 if own_count % 48 == 0 else 1, 3)
-    d_attn_out = d_attn_out.reshape(count, width)
+    d_resid_own, norm2_part, d_attn_out = turnaround(
+        dh_low,
+        resid_mid,
+        rate_second,
+        cotangent,
+        gain_second[None],
+        members,
+        2,
+    )
     d_context = matmul_nt(d_attn_out, out_weight).astype(jnp.bfloat16)
     d_query_pre, d_key_pre, d_value_pre = attend_back(
         lows,
@@ -1211,10 +1428,7 @@
         block,
     )
 
-    d_query_pre, d_key_pre, d_value_pre = after(
-        (d_query_pre, d_key_pre, d_value_pre), shared_sums
-    )
-    dh_first_low, norm1_part = unproject(
+    dh_first_low, norm1_part, *biases = unproject(
         (d_query_pre, d_key_pre, d_value_pre),
         (query_weight, key_weight, value_weight),
         group_tokens,
@@ -1222,39 +1436,44 @@
         block,
     )
     norm1_part = norm1_part[0]
-    attn_grads = tuple(
-        matmul_tn(normed_first, d_pre).astype(jnp.bfloat16)
-        for d_pre in (d_query_pre, d_key_pre, d_value_pre)
-    ) + (matmul_tn(attended, d_attn_out).astype(jnp.bfloat16),)
+    attn_grads = attend_grads(
+        after(normed_first, dh_first_low),
+        (d_query_pre, d_key_pre, d_value_pre),
+        attended,
+        d_attn_out,
+        math.gcd(width, 512),
+    )
     crossed_grads = exchange(after(expert_pieces, d_attn_out).transpose(1, 0, 2, 3))
-    dh_first_own = scatter(
-        after(dh_first_low, (attn_grads, crossed_grads)), members, 4
-    )
+    line_parts = jnp.concatenate([norm1_part, norm2_part, small_part.T.reshape(-1)])
+    stats = jnp.concatenate([line_parts] + [bias[0] for bias in biases]).reshape(-1, 128)
+    dh_first_own, stats, mixed_grads = scatter(
+        after(dh_first_low, attn_grads),
+        jnp.pad(stats, ((0, -stats.shape[0] % 8), (0, 0))),
+        crossed_grads,
+        line_parts.shape[0] // 128,
+        members,
+        columns,
+        4,
+        LONG_COST,
+    )
+    shared_sums, down_sum, block_low, block_sums = after(
+        (shared_sums, down_sum, block_low, block_sums), dh_first_own
+    )
+    stats = stats.reshape(-1)
+    block_out = resid_own + own_rows(block_low).astype(jnp.float32)
+    for came in block_sums:
+        block_out = block_out + came.astype(jnp.float32)
+    block_out = block_out.astype(jnp.bfloat16)
     grad_tokens = norm_back(
         d_resid_own, dh_first_own, tokens_own_wide, own_rows(rate_first), gain_first
     )
 
-    def pair_sum(values, axis, size):
-        if size & (size - 1):
-            return lax.psum(values, axis)
-        for bit in range(size.bit_length() - 1):
-            pairs = [(place, place ^ (1 << bit)) for place in range(size)]
-            values = values + lax.ppermute(values, axis, pairs)
-        return values
-
-    biases = [
-        jnp.sum(d_pre.astype(jnp.float32), axis=0)
-        for d_pre in (d_query_pre, d_key_pre, d_value_pre)
-    ]
-    stats = pair_sum(
-        jnp.concatenate([norm1_part, norm2_part, small_part.T.reshape(-1)]), "fsdp", members
-    )
-    stats = pair_sum(jnp.concatenate([stats] + biases), "expert", columns)
     small_sum = stats[2 * width : (2 + small_count) * width].reshape(-1, width)
-    bias_sums = stats[(2 + small_count) * width :].reshape(3, -1)
-
-    attn_sums = lax.psum(attn_grads, "expert")
-    expert_sums = grads_out(crossed_grads, dh_first_own)
+    bias_end = line_parts.shape[0] + 3 * biases[0].shape[1]
+    bias_sums = stats[line_parts.shape[0] : bias_end].reshape(3, -1)
+
+    attn_sums = after(lax.psum(attn_grads, "expert"), dh_first_own)
+    expert_sums = [mixed_grads[:, kind] for kind in range(3)]
 
     return (
         block_out,

time: 1540 us -> 1390 us (0.903)
  waiting for transfers between devices: 158 us -> 58.1 us
  matrix products: 74.7 us -> 20.1 us
  Pallas kernels: 1030 us -> 1080 us
  starting transfers between devices: 60.6 us -> 37.3 us
  local copies, waits for them, and re-layouts: 113 us -> 90.7 us
    pallas_call x2 -> x4, Pallas kernels: 230 us -> 372 us  [the longest x1 183 us: turnaround(): pl.pallas_call(functools.partial(turnaround_body, pieces), in_specs=[in_v...]
    pallas_call x2 -> x1, Pallas kernels: 201 us -> 101 us  [gather(): pl.pallas_call(functools.partial(gather_body, pieces), in_specs=[pl.Block...]
    dot_general x8 -> x2, matrix products: 67.8 us -> 16.5 us  [matmul_tn(): lax.dot_general(left_matrix, right_matrix, (((0,), (0,)), ((), ())), pref...]
    reduce_scatter x1, waiting for transfers between devices: 50.6 us -> 0.01 us  [shards(): lax.psum_scatter(expert_grads.reshape((columns, 3) + expert_grads.shape[3...]
    psum x2 -> x1, waiting for transfers between devices: 32 us -> 0.01 us  [shards(): attn_sums = after(lax.psum(attn_grads, 'expert'), dh_first_own)]
    ppermute x21 -> x12, starting transfers between devices: 56.2 us -> 33.7 us  [the longest x3 15.1 us: relay(): lax.ppermute(up_block, 'fsdp', up_pairs)]
    unnamed x175 -> x188, local copies, waits for them, and re-layouts: 63.7 us -> 57.6 us
  transfers between devices with their start and end apart: 32 -> 22, of which waited for: 8 -> 4; matrix products, arithmetic and copies ran while one was open for 11% -> 7% of each run, Pallas kernels for 67% -> 79%
where the time goes in v3:
time: 1390 us; the launch traced here: 1370 us
  Pallas kernels  1080 us (78%)
  local copies, waits for them, and re-layouts  90.7 us (7%)
  other arithmetic  70.3 us (5%)
  waiting for transfers between devices  58.1 us (4%)
  starting transfers between devices  37.3 us (3%)
  matrix products  20.1 us (1%)
  between operations  15.9 us (1%)
    pallas_call x1, Pallas kernels, arrive(): pl.pallas_call(functools.partial(arrive_body, members, local_experts, pie...  218 us
    pallas_call x1, Pallas kernels, turnaround(): pl.pallas_call(functools.partial(turnaround_body, pieces), in_specs=[in_v...  183 us
    pallas_call x1, Pallas kernels, scatter(): pl.pallas_call(functools.partial(scatter_body, pieces, columns, line_rows...  150 us
    pallas_call x2, Pallas kernels, expert_back(): pl.pallas_call(functools.partial(expert_back_body, turned), grid=(experts...  104 us
    pallas_call x1, Pallas kernels, gather(): pl.pallas_call(functools.partial(gather_body, pieces), in_specs=[pl.Block...  101 us
    pallas_call x2, Pallas kernels, expert(): pl.pallas_call(functools.partial(expert_body, turned), grid=(experts, cou...  97 us
    unnamed x188, local copies, waits for them, and re-layouts  57.6 us
    pallas_call x1, Pallas kernels, weight_grads(): pl.pallas_call(weight_grads_body, grid=(experts, members), in_specs=[by_c...  45.9 us
  transfers between devices with their start and end apart: 22, of which 4 were waited for; matrix products, arithmetic and copies ran while one was open for 7% of the time, Pallas kernels for 79%

profile of v3, /device:TPU:0, one launch (start us, length us, event | category | flops | bytes accessed | tf_op | source)
XLA Modules:
  0.0 1371.8 jit_solution(6728217142176343362)
XLA Ops:
  12.1 218.1 %arrive.1 = (bf16[4,384,2048]{2,1,0:T(8,128)(2,1)}, s32[4,4,384]{2,1,0:T(4,128)}, bf16[4,128,1408]{2,1,0:T(8,128)(2,1)}, bf16[4,128,1408]{2,1,0:T(8,128)(2,1)}, ...) custom-call(bf16[384,2048]{1,0:T(8,128)(2,1)} %refs_0_.1, ...), custom_call_target="tpu_custom_call" | custom-call | tf_op jit(solution)/shard_map/arrive/pallas_call | solution.py:735
  233.0 5.7 collective-permute-start
  239.2 2.8 fusion.18
  242.6 14.1 %project.1 = (bf16[1536,2048]{1,0:T(8,128)(2,1)}, f32[1536,1]{1,0:T(8,128)S(1)}, bf16[1536,512]{1,0:T(8,128)(2,1)S(1)}, bf16[1536,512]{1,0:T(8,128)(2,1)S(1)}, bf16[1536,512]{1,0:T(8,128)(2,1)S(1)}) custom-call(bf16[1536,2048]{1,0:T(8,128)(2,1)} %bitcast.162, f32[1,2048]{1,0:T(1,128)S(1)} %bitcast.140, bf16[2048,512]{1,0:T(8,128)(2,1)S(1)} %copy-done.11, ...), custom_call_target="tpu_custom_call" | custom-call | tf_op jit(solution)/shard_map/project/pallas_call | solution.py:117
  256.8 23.0 %attend.1 = (bf16[1536,512]{1,0:T(8,128)(2,1)S(1)}, f32[4,1,1536]{2,1,0:T(1,128)S(1)}) custom-call(s32[6]{0:T(128)S(1)} %and_select_fusion.lows_ref, s32[1,1536]{1,0:T(1,128)S(1)} %subtract_subtract_fusion.starts_ref, bf16[1536,512]{1,0:T(8,128)(2,1)S(1)} %get-tuple-element.109.query_ref, bf16[1536,512]{1,0:T(8,128)(2,1)S(1)} %get-tuple-element.110.key_ref, ...), custom_call_target="tpu_custom_call" | custom-call | tf_op jit(solution)/shard_map/attend/pallas_call | solution.py:175
  282.2 101.1 %gather.1.attended_ref = bf16[4,1536,512]{2,1,0:T(8,128)(2,1)} custom-call(bf16[1536,512]{1,0:T(8,128)(2,1)} %copy-done.33), custom_call_target="tpu_custom_call" | custom-call | tf_op jit(solution)/shard_map/gather/pallas_call | solution.py:777
  387.4 22.2 %settle.1 = (f32[1536,2048]{1,0:T(8,128)}, f32[1536,1]{1,0:T(8,128)S(1)}, bf16[1536,2048]{1,0:T(8,128)(2,1)S(1)}, f32[1536,128]{1,0:T(8,128)S(1)}) custom-call(bf16[1536,2048]{1,0:T(8,128)(2,1)} %bitcast.163, bf16[4,1536,512]{2,1,0:T(8,128)(2,1)} %gather.1.attended_ref, bf16[2048,2048]{1,0:T(8,128)(2,1)} %all-gather.8.cloned.1.call-done.weight_ref, ...), custom_call_target="tpu_custom_call" | custom-call | flops 12884901888 | bytes 37748736 | tf_op jit(solution)/shard_map/settle/pallas_call | solution.py:304
  413.1 6.3 collective-permute-done.3
  424.1 38.9 %expert.2 = (f32[1,1536,2048]{2,1,0:T(8,128)}, bf16[1,1536,1408]{2,1,0:T(8,128)(2,1)}, f32[1,1536,1408]{2,1,0:T(8,128)}, f32[1,1536,1408]{2,1,0:T(8,128)}) custom-call(bf16[1,1536,2048]{2,1,0:T(8,128)(2,1)} %bitcast.124, f32[1,1536,1]{2,1,0:T(8,128)} %bitcast.130, bf16[1,2048,1408]{2,1,0:T(8,128)(2,1)} %bitcast.165, bf16[1,2048,1408]{2,1,0:T(8,128)(2,1)} %bitcast.167, ...), custom_call_target="tpu_custom_call" | custom-call | tf_op jit(solution)/shard_map/expert/pallas_call | solution.py:458
  463.0 2.8 copy-done.3
  465.8 6.5 dispatch.2
  472.2 2.7 constant_dynamic-update-slice_fusion.8
  475.0 2.8 constant_dynamic-update-slice_fusion.7
  477.8 2.7 constant_dynamic-update-slice_fusion.6
  487.2 2.9 constant_dynamic-update-slice_fusion.2
  490.1 3.4 constant_dynamic-slice_fusion.1.source_ref
  493.6 11.3 convolution_convert_fusion
  504.9 42.7 %expert_back.2 = (f32[1,1536,1]{2,1,0:T(8,128)}, bf16[1,1536,2048]{2,1,0:T(8,128)(2,1)}, bf16[1,1536,1408]{2,1,0:T(8,128)(2,1)}, bf16[1,1536,1408]{2,1,0:T(8,128)(2,1)}, f32[1,1536,2048]{2,1,0:T(8,128)}) custom-call(bf16[1,1536,2048]{2,1,0:T(8,128)(2,1)} %bitcast.125, f32[1,1536,2048]{2,1,0:T(8,128)} %get-tuple-element.128.result_ref, ...), custom_call_target="tpu_custom_call" | custom-call | tf_op jit(solution)/shard_map/expert_back/pallas_call | solution.py:491
  552.0 22.8 %pair_grads.1 = (bf16[2048,1408]{1,0:T(8,128)(2,1)S(1)}, bf16[2048,1408]{1,0:T(8,128)(2,1)}) custom-call(bf16[1536,2048]{1,0:T(8,128)(2,1)} %copy-done.2, bf16[1536,1408]{1,0:T(8,128)(2,1)S(1)} %bitcast.136, bf16[1536,1408]{1,0:T(8,128)(2,1)S(1)} %bitcast.137), custom_call_target="tpu_custom_call" | custom-call | tf_op jit(solution)/shard_map/pair_grads/pallas_call | solution.py:546
  583.0 58.1 %expert.3 = (bf16[2,1024,2048]{2,1,0:T(8,128)(2,1)}, bf16[2,1024,1408]{2,1,0:T(8,128)(2,1)}, f32[2,1024,1408]{2,1,0:T(8,128)}, f32[2,1024,1408]{2,1,0:T(8,128)}, bf16[2,1024,2048]{2,1,0:T(8,128)(2,1)}) custom-call(bf16[2,1024,2048]{2,1,0:T(8,128)(2,1)} %bitcast.152, f32[2,1024,1]{2,1,0:T(8,128)} %copy.104.scale_ref, bf16[2,2048,1408]{2,1,0:T(8,128)(2,1)} %bitcast.155, ...), custom_call_target="tpu_custom_call" | custom-call | tf_op jit(solution)/shard_map/expert/pallas_call | solution.py:458
  641.2 9.3 collect.2
  655.8 6.9 collective-permute-start.6
  662.8 2.8 copy-done.5
  665.6 6.5 dispatch.3
  672.1 61.0 %expert_back.3 = (f32[2,1024,1]{2,1,0:T(8,128)}, bf16[2,1024,2048]{2,1,0:T(8,128)(2,1)}, bf16[2,1024,1408]{2,1,0:T(8,128)(2,1)}, bf16[2,1024,1408]{2,1,0:T(8,128)(2,1)}, bf16[2,1024,2048]{2,1,0:T(8,128)(2,1)}) custom-call(bf16[2,1024,2048]{2,1,0:T(8,128)(2,1)} %bitcast.161, bf16[2,1024,2048]{2,1,0:T(8,128)(2,1)} %get-tuple-element.143.result_ref, ...), custom_call_target="tpu_custom_call" | custom-call | tf_op jit(solution)/shard_map/expert_back/pallas_call | solution.py:491
  733.2 5.5 fusion.6
  745.7 45.9 %weight_grads.1 = bf16[2,4,3,512,1408]{4,3,2,1,0:T(8,128)(2,1)} custom-call(bf16[2,1024,2048]{2,1,0:T(8,128)(2,1)} %bitcast.153, bf16[2,1024,2048]{2,1,0:T(8,128)(2,1)} %get-tuple-element.151.d_out_ref, bf16[2,1024,1408]{2,1,0:T(8,128)(2,1)S(1)} %copy-done.36, bf16[2,1024,1408]{2,1,0:T(8,128)(2,1)S(1)} %copy-done.37, ...), custom_call_target="tpu_custom_call" | custom-call | tf_op jit(solution)/shard_map/weight_grads/pallas_call | solution.py:523
  809.1 6.1 fusion.5
  816.6 5.7 collective-permute-start.10
  824.7 5.1 fusion.26
  831.5 15.8 %collective-permute-done.11 = bf16[384,2048]{1,0:T(8,128)(2,1)} collective-permute-done((bf16[384,2048]{1,0:T(8,128)(2,1)}, bf16[384,2048]{1,0:T(8,128)(2,1)}, u32[]{:S(2)}, u32[]{:S(2)}) %collective-permute-start.11) | collective-permute-done | bytes 1572896 | tf_op jit(solution)/shard_map/ppermute | solution.py:1239
  849.6 13.3 collect.3
  865.6 182.9 %turnaround.1 = (f32[384,2048]{1,0:T(8,128)S(1)}, f32[1,2048]{1,0:T(1,128)S(1)}, bf16[4,384,2048]{2,1,0:T(8,128)(2,1)S(1)}) custom-call(bf16[4,384,2048]{2,1,0:T(8,128)(2,1)} %bitcast.129, f32[1536,2048]{1,0:T(8,128)} %get-tuple-element.115.refs_1_, f32[1536,1]{1,0:T(8,128)S(1)} %copy-done.49, bf16[384,2048]{1,0:T(8,128)(2,1)S(1)} %copy-done.24, ...), custom_call_target="tpu_custom_call" | custom-call | tf_op jit(solution)/shard_map/turnaround/pallas_call | solution.py:1035
  1052.9 3.8 dynamic-slice_bitcast_fusion.2
  1057.8 3.5 convolution_convert_fusion.1.grad_ref
  1061.4 29.5 %attend_back.1 = (bf16[1536,512]{1,0:T(8,128)(2,1)S(1)}, bf16[1536,512]{1,0:T(8,128)(2,1)S(1)}, bf16[1536,512]{1,0:T(8,128)(2,1)S(1)}) custom-call(s32[6]{0:T(128)S(1)} %copy-done.57, s32[1,1536]{1,0:T(1,128)S(1)} %copy-done.53, bf16[1536,512]{1,0:T(8,128)(2,1)S(1)} %copy-done.26, bf16[1536,512]{1,0:T(8,128)(2,1)S(1)} %copy-done.28, ...), custom_call_target="tpu_custom_call" | custom-call | tf_op jit(solution)/shard_map/attend_back/pallas_call | solution.py:251
  1091.0 14.5 %unproject.1 = (bf16[1536,2048]{1,0:T(8,128)(2,1)}, f32[1,2048]{1,0:T(1,128)S(1)}, f32[1,512]{1,0:T(1,128)S(1)}, f32[1,512]{1,0:T(1,128)S(1)}, f32[1,512]{1,0:T(1,128)S(1)}) custom-call(bf16[1536,512]{1,0:T(8,128)(2,1)S(1)} %get-tuple-element.165.refs_0_.d_query, bf16[1536,512]{1,0:T(8,128)(2,1)S(1)} %get-tuple-element.166.refs_1_.d_key, ...), custom_call_target="tpu_custom_call" | custom-call | tf_op jit(solution)/shard_map/unproject/pallas_call | solution.py:1090
  1105.5 16.5 %attend_grads.1 = (bf16[2048,512]{1,0:T(8,128)(2,1)S(1)}, bf16[2048,512]{1,0:T(8,128)(2,1)S(1)}, bf16[2048,512]{1,0:T(8,128)(2,1)S(1)}, bf16[512,2048]{1,0:T(8,128)(2,1)}) custom-call(bf16[1536,2048]{1,0:T(8,128)(2,1)} %get-tuple-element.171.rows_ref, bf16[1536,512]{1,0:T(8,128)(2,1)S(1)} %get-tuple-element.165.refs_0_.d_query, ...), custom_call_target="tpu_custom_call" | custom-call | tf_op jit(solution)/shard_map/attend_grads/pallas_call | solution.py:1121
  1126.0 2.7 collective-permute-start.13
  1132.2 33.4 %collective-permute-done.13 = bf16[3,128,1408]{2,1,0:T(8,128)(2,1)S(1)} collective-permute-done((bf16[3,128,1408]{2,1,0:T(8,128)(2,1)}, bf16[3,128,1408]{2,1,0:T(8,128)(2,1)S(1)}, u32[]{:S(2)}, u32[]{:S(2)}) %collective-permute-start.13) | collective-permute-done | bytes 1081376 | tf_op jit(solution)/shard_map/ppermute | solution.py:1203
  1166.0 150.1 %scatter.1 = (f32[384,2048]{1,0:T(8,128)S(1)}, f32[192,128]{1,0:T(8,128)S(1)}, bf16[4,3,128,1408]{3,2,1,0:T(8,128)(2,1)S(1)}) custom-call(bf16[4,384,2048]{2,1,0:T(8,128)(2,1)} %bitcast.201, f32[192,128]{1,0:T(8,128)S(1)} %pad.19.stats_ref, bf16[4,3,128,1408]{3,2,1,0:T(8,128)(2,1)S(1)} %bitcast_dynamic-update-slice_fusion.crossed_ref), custom_call_target="tpu_custom_call" | custom-call | flops 99999997952 | tf_op jit(solution)/shard_map/scatter/pallas_call | solution.py:958
  1320.3 3.1 convert.14
  1330.2 2.7 convert_element_type.202
  1332.9 2.7 convert_element_type.203
  1339.3 5.7 convert_element_type.205
  1345.0 5.2 convert_element_type.206
  1350.2 6.0 convert_element_type.207
  1356.2 5.7 add_convert_fusion
  (307 shorter events, 112.6 us)
Async XLA Ops:
  7.2 380.1 %all-gather.8.cloned.1.call-start = ((), (), s32[]{:S(2)}) async-start(), calls=%async_computation.1 | async-start | bytes 8650752 | tf_op jit(solution)/shard_map/all_gather | solution.py:1257
  9.5 573.5 %all-gather.10.cloned.1.call-start = ((), (), s32[]{:S(2)}) async-start(), calls=%async_computation.3 | async-start | bytes 12976128 | tf_op jit(solution)/shard_map/all_gather | solution.py:1245
  230.3 352.7 %all-gather.12.cloned.1.call-start = ((), (), s32[]{:S(2)}) async-start(), calls=%async_computation.4 | async-start | bytes 12976128 | tf_op jit(solution)/shard_map/all_gather | solution.py:1245
  231.0 352.0 %all-gather.14.cloned.1.call-start = ((), (), s32[]{:S(2)}) async-start(), calls=%async_computation.5 | async-start | bytes 12976128 | tf_op jit(solution)/shard_map/all_gather | solution.py:1245
  231.6 616.9 %all-reduce.11.cloned.1.call-start = ((), (), s32[]{:S(2)}) async-start(), calls=%async_computation.7 | async-start | bytes 34603008 | tf_op jit(solution)/shard_map/psum | solution.py:1342
  231.7 50.5 %collective-permute-start.1 = (bf16[384,2048]{1,0:T(8,128)(2,1)}, bf16[384,2048]{1,0:T(8,128)(2,1)}, u32[]{:S(2)}, u32[]{:S(2)}) collective-permute-start(bf16[384,2048]{1,0:T(8,128)(2,1)} %refs_3_.2), channel_id=1, source_target_pairs={{3,2},{2,1},{1,0},{7,6},{6,5},{5,4},{11,10},{10,9},{9,8},{15,14},{... | collective-permute-start | bytes 4718600 | tf_op jit(solution)/shard_map/ppermute | solution.py:1210
  233.0 49.2 %collective-permute-start = (bf16[384,2048]{1,0:T(8,128)(2,1)}, bf16[384,2048]{1,0:T(8,128)(2,1)}, u32[]{:S(2)}, u32[]{:S(2)}) collective-permute-start(bf16[384,2048]{1,0:T(8,128)(2,1)} %refs_3_.2), channel_id=1, source_target_pairs={{0,1},{1,2},{2,3},{4,5},{5,6},{6,7},{8,9},{9,10},{10,11},{12,13},{... | collective-permute-start | bytes 4718600 | tf_op jit(solution)/shard_map/ppermute | solution.py:1210
  238.9 148.4 %copy-start.54 = (f32[2048]{0:T(1024)}, f32[2048]{0:T(1024)S(1)}, u32[]{:S(2)}) copy-start(f32[2048]{0:T(1024)S(1)} %broadcast_in_dim.174) | copy-start | bytes 24580
  242.5 14.2 %copy-start.19 = (f32[1536,128]{1,0:T(8,128)}, f32[1536,128]{1,0:T(8,128)S(1)}, u32[]{:S(2)}) copy-start(f32[1536,128]{1,0:T(8,128)S(1)} %get-tuple-element.234.c.rest_0_) | copy-start | bytes 2359300
  242.5 14.2 %copy-start.21 = (f32[1536,128]{1,0:T(8,128)}, f32[1536,128]{1,0:T(8,128)S(1)}, u32[]{:S(2)}) copy-start(f32[1536,128]{1,0:T(8,128)S(1)} %get-tuple-element.235.s.rest_1_) | copy-start | bytes 2359300
  256.7 23.1 %copy-start.27 = (bf16[1536,512]{1,0:T(8,128)(2,1)}, bf16[1536,512]{1,0:T(8,128)(2,1)S(1)}, u32[]{:S(2)}) copy-start(bf16[1536,512]{1,0:T(8,128)(2,1)S(1)} %get-tuple-element.110.key_ref) | copy-start | bytes 4718596
  256.7 25.4 %copy-start.29 = (bf16[1536,512]{1,0:T(8,128)(2,1)}, bf16[1536,512]{1,0:T(8,128)(2,1)S(1)}, u32[]{:S(2)}) copy-start(bf16[1536,512]{1,0:T(8,128)(2,1)S(1)} %get-tuple-element.111.value_ref) | copy-start | bytes 4718596
  256.7 25.4 %copy-start.46 = (f32[1536,1]{1,0:T(8,128)}, f32[1536,1]{1,0:T(8,128)S(1)}, u32[]{:S(2)}) copy-start(f32[1536,1]{1,0:T(8,128)S(1)} %get-tuple-element.168.refs_7_) | copy-start | bytes 18436
  256.8 126.5 %copy-start.56 = (s32[6]{0:T(128)}, s32[6]{0:T(128)S(1)}, u32[]{:S(2)}) copy-start(s32[6]{0:T(128)S(1)} %and_select_fusion.lows_ref) | copy-start | bytes 76
  256.8 25.3 %copy-start.52 = (s32[1,1536]{1,0:T(1,128)}, s32[1,1536]{1,0:T(1,128)S(1)}, u32[]{:S(2)}) copy-start(s32[1,1536]{1,0:T(1,128)S(1)} %subtract_subtract_fusion.starts_ref) | copy-start | bytes 18436
  282.2 104.7 %copy-start.68 = (bf16[2048,8]{0,1:T(8,128)(2,1)S(1)}, bf16[2048,8]{0,1:T(8,128)(2,1)}, u32[]{:S(2)}) copy-start(bf16[2048,8]{0,1:T(8,128)(2,1)} %param.34) | copy-start | bytes 98308
  282.2 104.7 %copy-start.74 = (bf16[2048]{0:T(1024)(128)(2,1)S(1)}, bf16[2048]{0:T(1024)(128)(2,1)}, u32[]{:S(2)}) copy-start(bf16[2048]{0:T(1024)(128)(2,1)} %param.35) | copy-start | bytes 12292
  383.3 29.8 %collective-permute-start.2 = (bf16[384,2048]{1,0:T(8,128)(2,1)}, bf16[384,2048]{1,0:T(8,128)(2,1)}, u32[]{:S(2)}, u32[]{:S(2)}) collective-permute-start(bf16[384,2048]{1,0:T(8,128)(2,1)} %collective-permute-done), channel_id=1, source_target_pairs={{1,2},{2,3},{5,6},{6,7},{9,10},{10,11},{13,14},{14,15},{17,18},{18... | collective-permute-start | bytes 4718600 | tf_op jit(solution)/shard_map/ppermute | solution.py:1210
  385.1 34.4 %collective-permute-start.3 = (bf16[384,2048]{1,0:T(8,128)(2,1)}, bf16[384,2048]{1,0:T(8,128)(2,1)}, u32[]{:S(2)}, u32[]{:S(2)}) collective-permute-start(bf16[384,2048]{1,0:T(8,128)(2,1)} %collective-permute-done.1), channel_id=1, source_target_pairs={{2,1},{1,0},{6,5},{5,4},{10,9},{9,8},{14,13},{13,12},{18,17},{17,1... | collective-permute-start | bytes 4718600 | tf_op jit(solution)/shard_map/ppermute | solution.py:1210
  387.4 35.2 %copy-start.69 = (s32[4,4,384]{2,1,0:T(4,128)S(1)}, s32[4,4,384]{2,1,0:T(4,128)}, u32[]{:S(2)}) copy-start(s32[4,4,384]{2,1,0:T(4,128)} %get-tuple-element.135) | copy-start | bytes 73732
  419.5 52.8 %collective-permute-start.4 = (bf16[384,2048]{1,0:T(8,128)(2,1)}, bf16[384,2048]{1,0:T(8,128)(2,1)}, u32[]{:S(2)}, u32[]{:S(2)}) collective-permute-start(bf16[384,2048]{1,0:T(8,128)(2,1)} %collective-permute-done.2), channel_id=1, source_target_pairs={{2,3},{6,7},{10,11},{14,15},{18,19},{22,23},{26,27},{30,31}} | collective-permute-start | bytes 4718600 | tf_op jit(solution)/shard_map/ppermute | solution.py:1210
  421.3 51.0 %collective-permute-start.5 = (bf16[384,2048]{1,0:T(8,128)(2,1)}, bf16[384,2048]{1,0:T(8,128)(2,1)}, u32[]{:S(2)}, u32[]{:S(2)}) collective-permute-start(bf16[384,2048]{1,0:T(8,128)(2,1)} %collective-permute-done.3), channel_id=1, source_target_pairs={{1,0},{5,4},{9,8},{13,12},{17,16},{21,20},{25,24},{29,28}} | collective-permute-start | bytes 4718600 | tf_op jit(solution)/shard_map/ppermute | solution.py:1210
  577.3 475.6 %reduce-scatter.2.cloned.1.call-start = ((), (), s32[]{:S(2)}) async-start(), calls=%async_computation.2 | async-start | bytes 38928384 | tf_op jit(solution)/shard_map/reduce_scatter | solution.py:1371
  583.0 58.1 %copy-start.8 = (f32[1536,1]{1,0:T(8,128)S(1)}, f32[1536,1]{1,0:T(8,128)}, u32[]{:S(2)}) copy-start(f32[1536,1]{1,0:T(8,128)} %get-tuple-element.209.rest_0_) | copy-start | bytes 18436
  583.0 58.1 %copy-start.17 = (s32[4,384,2]{2,1,0:T(8,128)S(1)}, s32[4,384,2]{2,1,0:T(8,128)}, u32[]{:S(2)}) copy-start(s32[4,384,2]{2,1,0:T(8,128)} %copy.100) | copy-start | bytes 36868
  654.0 79.1 %collective-permute-start.7 = (bf16[384,2048]{1,0:T(8,128)(2,1)}, bf16[384,2048]{1,0:T(8,128)(2,1)}, u32[]{:S(2)}, u32[]{:S(2)}) collective-permute-start(bf16[384,2048]{1,0:T(8,128)(2,1)} %get-tuple-element.214), channel_id=1, source_target_pairs={{3,2},{7,6},{11,10},{15,14},{19,18},{23,22},{27,26},{31,30}} | collective-permute-start | bytes 4718600 | tf_op jit(solution)/shard_map/ppermute | solution.py:1239
  655.8 77.3 %collective-permute-start.6 = (bf16[384,2048]{1,0:T(8,128)(2,1)}, bf16[384,2048]{1,0:T(8,128)(2,1)}, u32[]{:S(2)}, u32[]{:S(2)}) collective-permute-start(bf16[384,2048]{1,0:T(8,128)(2,1)} %get-tuple-element.215), channel_id=1, source_target_pairs={{0,1},{4,5},{8,9},{12,13},{16,17},{20,21},{24,25},{28,29}} | collective-permute-start | bytes 4718600 | tf_op jit(solution)/shard_map/ppermute | solution.py:1238
  738.7 52.9 %collective-permute-start.9 = (bf16[384,2048]{1,0:T(8,128)(2,1)S(1)}, bf16[384,2048]{1,0:T(8,128)(2,1)}, u32[]{:S(2)}, u32[]{:S(2)}) collective-permute-start(bf16[384,2048]{1,0:T(8,128)(2,1)S(1)} %get-tuple-element.212), channel_id=1, source_target_pairs={{3,2},{2,1},{7,6},{6,5},{11,10},{10,9},{15,14},{14,13},{19,18},{18... | collective-permute-start | bytes 4718600 | tf_op jit(solution)/shard_map/ppermute | solution.py:1239
  740.5 51.0 %collective-permute-start.8 = (bf16[384,2048]{1,0:T(8,128)(2,1)S(1)}, bf16[384,2048]{1,0:T(8,128)(2,1)}, u32[]{:S(2)}, u32[]{:S(2)}) collective-permute-start(bf16[384,2048]{1,0:T(8,128)(2,1)S(1)} %get-tuple-element.213), channel_id=1, source_target_pairs={{0,1},{1,2},{4,5},{5,6},{8,9},{9,10},{12,13},{13,14},{16,17},{17,1... | collective-permute-start | bytes 4718600 | tf_op jit(solution)/shard_map/ppermute | solution.py:1238
  791.6 528.1 %all-reduce.9.cloned.1.call-start = ((), (), s32[]{:S(2)}) async-start(), calls=%async_computation.6 | async-start | bytes 16777216 | tf_op jit(solution)/shard_map/psum | solution.py:1475
  809.1 13.2 copy-start.61
  809.1 13.7 copy-start.67
  815.3 32.0 %collective-permute-start.11 = (bf16[384,2048]{1,0:T(8,128)(2,1)}, bf16[384,2048]{1,0:T(8,128)(2,1)}, u32[]{:S(2)}, u32[]{:S(2)}) collective-permute-start(bf16[384,2048]{1,0:T(8,128)(2,1)} %get-tuple-element.210), channel_id=1, source_target_pairs={{3,2},{2,1},{1,0},{7,6},{6,5},{5,4},{11,10},{10,9},{9,8},{15,14},{... | collective-permute-start | bytes 4718600 | tf_op jit(solution)/shard_map/ppermute | solution.py:1239
  816.6 31.9 %collective-permute-start.10 = (bf16[384,2048]{1,0:T(8,128)(2,1)}, bf16[384,2048]{1,0:T(8,128)(2,1)}, u32[]{:S(2)}, u32[]{:S(2)}) collective-permute-start(bf16[384,2048]{1,0:T(8,128)(2,1)} %get-tuple-element.211), channel_id=1, source_target_pairs={{0,1},{1,2},{2,3},{4,5},{5,6},{6,7},{8,9},{9,10},{10,11},{12,13},{... | collective-permute-start | bytes 4718600 | tf_op jit(solution)/shard_map/ppermute | solution.py:1238
  824.7 23.8 %copy-start.18 = (s32[4,384,2]{2,1,0:T(8,128)S(1)}, s32[4,384,2]{2,1,0:T(8,128)}, u32[]{:S(2)}) copy-start(s32[4,384,2]{2,1,0:T(8,128)} %copy.100) | copy-start | bytes 36868
  849.6 16.1 %copy-start.24 = (bf16[384,2048]{1,0:T(8,128)(2,1)S(1)}, bf16[384,2048]{1,0:T(8,128)(2,1)}, u32[]{:S(2)}) copy-start(bf16[384,2048]{1,0:T(8,128)(2,1)} %refs_3_.2) | copy-start | bytes 4718596
  849.6 16.1 %copy-start.49 = (f32[1536,1]{1,0:T(8,128)S(1)}, f32[1536,1]{1,0:T(8,128)}, u32[]{:S(2)}) copy-start(f32[1536,1]{1,0:T(8,128)} %copy-done.48) | copy-start | bytes 18436
  849.6 16.1 %copy-start.55 = (f32[2048]{0:T(1024)S(1)}, f32[2048]{0:T(1024)}, u32[]{:S(2)}) copy-start(f32[2048]{0:T(1024)} %copy-done.54) | copy-start | bytes 24580
  1056.8 75.3 %collective-permute-start.12 = (bf16[3,128,1408]{2,1,0:T(8,128)(2,1)}, bf16[3,128,1408]{2,1,0:T(8,128)(2,1)S(1)}, u32[]{:S(2)}, u32[]{:S(2)}) collective-permute-start(bf16[3,128,1408]{2,1,0:T(8,128)(2,1)} %get-tuple-element.220), channel_id=1, source_target_pairs={{0,1},{1,2},{2,3},{3,0},{4,5},{5,6},{6,7},{7,4},{8,9},{9,10},{10,1... | collective-permute-start | bytes 3244040 | tf_op jit(solution)/shard_map/ppermute | solution.py:1203
  1061.4 29.6 %copy-start.12 = (bf16[2048,512]{1,0:T(8,128)(2,1)S(1)}, bf16[2048,512]{1,0:T(8,128)(2,1)}, u32[]{:S(2)}) copy-start(bf16[2048,512]{1,0:T(8,128)(2,1)} %refs_3_.3) | copy-start | bytes 6291460
  1061.4 29.6 %copy-start.14 = (bf16[2048,512]{1,0:T(8,128)(2,1)S(1)}, bf16[2048,512]{1,0:T(8,128)(2,1)}, u32[]{:S(2)}) copy-start(bf16[2048,512]{1,0:T(8,128)(2,1)} %refs_4_.1) | copy-start | bytes 6291460
  1061.4 29.6 %copy-start.16 = (bf16[2048,512]{1,0:T(8,128)(2,1)S(1)}, bf16[2048,512]{1,0:T(8,128)(2,1)}, u32[]{:S(2)}) copy-start(bf16[2048,512]{1,0:T(8,128)(2,1)} %refs_5_.1) | copy-start | bytes 6291460
  1061.4 29.6 %copy-start.47 = (f32[1536,1]{1,0:T(8,128)S(1)}, f32[1536,1]{1,0:T(8,128)}, u32[]{:S(2)}) copy-start(f32[1536,1]{1,0:T(8,128)} %copy-done.46) | copy-start | bytes 18436
  1091.0 14.5 %copy-start.34 = (bf16[1536,512]{1,0:T(8,128)(2,1)S(1)}, bf16[1536,512]{1,0:T(8,128)(2,1)}, u32[]{:S(2)}) copy-start(bf16[1536,512]{1,0:T(8,128)(2,1)} %copy-done.33) | copy-start | bytes 4718596
  1126.0 39.6 %collective-permute-start.13 = (bf16[3,128,1408]{2,1,0:T(8,128)(2,1)}, bf16[3,128,1408]{2,1,0:T(8,128)(2,1)S(1)}, u32[]{:S(2)}, u32[]{:S(2)}) collective-permute-start(bf16[3,128,1408]{2,1,0:T(8,128)(2,1)} %get-tuple-element.219), channel_id=1, source_target_pairs={{0,2},{1,3},{2,0},{3,1},{4,6},{5,7},{6,4},{7,5},{8,10},{9,11},{10,... | collective-permute-start | bytes 3244040 | tf_op jit(solution)/shard_map/ppermute | solution.py:1203
  1128.8 37.0 %collective-permute-start.14 = (bf16[3,128,1408]{2,1,0:T(8,128)(2,1)}, bf16[3,128,1408]{2,1,0:T(8,128)(2,1)S(1)}, u32[]{:S(2)}, u32[]{:S(2)}) collective-permute-start(bf16[3,128,1408]{2,1,0:T(8,128)(2,1)} %get-tuple-element.218), channel_id=1, source_target_pairs={{0,3},{1,0},{2,1},{3,2},{4,7},{5,4},{6,5},{7,6},{8,11},{9,8},{10,9... | collective-permute-start | bytes 3244040 | tf_op jit(solution)/shard_map/ppermute | solution.py:1203
  1166.0 151.8 %copy-start.51 = (f32[2048]{0:T(1024)S(1)}, f32[2048]{0:T(1024)}, u32[]{:S(2)}) copy-start(f32[2048]{0:T(1024)} %copy-done.50) | copy-start | bytes 24580
  1166.0 151.8 %copy-start.58 = (bf16[384,2048]{1,0:T(8,128)(2,1)S(1)}, bf16[384,2048]{1,0:T(8,128)(2,1)}, u32[]{:S(2)}) copy-start(bf16[384,2048]{1,0:T(8,128)(2,1)} %refs_0_.1) | copy-start | bytes 4718596
  (61 other events, 269.5 us)
Sparse Core Ops, SparseCore 0:
  11.5 101.8 all-gather.7
  230.4 66.3 all-gather.9
  298.7 67.7 all-gather.11
  368.2 67.6 all-gather.13
  577.4 229.4 all-reduce.10
  810.5 210.5 reduce-scatter.1
  1126.1 181.5 all-reduce.8

commit v4 on v3

--- a/solution.py
+++ b/solution.py
@@ -1105,30 +1105,27 @@
     )(*grads, *weights, tokens, rates)
 
 
-def attend_grads_body(rows_ref, d_query, d_key, d_value, attended_ref, d_out_ref, *outs):
+def attend_grads_body(rows_ref, d_query, d_key, d_value, *outs):
     rows = rows_ref[...].T
     for d_ref, out in zip((d_query, d_key, d_value), outs):
         out[...] = matmul(rows, d_ref[...]).astype(jnp.bfloat16)
-    outs[3][...] = matmul(attended_ref[...].T, d_out_ref[...]).astype(jnp.bfloat16)
-
-
-def attend_grads(rows, d_pres, attended, d_out, cut):
+
+
+def attend_grads(rows, d_pres, cut):
     count, width = rows.shape
-    features = attended.shape[1]
-    by_cols = pl.BlockSpec((count, cut), lambda i: (0, i))
+    features = d_pres[0].shape[1]
     whole = pl.BlockSpec((count, features), lambda i: (0, 0))
     tall = pl.BlockSpec((cut, features), lambda i: (i, 0))
     return pl.pallas_call(
         attend_grads_body,
         grid=(width // cut,),
-        in_specs=[by_cols] + [whole] * 4 + [by_cols],
-        out_specs=[tall] * 3 + [pl.BlockSpec((features, cut), lambda i: (0, i))],
-        out_shape=[jax.ShapeDtypeStruct((width, features), jnp.bfloat16)] * 3
-        + [jax.ShapeDtypeStruct((features, width), jnp.bfloat16)],
+        in_specs=[pl.BlockSpec((count, cut), lambda i: (0, i))] + [whole] * 3,
+        out_specs=[tall] * 3,
+        out_shape=[jax.ShapeDtypeStruct((width, features), jnp.bfloat16)] * 3,
         compiler_params=pltpu.CompilerParams(vmem_limit_bytes=KERNEL_VMEM),
         cost_estimate=NO_COST,
         name="attend_grads",
-    )(rows, *d_pres, attended, d_out)
+    )(rows, *d_pres)
 
 
 def turn_body(piece_ref, out_ref):
@@ -1196,14 +1193,6 @@
     def after(value, other):
         return lax.optimization_barrier((value, other))[0]
 
-    def exchange(pieces):
-        result = pieces
-        for step in range(1, members):
-            sent = take(pieces, (member + step) % members)
-            came = lax.ppermute(sent, "fsdp", [(m, (m + step) % members) for m in range(members)])
-            result = put(result, came, (member - step) % members)
-        return result
-
     def one_hop(low, high, step):
         upward = [(m, m + 1) for m in range(step - 1, members - 1)]
         downward = [(members - 1 - m, members - 2 - m) for m in range(step - 1, members - 1)]
@@ -1396,7 +1385,7 @@
     )
     dh_low = collect(
         places,
-        after(d_in, (expert_grads, shared_sums, down_sum, block_sums)).reshape(by_block),
+        after(d_in, (expert_grads, shared_sums, down_sum)).reshape(by_block),
         dh_shared[0],
         members,
         d_small_both,
@@ -1414,7 +1403,9 @@
         members,
         2,
     )
+    d_attn_out, block_sums = lax.optimization_barrier((d_attn_out, block_sums))
     d_context = matmul_nt(d_attn_out, out_weight).astype(jnp.bfloat16)
+    out_sum = lax.psum(matmul_tn(attended, d_attn_out).astype(jnp.bfloat16), "expert")
     d_query_pre, d_key_pre, d_value_pre = attend_back(
         lows,
         starts,
@@ -1428,26 +1419,41 @@
         block,
     )
 
+    expert_pieces = expert_pieces.transpose(1, 0, 2, 3)
+
+    def cross(step, tie):
+        return lax.ppermute(
+            after(take(expert_pieces, (member + step) % members), tie),
+            "fsdp",
+            [(m, (m + step) % members) for m in range(members)],
+        )
+
+    arrived = [cross(step, d_attn_out) for step in range(1, members - 1)]
+    d_query_pre, arrived[0] = lax.optimization_barrier((d_query_pre, arrived[0]))
+    attn_grads = attend_grads(
+        normed_first, (d_query_pre, d_key_pre, d_value_pre), math.gcd(width, 512)
+    )
+    attn_grads, out_sum = lax.optimization_barrier((attn_grads, out_sum))
+    arrived.append(cross(members - 1, d_query_pre))
+    d_pres, arrived[1:-1] = after(
+        ((d_query_pre, d_key_pre, d_value_pre), arrived[1:-1]), attn_grads
+    )
     dh_first_low, norm1_part, *biases = unproject(
-        (d_query_pre, d_key_pre, d_value_pre),
-        (query_weight, key_weight, value_weight),
-        group_tokens,
-        rate_first,
-        block,
+        d_pres, (query_weight, key_weight, value_weight), group_tokens, rate_first, block
     )
     norm1_part = norm1_part[0]
-    attn_grads = attend_grads(
-        after(normed_first, dh_first_low),
-        (d_query_pre, d_key_pre, d_value_pre),
-        attended,
-        d_attn_out,
-        math.gcd(width, 512),
-    )
-    crossed_grads = exchange(after(expert_pieces, d_attn_out).transpose(1, 0, 2, 3))
+    crossed_grads = expert_pieces
+    for step, piece in enumerate(arrived, 1):
+        crossed_grads = put(crossed_grads, piece, (member - step) % members)
+
+    shared_sums, down_sum = after((shared_sums, down_sum), dh_first_low)
+    shared_out_grads = [
+        grad.astype(jnp.float32) for grad in (shared_sums[0], shared_sums[1], down_sum)
+    ]
     line_parts = jnp.concatenate([norm1_part, norm2_part, small_part.T.reshape(-1)])
     stats = jnp.concatenate([line_parts] + [bias[0] for bias in biases]).reshape(-1, 128)
     dh_first_own, stats, mixed_grads = scatter(
-        after(dh_first_low, attn_grads),
+        after(dh_first_low, (attn_grads, shared_out_grads)),
         jnp.pad(stats, ((0, -stats.shape[0] % 8), (0, 0))),
         crossed_grads,
         line_parts.shape[0] // 128,
@@ -1456,9 +1462,7 @@
         4,
         LONG_COST,
     )
-    shared_sums, down_sum, block_low, block_sums = after(
-        (shared_sums, down_sum, block_low, block_sums), dh_first_own
-    )
+    block_low, block_sums = after((block_low, block_sums), dh_first_own)
     stats = stats.reshape(-1)
     block_out = resid_own + own_rows(block_low).astype(jnp.float32)
     for came in block_sums:
@@ -1472,7 +1476,7 @@
     bias_end = line_parts.shape[0] + 3 * biases[0].shape[1]
     bias_sums = stats[line_parts.shape[0] : bias_end].reshape(3, -1)
 
-    attn_sums = after(lax.psum(attn_grads, "expert"), dh_first_own)
+    attn_sums = (*after(lax.psum(attn_grads, "expert"), dh_first_own), after(out_sum, dh_first_own))
     expert_sums = [mixed_grads[:, kind] for kind in range(3)]
 
     return (
@@ -1489,9 +1493,9 @@
         stats[width : 2 * width],
         small_sum[:experts_count].T,
         small_sum[experts_count],
-        shared_sums[0].astype(jnp.float32),
-        shared_sums[1].astype(jnp.float32),
-        down_sum.astype(jnp.float32),
+        shared_out_grads[0],
+        shared_out_grads[1],
+        shared_out_grads[2],
         expert_sums[0].reshape(1, width // members, -1).astype(jnp.float32),
         expert_sums[1].reshape(1, width // members, -1).astype(jnp.float32),
         turn(expert_sums[2])[None],

time: 1390 us -> 1360 us (0.978); the launches traced: 1370 us -> 1360 us
  waiting for transfers between devices: 58.1 us -> 25.2 us
  local copies, waits for them, and re-layouts: 90.7 us -> 110 us
    ppermute x3, waiting for transfers between devices: 33.4 us -> 0.01 us  [cross(): lax.ppermute(after(take(expert_pieces, (member + step) % members), tie),...]
    ppermute x3, waiting for transfers between devices: 15.8 us -> 0.01 us  [relay(): lax.ppermute(down_block, 'fsdp', down_pairs)]
    psum x1 -> x2, waiting for transfers between devices: 0.01 us -> 14.7 us  [the longest x1 14.7 us: shards(): lax.psum(matmul_tn(attended, d_attn_out).astype(jnp.bfloat16), 'expert')]
  transfers between devices with their start and end apart: 22 -> 23, of which waited for: 4 -> 2; matrix products, arithmetic and copies ran while one was open for 7% -> 11% of each run, Pallas kernels for 79% -> 79%
where the time goes in v4:
time: 1360 us
  Pallas kernels  1070 us (79%)
  local copies, waits for them, and re-layouts  110 us (8%)
  other arithmetic  75.6 us (6%)
  starting transfers between devices  37 us (3%)
  matrix products  28.7 us (2%)
  waiting for transfers between devices  25.2 us (2%)
  between operations  15.9 us (1%)
    pallas_call x1, Pallas kernels, arrive(): pl.pallas_call(functools.partial(arrive_body, members, local_experts, pie...  218 us
    pallas_call x1, Pallas kernels, turnaround(): pl.pallas_call(functools.partial(turnaround_body, pieces), in_specs=[in_v...  184 us
    pallas_call x1, Pallas kernels, scatter(): pl.pallas_call(functools.partial(scatter_body, pieces, columns, line_rows...  143 us
    pallas_call x2, Pallas kernels, expert_back(): pl.pallas_call(functools.partial(expert_back_body, turned), grid=(experts...  104 us
    pallas_call x1, Pallas kernels, gather(): pl.pallas_call(functools.partial(gather_body, pieces), in_specs=[pl.Block...  103 us
    pallas_call x2, Pallas kernels, expert(): pl.pallas_call(functools.partial(expert_body, turned), grid=(experts, cou...  97.2 us
    unnamed x188, local copies, waits for them, and re-layouts  69.3 us
    pallas_call x1, Pallas kernels, weight_grads(): pl.pallas_call(weight_grads_body, grid=(experts, members), in_specs=[by_c...  45.6 us
  transfers between devices with their start and end apart: 23, of which 2 were waited for; matrix products, arithmetic and copies ran while one was open for 11% of the time, Pallas kernels for 79%

profile of v4, /device:TPU:0, one launch (start us, length us, event | category | flops | bytes accessed | tf_op | source)
XLA Modules:
  0.0 1359.2 jit_solution(8465137316478272408)
XLA Ops:
  12.1 218.1 %arrive.1 = (bf16[4,384,2048]{2,1,0:T(8,128)(2,1)}, s32[4,4,384]{2,1,0:T(4,128)}, bf16[4,128,1408]{2,1,0:T(8,128)(2,1)}, bf16[4,128,1408]{2,1,0:T(8,128)(2,1)}, ...) custom-call(bf16[384,2048]{1,0:T(8,128)(2,1)} %refs_0_.1, ...), custom_call_target="tpu_custom_call" | custom-call | tf_op jit(solution)/shard_map/arrive/pallas_call | solution.py:735
  233.0 5.7 collective-permute-start
  239.2 2.8 fusion.18
  242.6 14.1 %project.1 = (bf16[1536,2048]{1,0:T(8,128)(2,1)}, f32[1536,1]{1,0:T(8,128)S(1)}, bf16[1536,512]{1,0:T(8,128)(2,1)S(1)}, bf16[1536,512]{1,0:T(8,128)(2,1)S(1)}, bf16[1536,512]{1,0:T(8,128)(2,1)S(1)}) custom-call(bf16[1536,2048]{1,0:T(8,128)(2,1)} %bitcast.164, f32[1,2048]{1,0:T(1,128)S(1)} %bitcast.140, bf16[2048,512]{1,0:T(8,128)(2,1)S(1)} %copy-done.11, ...), custom_call_target="tpu_custom_call" | custom-call | tf_op jit(solution)/shard_map/project/pallas_call | solution.py:117
  256.9 20.6 %attend.1 = (bf16[1536,512]{1,0:T(8,128)(2,1)S(1)}, f32[4,1,1536]{2,1,0:T(1,128)S(1)}) custom-call(s32[6]{0:T(128)S(1)} %and_select_fusion.lows_ref, s32[1,1536]{1,0:T(1,128)S(1)} %subtract_subtract_fusion.starts_ref, bf16[1536,512]{1,0:T(8,128)(2,1)S(1)} %get-tuple-element.122.query_ref, bf16[1536,512]{1,0:T(8,128)(2,1)S(1)} %get-tuple-element.123.key_ref, ...), custom_call_target="tpu_custom_call" | custom-call | tf_op jit(solution)/shard_map/attend/pallas_call | solution.py:175
  279.8 103.5 %gather.1.attended_ref = bf16[4,1536,512]{2,1,0:T(8,128)(2,1)} custom-call(bf16[1536,512]{1,0:T(8,128)(2,1)} %copy-done.47), custom_call_target="tpu_custom_call" | custom-call | tf_op jit(solution)/shard_map/gather/pallas_call | solution.py:777
  387.1 22.2 %settle.1 = (f32[1536,2048]{1,0:T(8,128)}, f32[1536,1]{1,0:T(8,128)S(1)}, bf16[1536,2048]{1,0:T(8,128)(2,1)S(1)}, f32[1536,128]{1,0:T(8,128)S(1)}) custom-call(bf16[1536,2048]{1,0:T(8,128)(2,1)} %bitcast.165, bf16[4,1536,512]{2,1,0:T(8,128)(2,1)} %gather.1.attended_ref, bf16[2048,2048]{1,0:T(8,128)(2,1)} %all-gather.8.cloned.1.call-done.weight_ref, ...), custom_call_target="tpu_custom_call" | custom-call | flops 12884901888 | bytes 37748736 | tf_op jit(solution)/shard_map/settle/pallas_call | solution.py:304
  412.8 9.0 collective-permute-done.3
  426.5 38.9 %expert.2 = (f32[1,1536,2048]{2,1,0:T(8,128)}, bf16[1,1536,1408]{2,1,0:T(8,128)(2,1)}, f32[1,1536,1408]{2,1,0:T(8,128)}, f32[1,1536,1408]{2,1,0:T(8,128)}) custom-call(bf16[1,1536,2048]{2,1,0:T(8,128)(2,1)} %bitcast.126, f32[1,1536,1]{2,1,0:T(8,128)} %bitcast.132, bf16[1,2048,1408]{2,1,0:T(8,128)(2,1)} %bitcast.167, bf16[1,2048,1408]{2,1,0:T(8,128)(2,1)} %bitcast.169, ...), custom_call_target="tpu_custom_call" | custom-call | tf_op jit(solution)/shard_map/expert/pallas_call | solution.py:458
  465.4 2.8 copy-done.3
  468.2 6.5 dispatch.2
  474.7 2.7 constant_dynamic-update-slice_fusion.8
  477.4 2.8 constant_dynamic-update-slice_fusion.7
  489.7 2.9 constant_dynamic-update-slice_fusion.2
  492.6 3.4 constant_dynamic-slice_fusion.1.source_ref
  496.0 11.4 convolution_convert_fusion
  507.4 42.9 %expert_back.2 = (f32[1,1536,1]{2,1,0:T(8,128)}, bf16[1,1536,2048]{2,1,0:T(8,128)(2,1)}, bf16[1,1536,1408]{2,1,0:T(8,128)(2,1)}, bf16[1,1536,1408]{2,1,0:T(8,128)(2,1)}, f32[1,1536,2048]{2,1,0:T(8,128)}) custom-call(bf16[1,1536,2048]{2,1,0:T(8,128)(2,1)} %bitcast.127, f32[1,1536,2048]{2,1,0:T(8,128)} %get-tuple-element.143.result_ref, ...), custom_call_target="tpu_custom_call" | custom-call | tf_op jit(solution)/shard_map/expert_back/pallas_call | solution.py:491
  554.7 22.8 %pair_grads.1 = (bf16[2048,1408]{1,0:T(8,128)(2,1)S(1)}, bf16[2048,1408]{1,0:T(8,128)(2,1)}) custom-call(bf16[1536,2048]{1,0:T(8,128)(2,1)} %copy-done.2, bf16[1536,1408]{1,0:T(8,128)(2,1)S(1)} %bitcast.136, bf16[1536,1408]{1,0:T(8,128)(2,1)S(1)} %bitcast.137), custom_call_target="tpu_custom_call" | custom-call | tf_op jit(solution)/shard_map/pair_grads/pallas_call | solution.py:546
  585.7 58.3 %expert.3 = (bf16[2,1024,2048]{2,1,0:T(8,128)(2,1)}, bf16[2,1024,1408]{2,1,0:T(8,128)(2,1)}, f32[2,1024,1408]{2,1,0:T(8,128)}, f32[2,1024,1408]{2,1,0:T(8,128)}, bf16[2,1024,2048]{2,1,0:T(8,128)(2,1)}) custom-call(bf16[2,1024,2048]{2,1,0:T(8,128)(2,1)} %bitcast.154, f32[2,1024,1]{2,1,0:T(8,128)} %copy.104.scale_ref, bf16[2,2048,1408]{2,1,0:T(8,128)(2,1)} %bitcast.157, ...), custom_call_target="tpu_custom_call" | custom-call | tf_op jit(solution)/shard_map/expert/pallas_call | solution.py:458
  644.0 9.4 collect.2
  658.8 6.3 collective-permute-start.6
  665.2 2.8 copy-done.5
  668.0 6.5 dispatch.3
  674.5 61.2 %expert_back.3 = (f32[2,1024,1]{2,1,0:T(8,128)}, bf16[2,1024,2048]{2,1,0:T(8,128)(2,1)}, bf16[2,1024,1408]{2,1,0:T(8,128)(2,1)}, bf16[2,1024,1408]{2,1,0:T(8,128)(2,1)}, bf16[2,1024,2048]{2,1,0:T(8,128)(2,1)}) custom-call(bf16[2,1024,2048]{2,1,0:T(8,128)(2,1)} %bitcast.163, bf16[2,1024,2048]{2,1,0:T(8,128)(2,1)} %get-tuple-element.156.result_ref, ...), custom_call_target="tpu_custom_call" | custom-call | tf_op jit(solution)/shard_map/expert_back/pallas_call | solution.py:491
  735.6 5.1 fusion.7
  745.1 2.8 copy-done.39
  747.9 45.6 %weight_grads.1 = bf16[2,4,3,512,1408]{4,3,2,1,0:T(8,128)(2,1)} custom-call(bf16[2,1024,2048]{2,1,0:T(8,128)(2,1)} %bitcast.155, bf16[2,1024,2048]{2,1,0:T(8,128)(2,1)} %get-tuple-element.164.d_out_ref, bf16[2,1024,1408]{2,1,0:T(8,128)(2,1)S(1)} %copy-done.38, bf16[2,1024,1408]{2,1,0:T(8,128)(2,1)S(1)} %copy-done.39, ...), custom_call_target="tpu_custom_call" | custom-call | tf_op jit(solution)/shard_map/weight_grads/pallas_call | solution.py:523
  811.1 6.1 fusion.5
  818.5 5.7 collective-permute-start.10
  826.7 6.1 fusion.26
  833.9 13.8 %collect.3 = bf16[1536,2048]{1,0:T(8,128)(2,1)S(1)} custom-call(s32[1536,2]{1,0:T(8,128)S(1)} %bitcast.135, bf16[2,4,256,2048]{3,2,1,0:T(8,128)(2,1)} %bitcast.179, f32[1536,2048]{1,0:T(8,128)} %bitcast.177, bf16[1536,128]{1,0:T(8,128)(2,1)S(1)} %copy-done.46, bf16[128,2048]{1,0:T(8,128)(2,1)S(1)} %fusion.17.rest_1_), custom_call_target="tpu_custom_call" | custom-call | tf_op jit(solution)/shard_map/collect/pallas_call | solution.py:406
  847.7 3.4 copy-done.7
  851.1 184.2 %turnaround.1 = (f32[384,2048]{1,0:T(8,128)S(1)}, f32[1,2048]{1,0:T(1,128)S(1)}, bf16[4,384,2048]{2,1,0:T(8,128)(2,1)S(1)}) custom-call(bf16[4,384,2048]{2,1,0:T(8,128)(2,1)} %bitcast.131, f32[1536,2048]{1,0:T(8,128)} %get-tuple-element.128.refs_1_, f32[1536,1]{1,0:T(8,128)S(1)} %copy-done.52, bf16[384,2048]{1,0:T(8,128)(2,1)S(1)} %copy-done.24, ...), custom_call_target="tpu_custom_call" | custom-call | tf_op jit(solution)/shard_map/turnaround/pallas_call | solution.py:1035
  1039.7 4.6 convolution_convert_fusion.1
  1044.4 3.7 dynamic-slice_bitcast_fusion.2
  1049.5 6.4 convolution_convert_fusion.2.grad_ref
  1056.0 26.2 %attend_back.1 = (bf16[1536,512]{1,0:T(8,128)(2,1)S(1)}, bf16[1536,512]{1,0:T(8,128)(2,1)S(1)}, bf16[1536,512]{1,0:T(8,128)(2,1)S(1)}) custom-call(s32[6]{0:T(128)S(1)} %copy-done.60, s32[1,1536]{1,0:T(1,128)S(1)} %copy-done.56, bf16[1536,512]{1,0:T(8,128)(2,1)S(1)} %copy-done.26, bf16[1536,512]{1,0:T(8,128)(2,1)S(1)} %copy-done.28, ...), custom_call_target="tpu_custom_call" | custom-call | tf_op jit(solution)/shard_map/attend_back/pallas_call | solution.py:251
  1085.8 12.9 attend_grads.1
  1098.6 14.7 %all-reduce.10.cloned.1.call-done = bf16[512,2048]{1,0:T(8,128)(2,1)} async-done(((bf16[512,2048]{1,0:T(8,128)(2,1)}), bf16[512,2048]{1,0:T(8,128)(2,1)}) %all-reduce.10.cloned.1.call-update) | async-done | bytes 2097168 | tf_op jit(solution)/shard_map/psum | solution.py:1408
  1113.4 3.5 collective-permute-start.14
  1125.9 14.4 %unproject.1 = (bf16[1536,2048]{1,0:T(8,128)(2,1)}, f32[1,2048]{1,0:T(1,128)S(1)}, f32[1,512]{1,0:T(1,128)S(1)}, f32[1,512]{1,0:T(1,128)S(1)}, f32[1,512]{1,0:T(1,128)S(1)}) custom-call(bf16[1536,512]{1,0:T(8,128)(2,1)S(1)} %copy-done.32, bf16[1536,512]{1,0:T(8,128)(2,1)S(1)} %copy-done.34, bf16[1536,512]{1,0:T(8,128)(2,1)S(1)} %copy-done.36, ...), custom_call_target="tpu_custom_call" | custom-call | tf_op jit(solution)/shard_map/unproject/pallas_call | solution.py:1090
  1140.3 8.0 convert_element_type.200
  1148.3 7.9 convert_element_type.201
  1156.2 6.0 convert_element_type.202
  1171.5 142.9 %scatter.1 = (f32[384,2048]{1,0:T(8,128)S(1)}, f32[192,128]{1,0:T(8,128)S(1)}, bf16[4,3,128,1408]{3,2,1,0:T(8,128)(2,1)S(1)}) custom-call(bf16[4,384,2048]{2,1,0:T(8,128)(2,1)} %bitcast.201, f32[192,128]{1,0:T(8,128)S(1)} %pad.19.stats_ref, bf16[4,3,128,1408]{3,2,1,0:T(8,128)(2,1)S(1)} %copy-done.43), custom_call_target="tpu_custom_call" | custom-call | flops 99999997952 | tf_op jit(solution)/shard_map/scatter/pallas_call | solution.py:958
  1334.0 5.7 add_convert_fusion
  1342.2 4.3 convert_element_type.208
  1346.6 2.7 convert_element_type.209
  (310 shorter events, 128.9 us)
Async XLA Ops:
  7.2 379.9 %all-gather.8.cloned.1.call-start = ((), (), s32[]{:S(2)}) async-start(), calls=%async_computation.1 | async-start | bytes 8650752 | tf_op jit(solution)/shard_map/all_gather | solution.py:1246
  9.5 576.2 %all-gather.10.cloned.1.call-start = ((), (), s32[]{:S(2)}) async-start(), calls=%async_computation.4 | async-start | bytes 12976128 | tf_op jit(solution)/shard_map/all_gather | solution.py:1234
  230.3 355.4 %all-gather.12.cloned.1.call-start = ((), (), s32[]{:S(2)}) async-start(), calls=%async_computation.5 | async-start | bytes 12976128 | tf_op jit(solution)/shard_map/all_gather | solution.py:1234
  231.0 354.7 %all-gather.14.cloned.1.call-start = ((), (), s32[]{:S(2)}) async-start(), calls=%async_computation.6 | async-start | bytes 12976128 | tf_op jit(solution)/shard_map/all_gather | solution.py:1234
  231.6 601.1 %all-reduce.14.cloned.1.call-start = ((), (), s32[]{:S(2)}) async-start(), calls=%async_computation.8 | async-start | bytes 34603008 | tf_op jit(solution)/shard_map/psum | solution.py:1331
  231.7 48.1 %collective-permute-start.1 = (bf16[384,2048]{1,0:T(8,128)(2,1)}, bf16[384,2048]{1,0:T(8,128)(2,1)}, u32[]{:S(2)}, u32[]{:S(2)}) collective-permute-start(bf16[384,2048]{1,0:T(8,128)(2,1)} %refs_3_.2), channel_id=1, source_target_pairs={{3,2},{2,1},{1,0},{7,6},{6,5},{5,4},{11,10},{10,9},{9,8},{15,14},{... | collective-permute-start | bytes 4718600 | tf_op jit(solution)/shard_map/ppermute | solution.py:1199
  233.0 46.8 %collective-permute-start = (bf16[384,2048]{1,0:T(8,128)(2,1)}, bf16[384,2048]{1,0:T(8,128)(2,1)}, u32[]{:S(2)}, u32[]{:S(2)}) collective-permute-start(bf16[384,2048]{1,0:T(8,128)(2,1)} %refs_3_.2), channel_id=1, source_target_pairs={{0,1},{1,2},{2,3},{4,5},{5,6},{6,7},{8,9},{9,10},{10,11},{12,13},{... | collective-permute-start | bytes 4718600 | tf_op jit(solution)/shard_map/ppermute | solution.py:1199
  239.0 148.1 %copy-start.57 = (f32[2048]{0:T(1024)}, f32[2048]{0:T(1024)S(1)}, u32[]{:S(2)}) copy-start(f32[2048]{0:T(1024)S(1)} %broadcast_in_dim.174) | copy-start | bytes 24580
  242.5 14.2 %copy-start.19 = (f32[1536,128]{1,0:T(8,128)}, f32[1536,128]{1,0:T(8,128)S(1)}, u32[]{:S(2)}) copy-start(f32[1536,128]{1,0:T(8,128)S(1)} %get-tuple-element.259.c.rest_0_) | copy-start | bytes 2359300
  242.5 14.2 %copy-start.21 = (f32[1536,128]{1,0:T(8,128)}, f32[1536,128]{1,0:T(8,128)S(1)}, u32[]{:S(2)}) copy-start(f32[1536,128]{1,0:T(8,128)S(1)} %get-tuple-element.260.s.rest_1_) | copy-start | bytes 2359300
  256.8 20.7 %copy-start.27 = (bf16[1536,512]{1,0:T(8,128)(2,1)}, bf16[1536,512]{1,0:T(8,128)(2,1)S(1)}, u32[]{:S(2)}) copy-start(bf16[1536,512]{1,0:T(8,128)(2,1)S(1)} %get-tuple-element.123.key_ref) | copy-start | bytes 4718596
  256.8 23.0 %copy-start.29 = (bf16[1536,512]{1,0:T(8,128)(2,1)}, bf16[1536,512]{1,0:T(8,128)(2,1)S(1)}, u32[]{:S(2)}) copy-start(bf16[1536,512]{1,0:T(8,128)(2,1)S(1)} %get-tuple-element.124.value_ref) | copy-start | bytes 4718596
  256.8 23.0 %copy-start.49 = (f32[1536,1]{1,0:T(8,128)}, f32[1536,1]{1,0:T(8,128)S(1)}, u32[]{:S(2)}) copy-start(f32[1536,1]{1,0:T(8,128)S(1)} %get-tuple-element.197.refs_7_) | copy-start | bytes 18436
  256.8 126.5 %copy-start.59 = (s32[6]{0:T(128)}, s32[6]{0:T(128)S(1)}, u32[]{:S(2)}) copy-start(s32[6]{0:T(128)S(1)} %and_select_fusion.lows_ref) | copy-start | bytes 76
  256.8 22.9 %copy-start.55 = (s32[1,1536]{1,0:T(1,128)}, s32[1,1536]{1,0:T(1,128)S(1)}, u32[]{:S(2)}) copy-start(s32[1,1536]{1,0:T(1,128)S(1)} %subtract_subtract_fusion.starts_ref) | copy-start | bytes 18436
  279.8 106.8 %copy-start.70 = (bf16[2048,8]{0,1:T(8,128)(2,1)S(1)}, bf16[2048,8]{0,1:T(8,128)(2,1)}, u32[]{:S(2)}) copy-start(bf16[2048,8]{0,1:T(8,128)(2,1)} %param.34) | copy-start | bytes 98308
  279.8 106.8 %copy-start.76 = (bf16[2048]{0:T(1024)(128)(2,1)S(1)}, bf16[2048]{0:T(1024)(128)(2,1)}, u32[]{:S(2)}) copy-start(bf16[2048]{0:T(1024)(128)(2,1)} %param.35) | copy-start | bytes 12292
  383.3 29.5 %collective-permute-start.2 = (bf16[384,2048]{1,0:T(8,128)(2,1)}, bf16[384,2048]{1,0:T(8,128)(2,1)}, u32[]{:S(2)}, u32[]{:S(2)}) collective-permute-start(bf16[384,2048]{1,0:T(8,128)(2,1)} %collective-permute-done), channel_id=1, source_target_pairs={{1,2},{2,3},{5,6},{6,7},{9,10},{10,11},{13,14},{14,15},{17,18},{18... | collective-permute-start | bytes 4718600 | tf_op jit(solution)/shard_map/ppermute | solution.py:1199
  385.1 36.7 %collective-permute-start.3 = (bf16[384,2048]{1,0:T(8,128)(2,1)}, bf16[384,2048]{1,0:T(8,128)(2,1)}, u32[]{:S(2)}, u32[]{:S(2)}) collective-permute-start(bf16[384,2048]{1,0:T(8,128)(2,1)} %collective-permute-done.1), channel_id=1, source_target_pairs={{2,1},{1,0},{6,5},{5,4},{10,9},{9,8},{14,13},{13,12},{18,17},{17,1... | collective-permute-start | bytes 4718600 | tf_op jit(solution)/shard_map/ppermute | solution.py:1199
  387.1 37.8 %copy-start.71 = (s32[4,4,384]{2,1,0:T(4,128)S(1)}, s32[4,4,384]{2,1,0:T(4,128)}, u32[]{:S(2)}) copy-start(s32[4,4,384]{2,1,0:T(4,128)} %get-tuple-element.129) | copy-start | bytes 73732
  421.8 52.8 %collective-permute-start.4 = (bf16[384,2048]{1,0:T(8,128)(2,1)}, bf16[384,2048]{1,0:T(8,128)(2,1)}, u32[]{:S(2)}, u32[]{:S(2)}) collective-permute-start(bf16[384,2048]{1,0:T(8,128)(2,1)} %collective-permute-done.2), channel_id=1, source_target_pairs={{2,3},{6,7},{10,11},{14,15},{18,19},{22,23},{26,27},{30,31}} | collective-permute-start | bytes 4718600 | tf_op jit(solution)/shard_map/ppermute | solution.py:1199
  423.7 51.0 %collective-permute-start.5 = (bf16[384,2048]{1,0:T(8,128)(2,1)}, bf16[384,2048]{1,0:T(8,128)(2,1)}, u32[]{:S(2)}, u32[]{:S(2)}) collective-permute-start(bf16[384,2048]{1,0:T(8,128)(2,1)} %collective-permute-done.3), channel_id=1, source_target_pairs={{1,0},{5,4},{9,8},{13,12},{17,16},{21,20},{25,24},{29,28}} | collective-permute-start | bytes 4718600 | tf_op jit(solution)/shard_map/ppermute | solution.py:1199
  496.0 11.4 copy-start.4
  580.0 464.4 %reduce-scatter.2.cloned.1.call-start = ((), (), s32[]{:S(2)}) async-start(), calls=%async_computation.2 | async-start | bytes 38928384 | tf_op jit(solution)/shard_map/reduce_scatter | solution.py:1360
  585.7 58.3 %copy-start.8 = (f32[1536,1]{1,0:T(8,128)S(1)}, f32[1536,1]{1,0:T(8,128)}, u32[]{:S(2)}) copy-start(f32[1536,1]{1,0:T(8,128)} %get-tuple-element.234.rest_0_) | copy-start | bytes 18436
  585.7 58.3 %copy-start.17 = (s32[4,384,2]{2,1,0:T(8,128)S(1)}, s32[4,384,2]{2,1,0:T(8,128)}, u32[]{:S(2)}) copy-start(s32[4,384,2]{2,1,0:T(8,128)} %copy.100) | copy-start | bytes 36868
  657.0 78.6 %collective-permute-start.7 = (bf16[384,2048]{1,0:T(8,128)(2,1)}, bf16[384,2048]{1,0:T(8,128)(2,1)}, u32[]{:S(2)}, u32[]{:S(2)}) collective-permute-start(bf16[384,2048]{1,0:T(8,128)(2,1)} %get-tuple-element.239), channel_id=1, source_target_pairs={{3,2},{7,6},{11,10},{15,14},{19,18},{23,22},{27,26},{31,30}} | collective-permute-start | bytes 4718600 | tf_op jit(solution)/shard_map/ppermute | solution.py:1228
  658.8 76.8 %collective-permute-start.6 = (bf16[384,2048]{1,0:T(8,128)(2,1)}, bf16[384,2048]{1,0:T(8,128)(2,1)}, u32[]{:S(2)}, u32[]{:S(2)}) collective-permute-start(bf16[384,2048]{1,0:T(8,128)(2,1)} %get-tuple-element.240), channel_id=1, source_target_pairs={{0,1},{4,5},{8,9},{12,13},{16,17},{20,21},{24,25},{28,29}} | collective-permute-start | bytes 4718600 | tf_op jit(solution)/shard_map/ppermute | solution.py:1227
  735.6 9.5 copy-start.38
  740.8 52.6 %collective-permute-start.9 = (bf16[384,2048]{1,0:T(8,128)(2,1)S(1)}, bf16[384,2048]{1,0:T(8,128)(2,1)}, u32[]{:S(2)}, u32[]{:S(2)}) collective-permute-start(bf16[384,2048]{1,0:T(8,128)(2,1)S(1)} %get-tuple-element.237), channel_id=1, source_target_pairs={{3,2},{2,1},{7,6},{6,5},{11,10},{10,9},{15,14},{14,13},{19,18},{18... | collective-permute-start | bytes 4718600 | tf_op jit(solution)/shard_map/ppermute | solution.py:1228
  742.6 50.8 %collective-permute-start.8 = (bf16[384,2048]{1,0:T(8,128)(2,1)S(1)}, bf16[384,2048]{1,0:T(8,128)(2,1)}, u32[]{:S(2)}, u32[]{:S(2)}) collective-permute-start(bf16[384,2048]{1,0:T(8,128)(2,1)S(1)} %get-tuple-element.238), channel_id=1, source_target_pairs={{0,1},{1,2},{4,5},{5,6},{8,9},{9,10},{12,13},{13,14},{16,17},{17,1... | collective-permute-start | bytes 4718600 | tf_op jit(solution)/shard_map/ppermute | solution.py:1227
  793.5 319.9 %all-reduce.10.cloned.1.call-start = ((), (), s32[]{:S(2)}) async-start(), calls=%async_computation.3 | async-start | bytes 4194304 | tf_op jit(solution)/shard_map/psum | solution.py:1408
  811.1 13.2 copy-start.64
  811.1 13.7 %copy-start.69 = (f32[1536,8]{0,1:T(8,128)S(1)}, f32[1536,8]{0,1:T(8,128)}, u32[]{:S(2)}) copy-start(f32[1536,8]{0,1:T(8,128)} %copy.108) | copy-start | bytes 147460
  817.2 219.8 %collective-permute-start.11 = (bf16[384,2048]{1,0:T(8,128)(2,1)}, bf16[384,2048]{1,0:T(8,128)(2,1)}, u32[]{:S(2)}, u32[]{:S(2)}) collective-permute-start(bf16[384,2048]{1,0:T(8,128)(2,1)} %get-tuple-element.235), channel_id=1, source_target_pairs={{3,2},{2,1},{1,0},{7,6},{6,5},{5,4},{11,10},{10,9},{9,8},{15,14},{... | collective-permute-start | bytes 4718600 | tf_op jit(solution)/shard_map/ppermute | solution.py:1228
  818.5 218.5 %collective-permute-start.10 = (bf16[384,2048]{1,0:T(8,128)(2,1)}, bf16[384,2048]{1,0:T(8,128)(2,1)}, u32[]{:S(2)}, u32[]{:S(2)}) collective-permute-start(bf16[384,2048]{1,0:T(8,128)(2,1)} %get-tuple-element.236), channel_id=1, source_target_pairs={{0,1},{1,2},{2,3},{4,5},{5,6},{6,7},{8,9},{9,10},{10,11},{12,13},{... | collective-permute-start | bytes 4718600 | tf_op jit(solution)/shard_map/ppermute | solution.py:1227
  833.9 17.2 %copy-start.24 = (bf16[384,2048]{1,0:T(8,128)(2,1)S(1)}, bf16[384,2048]{1,0:T(8,128)(2,1)}, u32[]{:S(2)}) copy-start(bf16[384,2048]{1,0:T(8,128)(2,1)} %refs_3_.2) | copy-start | bytes 4718596
  833.9 17.2 %copy-start.52 = (f32[1536,1]{1,0:T(8,128)S(1)}, f32[1536,1]{1,0:T(8,128)}, u32[]{:S(2)}) copy-start(f32[1536,1]{1,0:T(8,128)} %copy-done.51) | copy-start | bytes 18436
  833.9 17.2 %copy-start.58 = (f32[2048]{0:T(1024)S(1)}, f32[2048]{0:T(1024)}, u32[]{:S(2)}) copy-start(f32[2048]{0:T(1024)} %copy-done.57) | copy-start | bytes 24580
  851.1 188.6 %copy-start.48 = (bf16[1536,512]{1,0:T(8,128)(2,1)S(1)}, bf16[1536,512]{1,0:T(8,128)(2,1)}, u32[]{:S(2)}) copy-start(bf16[1536,512]{1,0:T(8,128)(2,1)} %copy-done.47) | copy-start | bytes 4718596
  1044.3 297.9 %all-reduce.12.cloned.1.call-start = ((), (), s32[]{:S(2)}) async-start(), calls=%async_computation.7 | async-start | bytes 12582912 | tf_op jit(solution)/shard_map/psum | solution.py:1479
  1048.1 36.9 %collective-permute-start.12 = (bf16[3,128,1408]{2,1,0:T(8,128)(2,1)}, bf16[3,128,1408]{2,1,0:T(8,128)(2,1)}, u32[]{:S(2)}, u32[]{:S(2)}) collective-permute-start(bf16[3,128,1408]{2,1,0:T(8,128)(2,1)} %get-tuple-element.182), channel_id=1, source_target_pairs={{0,1},{1,2},{2,3},{3,0},{4,5},{5,6},{6,7},{7,4},{8,9},{9,10},{10,1... | collective-permute-start | bytes 3244040 | tf_op jit(solution)/shard_map/ppermute | solution.py:1425
  1048.3 68.6 %collective-permute-start.13 = (bf16[3,128,1408]{2,1,0:T(8,128)(2,1)}, bf16[3,128,1408]{2,1,0:T(8,128)(2,1)}, u32[]{:S(2)}, u32[]{:S(2)}) collective-permute-start(bf16[3,128,1408]{2,1,0:T(8,128)(2,1)} %get-tuple-element.186), channel_id=1, source_target_pairs={{0,2},{1,3},{2,0},{3,1},{4,6},{5,7},{6,4},{7,5},{8,10},{9,11},{10,... | collective-permute-start | bytes 3244040 | tf_op jit(solution)/shard_map/ppermute | solution.py:1425
  1048.3 33.9 %slice-start = ((s8[4325376]{0:T(1024)(128)(4,1)}), s8[131072]{0:T(1024)(128)(4,1)S(1)}, s32[]{:S(2)}) async-start(s8[4325376]{0:T(1024)(128)(4,1)} %bitcast.174), calls=%async_computation.9 | async-start | bytes 262144
  1049.5 32.7 %slice-start.1 = ((s8[4325376]{0:T(1024)(128)(4,1)}), s8[4194304]{0:T(1024)(128)(4,1)S(1)}, s32[]{:S(2)}) async-start(s8[4325376]{0:T(1024)(128)(4,1)} %bitcast.174), calls=%async_computation.10 | async-start | bytes 8388608
  1085.8 31.2 %copy-start.50 = (f32[1536,1]{1,0:T(8,128)S(1)}, f32[1536,1]{1,0:T(8,128)}, u32[]{:S(2)}) copy-start(f32[1536,1]{1,0:T(8,128)} %copy-done.49) | copy-start | bytes 18436
  1113.4 53.6 %collective-permute-start.14 = (bf16[3,128,1408]{2,1,0:T(8,128)(2,1)}, bf16[3,128,1408]{2,1,0:T(8,128)(2,1)}, u32[]{:S(2)}, u32[]{:S(2)}) collective-permute-start(bf16[3,128,1408]{2,1,0:T(8,128)(2,1)} %get-tuple-element.210), channel_id=1, source_target_pairs={{0,3},{1,0},{2,1},{3,2},{4,7},{5,4},{6,5},{7,6},{8,11},{9,8},{10,9... | collective-permute-start | bytes 3244040 | tf_op jit(solution)/shard_map/ppermute | solution.py:1425
  1140.3 15.9 %slice-start.2 = ((s8[5767168]{0:T(1024)(128)(4,1)}), s8[4194304]{0:T(1024)(128)(4,1)S(1)}, s32[]{:S(2)}) async-start(s8[5767168]{0:T(1024)(128)(4,1)} %bitcast.181), calls=%async_computation.11 | async-start | bytes 8388608
  (62 other events, 244.3 us)
Sparse Core Ops, SparseCore 0:
  11.5 101.8 all-gather.7
  230.4 66.3 all-gather.9
  298.8 67.7 all-gather.11
  368.3 67.6 all-gather.13
  580.1 228.0 all-reduce.13
  811.7 210.5 reduce-scatter.1
  1044.5 68.8 all-reduce.9
  1162.4 172.4 all-reduce.11

commit v5 on v4

--- a/solution.py
+++ b/solution.py
@@ -1446,14 +1446,21 @@
     for step, piece in enumerate(arrived, 1):
         crossed_grads = put(crossed_grads, piece, (member - step) % members)
 
-    shared_sums, down_sum = after((shared_sums, down_sum), dh_first_low)
+    shared_sums, down_sum, out_sum, block_low, block_sums = after(
+        (shared_sums, down_sum, out_sum, block_low, block_sums), dh_first_low
+    )
+    out_grad = out_sum.astype(jnp.float32)
+    block_out = resid_own + own_rows(block_low).astype(jnp.float32)
+    for came in block_sums:
+        block_out = block_out + came.astype(jnp.float32)
+    block_out = block_out.astype(jnp.bfloat16)
     shared_out_grads = [
         grad.astype(jnp.float32) for grad in (shared_sums[0], shared_sums[1], down_sum)
     ]
     line_parts = jnp.concatenate([norm1_part, norm2_part, small_part.T.reshape(-1)])
     stats = jnp.concatenate([line_parts] + [bias[0] for bias in biases]).reshape(-1, 128)
     dh_first_own, stats, mixed_grads = scatter(
-        after(dh_first_low, (attn_grads, shared_out_grads)),
+        after(dh_first_low, (attn_grads, shared_out_grads, out_grad, block_out)),
         jnp.pad(stats, ((0, -stats.shape[0] % 8), (0, 0))),
         crossed_grads,
         line_parts.shape[0] // 128,
@@ -1462,12 +1469,7 @@
         4,
         LONG_COST,
     )
-    block_low, block_sums = after((block_low, block_sums), dh_first_own)
     stats = stats.reshape(-1)
-    block_out = resid_own + own_rows(block_low).astype(jnp.float32)
-    for came in block_sums:
-        block_out = block_out + came.astype(jnp.float32)
-    block_out = block_out.astype(jnp.bfloat16)
     grad_tokens = norm_back(
         d_resid_own, dh_first_own, tokens_own_wide, own_rows(rate_first), gain_first
     )
@@ -1476,7 +1478,7 @@
     bias_end = line_parts.shape[0] + 3 * biases[0].shape[1]
     bias_sums = stats[line_parts.shape[0] : bias_end].reshape(3, -1)
 
-    attn_sums = (*after(lax.psum(attn_grads, "expert"), dh_first_own), after(out_sum, dh_first_own))
+    attn_sums = after(lax.psum(attn_grads, "expert"), dh_first_own)
     expert_sums = [mixed_grads[:, kind] for kind in range(3)]
 
     return (
@@ -1489,7 +1491,7 @@
         bias_sums[1],
         attn_sums[2].astype(jnp.float32),
         bias_sums[2],
-        attn_sums[3].astype(jnp.float32),
+        out_grad,
         stats[width : 2 * width],
         small_sum[:experts_count].T,
         small_sum[experts_count],

time: 1360 us -> 1360 us (level)
    unnamed x188 -> x192, local copies, waits for them, and re-layouts: 69.3 us -> 68.4 us
  transfers between devices with their start and end apart: 23 -> 23, of which waited for: 2 -> 3; matrix products, arithmetic and copies ran while one was open for 11% -> 11% of each run, Pallas kernels for 79% -> 79%
where the time goes in v5:
time: 1360 us; the launch traced here: 1350 us
  Pallas kernels  1060 us (78%)
  local copies, waits for them, and re-layouts  109 us (8%)
  other arithmetic  72.5 us (5%)
  starting transfers between devices  37.3 us (3%)
  matrix products  28.8 us (2%)
  waiting for transfers between devices  25.4 us (2%)
  between operations  15.9 us (1%)
    pallas_call x1, Pallas kernels, arrive(): pl.pallas_call(functools.partial(arrive_body, members, local_experts, pie...  218 us
    pallas_call x1, Pallas kernels, turnaround(): pl.pallas_call(functools.partial(turnaround_body, pieces), in_specs=[in_v...  181 us
    pallas_call x1, Pallas kernels, scatter(): pl.pallas_call(functools.partial(scatter_body, pieces, columns, line_rows...  139 us
    pallas_call x1, Pallas kernels, gather(): pl.pallas_call(functools.partial(gather_body, pieces), in_specs=[pl.Block...  105 us
    pallas_call x2, Pallas kernels, expert_back(): pl.pallas_call(functools.partial(expert_back_body, turned), grid=(experts...  104 us
    pallas_call x2, Pallas kernels, expert(): pl.pallas_call(functools.partial(expert_body, turned), grid=(experts, cou...  95.7 us
    unnamed x192, local copies, waits for them, and re-layouts  68.4 us
    pallas_call x1, Pallas kernels, weight_grads(): pl.pallas_call(weight_grads_body, grid=(experts, members), in_specs=[by_c...  45.6 us
  transfers between devices with their start and end apart: 23, of which 3 were waited for; matrix products, arithmetic and copies ran while one was open for 11% of the time, Pallas kernels for 79%

profile of v5, /device:TPU:0, one launch (start us, length us, event | category | flops | bytes accessed | tf_op | source)
XLA Modules:
  0.0 1349.3 jit_solution(1206619491162735717)
XLA Ops:
  12.1 218.1 %arrive.1 = (bf16[4,384,2048]{2,1,0:T(8,128)(2,1)}, s32[4,4,384]{2,1,0:T(4,128)}, bf16[4,128,1408]{2,1,0:T(8,128)(2,1)}, bf16[4,128,1408]{2,1,0:T(8,128)(2,1)}, ...) custom-call(bf16[384,2048]{1,0:T(8,128)(2,1)} %refs_0_.1, ...), custom_call_target="tpu_custom_call" | custom-call | tf_op jit(solution)/shard_map/arrive/pallas_call | solution.py:735
  233.0 5.7 collective-permute-start
  239.2 2.8 fusion.18
  242.6 14.2 %project.1 = (bf16[1536,2048]{1,0:T(8,128)(2,1)}, f32[1536,1]{1,0:T(8,128)S(1)}, bf16[1536,512]{1,0:T(8,128)(2,1)S(1)}, bf16[1536,512]{1,0:T(8,128)(2,1)S(1)}, bf16[1536,512]{1,0:T(8,128)(2,1)S(1)}) custom-call(bf16[1536,2048]{1,0:T(8,128)(2,1)} %bitcast.164, f32[1,2048]{1,0:T(1,128)S(1)} %bitcast.140, bf16[2048,512]{1,0:T(8,128)(2,1)S(1)} %copy-done.11, ...), custom_call_target="tpu_custom_call" | custom-call | tf_op jit(solution)/shard_map/project/pallas_call | solution.py:117
  256.8 20.7 %attend.1 = (bf16[1536,512]{1,0:T(8,128)(2,1)S(1)}, f32[4,1,1536]{2,1,0:T(1,128)S(1)}) custom-call(s32[6]{0:T(128)S(1)} %and_select_fusion.lows_ref, s32[1,1536]{1,0:T(1,128)S(1)} %subtract_subtract_fusion.starts_ref, bf16[1536,512]{1,0:T(8,128)(2,1)S(1)} %get-tuple-element.122.query_ref, bf16[1536,512]{1,0:T(8,128)(2,1)S(1)} %get-tuple-element.123.key_ref, ...), custom_call_target="tpu_custom_call" | custom-call | tf_op jit(solution)/shard_map/attend/pallas_call | solution.py:175
  279.9 105.2 %gather.1.attended_ref = bf16[4,1536,512]{2,1,0:T(8,128)(2,1)} custom-call(bf16[1536,512]{1,0:T(8,128)(2,1)} %copy-done.47), custom_call_target="tpu_custom_call" | custom-call | tf_op jit(solution)/shard_map/gather/pallas_call | solution.py:777
  388.9 22.2 %settle.1 = (f32[1536,2048]{1,0:T(8,128)}, f32[1536,1]{1,0:T(8,128)S(1)}, bf16[1536,2048]{1,0:T(8,128)(2,1)S(1)}, f32[1536,128]{1,0:T(8,128)S(1)}) custom-call(bf16[1536,2048]{1,0:T(8,128)(2,1)} %bitcast.165, bf16[4,1536,512]{2,1,0:T(8,128)(2,1)} %gather.1.attended_ref, bf16[2048,2048]{1,0:T(8,128)(2,1)} %all-gather.8.cloned.1.call-done.weight_ref, ...), custom_call_target="tpu_custom_call" | custom-call | flops 12884901888 | bytes 37748736 | tf_op jit(solution)/shard_map/settle/pallas_call | solution.py:304
  414.6 11.4 collective-permute-done.3
  430.6 38.9 %expert.2 = (f32[1,1536,2048]{2,1,0:T(8,128)}, bf16[1,1536,1408]{2,1,0:T(8,128)(2,1)}, f32[1,1536,1408]{2,1,0:T(8,128)}, f32[1,1536,1408]{2,1,0:T(8,128)}) custom-call(bf16[1,1536,2048]{2,1,0:T(8,128)(2,1)} %bitcast.126, f32[1,1536,1]{2,1,0:T(8,128)} %bitcast.132, bf16[1,2048,1408]{2,1,0:T(8,128)(2,1)} %bitcast.167, bf16[1,2048,1408]{2,1,0:T(8,128)(2,1)} %bitcast.169, ...), custom_call_target="tpu_custom_call" | custom-call | tf_op jit(solution)/shard_map/expert/pallas_call | solution.py:458
  469.6 2.8 copy-done.3
  472.3 6.5 dispatch.2
  481.6 2.8 constant_dynamic-update-slice_fusion.7
  493.8 2.9 constant_dynamic-update-slice_fusion.2
  496.7 3.4 constant_dynamic-slice_fusion.1.source_ref
  500.1 11.3 convolution_convert_fusion
  511.5 42.9 %expert_back.2 = (f32[1,1536,1]{2,1,0:T(8,128)}, bf16[1,1536,2048]{2,1,0:T(8,128)(2,1)}, bf16[1,1536,1408]{2,1,0:T(8,128)(2,1)}, bf16[1,1536,1408]{2,1,0:T(8,128)(2,1)}, f32[1,1536,2048]{2,1,0:T(8,128)}) custom-call(bf16[1,1536,2048]{2,1,0:T(8,128)(2,1)} %bitcast.127, f32[1,1536,2048]{2,1,0:T(8,128)} %get-tuple-element.141.result_ref, ...), custom_call_target="tpu_custom_call" | custom-call | tf_op jit(solution)/shard_map/expert_back/pallas_call | solution.py:491
  558.8 22.8 %pair_grads.1 = (bf16[2048,1408]{1,0:T(8,128)(2,1)S(1)}, bf16[2048,1408]{1,0:T(8,128)(2,1)}) custom-call(bf16[1536,2048]{1,0:T(8,128)(2,1)} %copy-done.2, bf16[1536,1408]{1,0:T(8,128)(2,1)S(1)} %bitcast.136, bf16[1536,1408]{1,0:T(8,128)(2,1)S(1)} %bitcast.137), custom_call_target="tpu_custom_call" | custom-call | tf_op jit(solution)/shard_map/pair_grads/pallas_call | solution.py:546
  589.9 56.8 %expert.3 = (bf16[2,1024,2048]{2,1,0:T(8,128)(2,1)}, bf16[2,1024,1408]{2,1,0:T(8,128)(2,1)}, f32[2,1024,1408]{2,1,0:T(8,128)}, f32[2,1024,1408]{2,1,0:T(8,128)}, bf16[2,1024,2048]{2,1,0:T(8,128)(2,1)}) custom-call(bf16[2,1024,2048]{2,1,0:T(8,128)(2,1)} %bitcast.154, f32[2,1024,1]{2,1,0:T(8,128)} %copy.104.scale_ref, bf16[2,2048,1408]{2,1,0:T(8,128)(2,1)} %bitcast.157, ...), custom_call_target="tpu_custom_call" | custom-call | tf_op jit(solution)/shard_map/expert/pallas_call | solution.py:458
  646.7 9.4 collect.2
  661.5 6.8 collective-permute-start.6
  668.2 2.8 copy-done.5
  671.0 6.5 dispatch.3
  677.5 61.0 %expert_back.3 = (f32[2,1024,1]{2,1,0:T(8,128)}, bf16[2,1024,2048]{2,1,0:T(8,128)(2,1)}, bf16[2,1024,1408]{2,1,0:T(8,128)(2,1)}, bf16[2,1024,1408]{2,1,0:T(8,128)(2,1)}, bf16[2,1024,2048]{2,1,0:T(8,128)(2,1)}) custom-call(bf16[2,1024,2048]{2,1,0:T(8,128)(2,1)} %bitcast.163, bf16[2,1024,2048]{2,1,0:T(8,128)(2,1)} %get-tuple-element.157.result_ref, ...), custom_call_target="tpu_custom_call" | custom-call | tf_op jit(solution)/shard_map/expert_back/pallas_call | solution.py:491
  738.6 4.7 fusion.7
  747.6 2.7 copy-done.39
  750.3 45.6 %weight_grads.1 = bf16[2,4,3,512,1408]{4,3,2,1,0:T(8,128)(2,1)} custom-call(bf16[2,1024,2048]{2,1,0:T(8,128)(2,1)} %bitcast.155, bf16[2,1024,2048]{2,1,0:T(8,128)(2,1)} %get-tuple-element.165.d_out_ref, bf16[2,1024,1408]{2,1,0:T(8,128)(2,1)S(1)} %copy-done.38, bf16[2,1024,1408]{2,1,0:T(8,128)(2,1)S(1)} %copy-done.39, ...), custom_call_target="tpu_custom_call" | custom-call | tf_op jit(solution)/shard_map/weight_grads/pallas_call | solution.py:523
  813.5 6.5 fusion.5
  821.3 5.7 collective-permute-start.10
  829.4 6.1 fusion.26
  836.6 13.8 %collect.3 = bf16[1536,2048]{1,0:T(8,128)(2,1)S(1)} custom-call(s32[1536,2]{1,0:T(8,128)S(1)} %bitcast.135, bf16[2,4,256,2048]{3,2,1,0:T(8,128)(2,1)} %bitcast.179, f32[1536,2048]{1,0:T(8,128)} %bitcast.177, bf16[1536,128]{1,0:T(8,128)(2,1)S(1)} %copy-done.46, bf16[128,2048]{1,0:T(8,128)(2,1)S(1)} %fusion.17.rest_1_), custom_call_target="tpu_custom_call" | custom-call | tf_op jit(solution)/shard_map/collect/pallas_call | solution.py:406
  850.4 3.4 copy-done.7
  853.9 181.4 %turnaround.1 = (f32[384,2048]{1,0:T(8,128)S(1)}, f32[1,2048]{1,0:T(1,128)S(1)}, bf16[4,384,2048]{2,1,0:T(8,128)(2,1)S(1)}) custom-call(bf16[4,384,2048]{2,1,0:T(8,128)(2,1)} %bitcast.131, f32[1536,2048]{1,0:T(8,128)} %get-tuple-element.128.refs_1_, f32[1536,1]{1,0:T(8,128)S(1)} %copy-done.52, bf16[384,2048]{1,0:T(8,128)(2,1)S(1)} %copy-done.24, ...), custom_call_target="tpu_custom_call" | custom-call | tf_op jit(solution)/shard_map/turnaround/pallas_call | solution.py:1035
  1039.7 4.6 convolution_convert_fusion.1
  1044.4 3.7 dynamic-slice_bitcast_fusion.2
  1049.5 6.5 convolution_convert_fusion.2.grad_ref
  1056.1 26.2 %attend_back.1 = (bf16[1536,512]{1,0:T(8,128)(2,1)S(1)}, bf16[1536,512]{1,0:T(8,128)(2,1)S(1)}, bf16[1536,512]{1,0:T(8,128)(2,1)S(1)}) custom-call(s32[6]{0:T(128)S(1)} %copy-done.60, s32[1,1536]{1,0:T(1,128)S(1)} %copy-done.56, bf16[1536,512]{1,0:T(8,128)(2,1)S(1)} %copy-done.26, bf16[1536,512]{1,0:T(8,128)(2,1)S(1)} %copy-done.28, ...), custom_call_target="tpu_custom_call" | custom-call | tf_op jit(solution)/shard_map/attend_back/pallas_call | solution.py:251
  1085.8 12.8 attend_grads.1
  1098.7 7.4 all-reduce.10.cloned.1.call-done
  1106.1 3.5 collective-permute-start.14
  1109.6 5.2 collective-permute-done.13
  1123.9 14.5 %unproject.1 = (bf16[1536,2048]{1,0:T(8,128)(2,1)}, f32[1,2048]{1,0:T(1,128)S(1)}, f32[1,512]{1,0:T(1,128)S(1)}, f32[1,512]{1,0:T(1,128)S(1)}, f32[1,512]{1,0:T(1,128)S(1)}) custom-call(bf16[1536,512]{1,0:T(8,128)(2,1)S(1)} %copy-done.32, bf16[1536,512]{1,0:T(8,128)(2,1)S(1)} %copy-done.34, bf16[1536,512]{1,0:T(8,128)(2,1)S(1)} %copy-done.36, ...), custom_call_target="tpu_custom_call" | custom-call | tf_op jit(solution)/shard_map/unproject/pallas_call | solution.py:1090
  1141.1 8.0 convert_element_type.204
  1149.1 5.2 convert_element_type.205
  1154.2 6.0 convert_element_type.206
  1160.2 5.5 add_convert_fusion
  1175.1 138.8 %scatter.1 = (f32[384,2048]{1,0:T(8,128)S(1)}, f32[192,128]{1,0:T(8,128)S(1)}, bf16[4,3,128,1408]{3,2,1,0:T(8,128)(2,1)S(1)}) custom-call(bf16[4,384,2048]{2,1,0:T(8,128)(2,1)} %bitcast.203, f32[192,128]{1,0:T(8,128)S(1)} %pad.19.stats_ref, bf16[4,3,128,1408]{3,2,1,0:T(8,128)(2,1)S(1)} %copy-done.43), custom_call_target="tpu_custom_call" | custom-call | flops 99999997952 | tf_op jit(solution)/shard_map/scatter/pallas_call | solution.py:958
  1332.3 4.3 convert_element_type.209
  1336.7 2.7 convert_element_type.210
  (315 shorter events, 130.4 us)
Async XLA Ops:
  7.2 381.6 %all-gather.8.cloned.1.call-start = ((), (), s32[]{:S(2)}) async-start(), calls=%async_computation.1 | async-start | bytes 8650752 | tf_op jit(solution)/shard_map/all_gather | solution.py:1246
  9.5 580.3 %all-gather.10.cloned.1.call-start = ((), (), s32[]{:S(2)}) async-start(), calls=%async_computation.4 | async-start | bytes 12976128 | tf_op jit(solution)/shard_map/all_gather | solution.py:1234
  230.3 359.6 %all-gather.12.cloned.1.call-start = ((), (), s32[]{:S(2)}) async-start(), calls=%async_computation.5 | async-start | bytes 12976128 | tf_op jit(solution)/shard_map/all_gather | solution.py:1234
  231.0 358.8 %all-gather.14.cloned.1.call-start = ((), (), s32[]{:S(2)}) async-start(), calls=%async_computation.6 | async-start | bytes 12976128 | tf_op jit(solution)/shard_map/all_gather | solution.py:1234
  231.6 603.9 %all-reduce.14.cloned.1.call-start = ((), (), s32[]{:S(2)}) async-start(), calls=%async_computation.8 | async-start | bytes 34603008 | tf_op jit(solution)/shard_map/psum | solution.py:1331
  231.7 48.1 %collective-permute-start.1 = (bf16[384,2048]{1,0:T(8,128)(2,1)}, bf16[384,2048]{1,0:T(8,128)(2,1)}, u32[]{:S(2)}, u32[]{:S(2)}) collective-permute-start(bf16[384,2048]{1,0:T(8,128)(2,1)} %refs_3_.2), channel_id=1, source_target_pairs={{3,2},{2,1},{1,0},{7,6},{6,5},{5,4},{11,10},{10,9},{9,8},{15,14},{... | collective-permute-start | bytes 4718600 | tf_op jit(solution)/shard_map/ppermute | solution.py:1199
  233.0 46.8 %collective-permute-start = (bf16[384,2048]{1,0:T(8,128)(2,1)}, bf16[384,2048]{1,0:T(8,128)(2,1)}, u32[]{:S(2)}, u32[]{:S(2)}) collective-permute-start(bf16[384,2048]{1,0:T(8,128)(2,1)} %refs_3_.2), channel_id=1, source_target_pairs={{0,1},{1,2},{2,3},{4,5},{5,6},{6,7},{8,9},{9,10},{10,11},{12,13},{... | collective-permute-start | bytes 4718600 | tf_op jit(solution)/shard_map/ppermute | solution.py:1199
  239.0 149.9 %copy-start.57 = (f32[2048]{0:T(1024)}, f32[2048]{0:T(1024)S(1)}, u32[]{:S(2)}) copy-start(f32[2048]{0:T(1024)S(1)} %broadcast_in_dim.174) | copy-start | bytes 24580
  242.5 14.2 %copy-start.19 = (f32[1536,128]{1,0:T(8,128)}, f32[1536,128]{1,0:T(8,128)S(1)}, u32[]{:S(2)}) copy-start(f32[1536,128]{1,0:T(8,128)S(1)} %get-tuple-element.259.c.rest_0_) | copy-start | bytes 2359300
  242.5 14.2 %copy-start.21 = (f32[1536,128]{1,0:T(8,128)}, f32[1536,128]{1,0:T(8,128)S(1)}, u32[]{:S(2)}) copy-start(f32[1536,128]{1,0:T(8,128)S(1)} %get-tuple-element.260.s.rest_1_) | copy-start | bytes 2359300
  256.7 20.8 %copy-start.27 = (bf16[1536,512]{1,0:T(8,128)(2,1)}, bf16[1536,512]{1,0:T(8,128)(2,1)S(1)}, u32[]{:S(2)}) copy-start(bf16[1536,512]{1,0:T(8,128)(2,1)S(1)} %get-tuple-element.123.key_ref) | copy-start | bytes 4718596
  256.8 23.0 %copy-start.29 = (bf16[1536,512]{1,0:T(8,128)(2,1)}, bf16[1536,512]{1,0:T(8,128)(2,1)S(1)}, u32[]{:S(2)}) copy-start(bf16[1536,512]{1,0:T(8,128)(2,1)S(1)} %get-tuple-element.124.value_ref) | copy-start | bytes 4718596
  256.8 23.0 %copy-start.49 = (f32[1536,1]{1,0:T(8,128)}, f32[1536,1]{1,0:T(8,128)S(1)}, u32[]{:S(2)}) copy-start(f32[1536,1]{1,0:T(8,128)S(1)} %get-tuple-element.198.refs_7_) | copy-start | bytes 18436
  256.8 128.3 %copy-start.59 = (s32[6]{0:T(128)}, s32[6]{0:T(128)S(1)}, u32[]{:S(2)}) copy-start(s32[6]{0:T(128)S(1)} %and_select_fusion.lows_ref) | copy-start | bytes 76
  256.8 23.0 %copy-start.55 = (s32[1,1536]{1,0:T(1,128)}, s32[1,1536]{1,0:T(1,128)S(1)}, u32[]{:S(2)}) copy-start(s32[1,1536]{1,0:T(1,128)S(1)} %subtract_subtract_fusion.starts_ref) | copy-start | bytes 18436
  279.8 108.5 %copy-start.70 = (bf16[2048,8]{0,1:T(8,128)(2,1)S(1)}, bf16[2048,8]{0,1:T(8,128)(2,1)}, u32[]{:S(2)}) copy-start(bf16[2048,8]{0,1:T(8,128)(2,1)} %param.34) | copy-start | bytes 98308
  279.8 108.5 %copy-start.76 = (bf16[2048]{0:T(1024)(128)(2,1)S(1)}, bf16[2048]{0:T(1024)(128)(2,1)}, u32[]{:S(2)}) copy-start(bf16[2048]{0:T(1024)(128)(2,1)} %param.35) | copy-start | bytes 12292
  385.1 29.6 %collective-permute-start.2 = (bf16[384,2048]{1,0:T(8,128)(2,1)}, bf16[384,2048]{1,0:T(8,128)(2,1)}, u32[]{:S(2)}, u32[]{:S(2)}) collective-permute-start(bf16[384,2048]{1,0:T(8,128)(2,1)} %collective-permute-done), channel_id=1, source_target_pairs={{1,2},{2,3},{5,6},{6,7},{9,10},{10,11},{13,14},{14,15},{17,18},{18... | collective-permute-start | bytes 4718600 | tf_op jit(solution)/shard_map/ppermute | solution.py:1199
  386.8 39.2 %collective-permute-start.3 = (bf16[384,2048]{1,0:T(8,128)(2,1)}, bf16[384,2048]{1,0:T(8,128)(2,1)}, u32[]{:S(2)}, u32[]{:S(2)}) collective-permute-start(bf16[384,2048]{1,0:T(8,128)(2,1)} %collective-permute-done.1), channel_id=1, source_target_pairs={{2,1},{1,0},{6,5},{5,4},{10,9},{9,8},{14,13},{13,12},{18,17},{17,1... | collective-permute-start | bytes 4718600 | tf_op jit(solution)/shard_map/ppermute | solution.py:1199
  388.9 40.3 %copy-start.71 = (s32[4,4,384]{2,1,0:T(4,128)S(1)}, s32[4,4,384]{2,1,0:T(4,128)}, u32[]{:S(2)}) copy-start(s32[4,4,384]{2,1,0:T(4,128)} %get-tuple-element.149) | copy-start | bytes 73732
  426.0 52.8 %collective-permute-start.4 = (bf16[384,2048]{1,0:T(8,128)(2,1)}, bf16[384,2048]{1,0:T(8,128)(2,1)}, u32[]{:S(2)}, u32[]{:S(2)}) collective-permute-start(bf16[384,2048]{1,0:T(8,128)(2,1)} %collective-permute-done.2), channel_id=1, source_target_pairs={{2,3},{6,7},{10,11},{14,15},{18,19},{22,23},{26,27},{30,31}} | collective-permute-start | bytes 4718600 | tf_op jit(solution)/shard_map/ppermute | solution.py:1199
  427.8 51.0 %collective-permute-start.5 = (bf16[384,2048]{1,0:T(8,128)(2,1)}, bf16[384,2048]{1,0:T(8,128)(2,1)}, u32[]{:S(2)}, u32[]{:S(2)}) collective-permute-start(bf16[384,2048]{1,0:T(8,128)(2,1)} %collective-permute-done.3), channel_id=1, source_target_pairs={{1,0},{5,4},{9,8},{13,12},{17,16},{21,20},{25,24},{29,28}} | collective-permute-start | bytes 4718600 | tf_op jit(solution)/shard_map/ppermute | solution.py:1199
  500.1 11.4 copy-start.4
  584.1 460.2 %reduce-scatter.2.cloned.1.call-start = ((), (), s32[]{:S(2)}) async-start(), calls=%async_computation.2 | async-start | bytes 38928384 | tf_op jit(solution)/shard_map/reduce_scatter | solution.py:1360
  589.9 56.8 %copy-start.8 = (f32[1536,1]{1,0:T(8,128)S(1)}, f32[1536,1]{1,0:T(8,128)}, u32[]{:S(2)}) copy-start(f32[1536,1]{1,0:T(8,128)} %get-tuple-element.234.rest_0_) | copy-start | bytes 18436
  589.9 56.8 %copy-start.17 = (s32[4,384,2]{2,1,0:T(8,128)S(1)}, s32[4,384,2]{2,1,0:T(8,128)}, u32[]{:S(2)}) copy-start(s32[4,384,2]{2,1,0:T(8,128)} %copy.100) | copy-start | bytes 36868
  659.6 78.9 %collective-permute-start.7 = (bf16[384,2048]{1,0:T(8,128)(2,1)}, bf16[384,2048]{1,0:T(8,128)(2,1)}, u32[]{:S(2)}, u32[]{:S(2)}) collective-permute-start(bf16[384,2048]{1,0:T(8,128)(2,1)} %get-tuple-element.239), channel_id=1, source_target_pairs={{3,2},{7,6},{11,10},{15,14},{19,18},{23,22},{27,26},{31,30}} | collective-permute-start | bytes 4718600 | tf_op jit(solution)/shard_map/ppermute | solution.py:1228
  661.5 77.1 %collective-permute-start.6 = (bf16[384,2048]{1,0:T(8,128)(2,1)}, bf16[384,2048]{1,0:T(8,128)(2,1)}, u32[]{:S(2)}, u32[]{:S(2)}) collective-permute-start(bf16[384,2048]{1,0:T(8,128)(2,1)} %get-tuple-element.240), channel_id=1, source_target_pairs={{0,1},{4,5},{8,9},{12,13},{16,17},{20,21},{24,25},{28,29}} | collective-permute-start | bytes 4718600 | tf_op jit(solution)/shard_map/ppermute | solution.py:1227
  743.3 52.7 %collective-permute-start.9 = (bf16[384,2048]{1,0:T(8,128)(2,1)S(1)}, bf16[384,2048]{1,0:T(8,128)(2,1)}, u32[]{:S(2)}, u32[]{:S(2)}) collective-permute-start(bf16[384,2048]{1,0:T(8,128)(2,1)S(1)} %get-tuple-element.237), channel_id=1, source_target_pairs={{3,2},{2,1},{7,6},{6,5},{11,10},{10,9},{15,14},{14,13},{19,18},{18... | collective-permute-start | bytes 4718600 | tf_op jit(solution)/shard_map/ppermute | solution.py:1228
  745.1 50.9 %collective-permute-start.8 = (bf16[384,2048]{1,0:T(8,128)(2,1)S(1)}, bf16[384,2048]{1,0:T(8,128)(2,1)}, u32[]{:S(2)}, u32[]{:S(2)}) collective-permute-start(bf16[384,2048]{1,0:T(8,128)(2,1)S(1)} %get-tuple-element.238), channel_id=1, source_target_pairs={{0,1},{1,2},{4,5},{5,6},{8,9},{9,10},{12,13},{13,14},{16,17},{17,1... | collective-permute-start | bytes 4718600 | tf_op jit(solution)/shard_map/ppermute | solution.py:1227
  796.0 310.1 %all-reduce.10.cloned.1.call-start = ((), (), s32[]{:S(2)}) async-start(), calls=%async_computation.3 | async-start | bytes 4194304 | tf_op jit(solution)/shard_map/psum | solution.py:1408
  813.5 13.5 copy-start.64
  813.5 14.0 %copy-start.69 = (f32[1536,8]{0,1:T(8,128)S(1)}, f32[1536,8]{0,1:T(8,128)}, u32[]{:S(2)}) copy-start(f32[1536,8]{0,1:T(8,128)} %copy.108) | copy-start | bytes 147460
  820.0 217.0 %collective-permute-start.11 = (bf16[384,2048]{1,0:T(8,128)(2,1)}, bf16[384,2048]{1,0:T(8,128)(2,1)}, u32[]{:S(2)}, u32[]{:S(2)}) collective-permute-start(bf16[384,2048]{1,0:T(8,128)(2,1)} %get-tuple-element.235), channel_id=1, source_target_pairs={{3,2},{2,1},{1,0},{7,6},{6,5},{5,4},{11,10},{10,9},{9,8},{15,14},{... | collective-permute-start | bytes 4718600 | tf_op jit(solution)/shard_map/ppermute | solution.py:1228
  821.3 215.7 %collective-permute-start.10 = (bf16[384,2048]{1,0:T(8,128)(2,1)}, bf16[384,2048]{1,0:T(8,128)(2,1)}, u32[]{:S(2)}, u32[]{:S(2)}) collective-permute-start(bf16[384,2048]{1,0:T(8,128)(2,1)} %get-tuple-element.236), channel_id=1, source_target_pairs={{0,1},{1,2},{2,3},{4,5},{5,6},{6,7},{8,9},{9,10},{10,11},{12,13},{... | collective-permute-start | bytes 4718600 | tf_op jit(solution)/shard_map/ppermute | solution.py:1227
  836.6 17.3 %copy-start.24 = (bf16[384,2048]{1,0:T(8,128)(2,1)S(1)}, bf16[384,2048]{1,0:T(8,128)(2,1)}, u32[]{:S(2)}) copy-start(bf16[384,2048]{1,0:T(8,128)(2,1)} %refs_3_.2) | copy-start | bytes 4718596
  836.6 17.3 %copy-start.52 = (f32[1536,1]{1,0:T(8,128)S(1)}, f32[1536,1]{1,0:T(8,128)}, u32[]{:S(2)}) copy-start(f32[1536,1]{1,0:T(8,128)} %copy-done.51) | copy-start | bytes 18436
  836.6 17.3 %copy-start.58 = (f32[2048]{0:T(1024)S(1)}, f32[2048]{0:T(1024)}, u32[]{:S(2)}) copy-start(f32[2048]{0:T(1024)} %copy-done.57) | copy-start | bytes 24580
  853.9 185.8 %copy-start.48 = (bf16[1536,512]{1,0:T(8,128)(2,1)S(1)}, bf16[1536,512]{1,0:T(8,128)(2,1)}, u32[]{:S(2)}) copy-start(bf16[1536,512]{1,0:T(8,128)(2,1)} %copy-done.47) | copy-start | bytes 4718596
  1044.3 288.0 %all-reduce.12.cloned.1.call-start = ((), (), s32[]{:S(2)}) async-start(), calls=%async_computation.7 | async-start | bytes 12582912 | tf_op jit(solution)/shard_map/psum | solution.py:1481
  1048.1 37.0 %collective-permute-start.12 = (bf16[3,128,1408]{2,1,0:T(8,128)(2,1)}, bf16[3,128,1408]{2,1,0:T(8,128)(2,1)}, u32[]{:S(2)}, u32[]{:S(2)}) collective-permute-start(bf16[3,128,1408]{2,1,0:T(8,128)(2,1)} %get-tuple-element.181), channel_id=1, source_target_pairs={{0,1},{1,2},{2,3},{3,0},{4,5},{5,6},{6,7},{7,4},{8,9},{9,10},{10,1... | collective-permute-start | bytes 3244040 | tf_op jit(solution)/shard_map/ppermute | solution.py:1425
  1048.2 66.6 %collective-permute-start.13 = (bf16[3,128,1408]{2,1,0:T(8,128)(2,1)}, bf16[3,128,1408]{2,1,0:T(8,128)(2,1)}, u32[]{:S(2)}, u32[]{:S(2)}) collective-permute-start(bf16[3,128,1408]{2,1,0:T(8,128)(2,1)} %get-tuple-element.191), channel_id=1, source_target_pairs={{0,2},{1,3},{2,0},{3,1},{4,6},{5,7},{6,4},{7,5},{8,10},{9,11},{10,... | collective-permute-start | bytes 3244040 | tf_op jit(solution)/shard_map/ppermute | solution.py:1425
  1048.3 34.0 %slice-start = ((s8[4325376]{0:T(1024)(128)(4,1)}), s8[131072]{0:T(1024)(128)(4,1)S(1)}, s32[]{:S(2)}) async-start(s8[4325376]{0:T(1024)(128)(4,1)} %bitcast.174), calls=%async_computation.9 | async-start | bytes 262144
  1049.5 32.9 %slice-start.1 = ((s8[4325376]{0:T(1024)(128)(4,1)}), s8[4194304]{0:T(1024)(128)(4,1)S(1)}, s32[]{:S(2)}) async-start(s8[4325376]{0:T(1024)(128)(4,1)} %bitcast.174), calls=%async_computation.10 | async-start | bytes 8388608
  1085.8 29.0 %copy-start.50 = (f32[1536,1]{1,0:T(8,128)S(1)}, f32[1536,1]{1,0:T(8,128)}, u32[]{:S(2)}) copy-start(f32[1536,1]{1,0:T(8,128)} %copy-done.49) | copy-start | bytes 18436
  1106.1 64.4 %collective-permute-start.14 = (bf16[3,128,1408]{2,1,0:T(8,128)(2,1)}, bf16[3,128,1408]{2,1,0:T(8,128)(2,1)}, u32[]{:S(2)}, u32[]{:S(2)}) collective-permute-start(bf16[3,128,1408]{2,1,0:T(8,128)(2,1)} %get-tuple-element.216), channel_id=1, source_target_pairs={{0,3},{1,0},{2,1},{3,2},{4,7},{5,4},{6,5},{7,6},{8,11},{9,8},{10,9... | collective-permute-start | bytes 3244040 | tf_op jit(solution)/shard_map/ppermute | solution.py:1425
  1123.9 14.6 %copy-start.68 = (bf16[512,2048]{1,0:T(8,128)(2,1)S(1)}, bf16[512,2048]{1,0:T(8,128)(2,1)}, u32[]{:S(2)}) copy-start(bf16[512,2048]{1,0:T(8,128)(2,1)} %all-reduce.10.cloned.1.call-done) | copy-start | bytes 6291460
  1141.1 13.1 slice-start.2
  (64 other events, 256.8 us)
Sparse Core Ops, SparseCore 0:
  11.5 101.8 all-gather.7
  230.4 66.3 all-gather.9
  298.7 67.6 all-gather.11
  368.2 67.6 all-gather.13
  584.3 222.9 all-reduce.13
  810.7 210.6 reduce-scatter.1
  1044.4 61.6 all-reduce.9
  1165.9 163.5 all-reduce.11
